TPU v7x, 32 devices: a whole 2x2x4 slice. The times are simulated.
32 devices in a mesh: section: 4 (over z), head: 8 (over y, x, core).
Axes of the slice: x: 2, y: 2, z: 4, core: 2. Of those that a mesh axis runs over, the one named last changes fastest.
Arguments:
- hidden_in: bfloat16 [12288, 2048], P(('section', 'head')), may hold values from -3 to 3
- norm_gain: float32 [2048], replicated, may hold values from 0.1 to 1.9
- w_qkv: bfloat16 [2048, 3, 2048], P(None, None, 'head'), may hold values from -0.5 to 0.5
- w_out: bfloat16 [2048, 2048], P('head'), may hold values from -0.375 to 0.375
- block_lists: int32 [24, 12], P('section'), may hold values from -1 to 23, as said below
Outputs:
- mixed: bfloat16 [12288, 2048], P(('section', 'head'))
Inputs may be any that keep to these rules, and one draw needn't show every extreme that they name: `block_lists`: row b starts with b itself, then holds 1 + b * 11 // 23 - 1 further distinct blocks below b, then -1 in every remaining slot.
All inputs are finite; a program needn't handle non-finite values.
Results may differ from a plain program's by a relative error of at most 0.015.
Values may be sent and summed in bfloat16 or wider, within the bound.
No kernel may reach another device: no remote copies, remote signals or barrier semaphores. Data moves between devices by JAX's collectives and lax.ppermute only.
A program may use at most 128 MiB of HBM per device.

v0:
```python
import math

import jax
import jax.numpy as jnp
from jax import lax
from jax.sharding import PartitionSpec as P

D = 2048
HD = 128
BLK = 512


EPS = 1e-05
THETA = 10000.0


def rotate(vectors, cosine, sine):
    half = vectors.shape[-1] // 2
    first = vectors[..., :half]
    second = vectors[..., half:]
    return jnp.concatenate(
        [first * cosine - second * sine, second * cosine + first * sine], axis=-1
    )


def local(hidden_in, norm_gain, w_qkv, w_out, block_lists):
    section_id = lax.axis_index("section")
    width = w_qkv.shape[2]
    heads_here = width // HD
    blocks_here = block_lists.shape[0]
    tok_dev = blocks_here * BLK
    scale = 1.0 / math.sqrt(HD)
    resid = hidden_in.astype(jnp.float32)
    normed = (
        resid * lax.rsqrt(jnp.mean(resid * resid, axis=-1, keepdims=True) + EPS) * norm_gain
    ).astype(jnp.bfloat16)
    flat_weight = w_qkv.reshape(D, 3 * width)
    frequency = THETA ** (-(2.0 * jnp.arange(HD // 2, dtype=jnp.float32)) / HD)
    piece = lax.all_gather(normed, "head", axis=0, tiled=True)
    count = piece.shape[0]
    mixed_rows = jnp.dot(piece, flat_weight, preferred_element_type=jnp.float32).reshape(
        count, 3, heads_here, HD
    )
    positions = (section_id * tok_dev + jnp.arange(count, dtype=jnp.int32)).astype(jnp.float32)
    angle = positions[:, None] * frequency[None, :]
    cosine = jnp.cos(angle)[:, None, :]
    sine = jnp.sin(angle)[:, None, :]
    query_part = rotate(mixed_rows[:, 0], cosine, sine).astype(jnp.bfloat16).reshape(count, width)
    key_part = rotate(mixed_rows[:, 1], cosine, sine).astype(jnp.bfloat16).reshape(count, width)
    value_part = mixed_rows[:, 2].astype(jnp.bfloat16).reshape(count, width)
    section_rows = jnp.concatenate([query_part, key_part, value_part], axis=1)
    query = section_rows[:, :width]
    keys = section_rows[:, width : 2 * width]
    values = section_rows[:, 2 * width :]
    keys_all, values_all = (
        lax.all_gather(keys, "section", axis=0, tiled=True),
        lax.all_gather(values, "section", axis=0, tiled=True),
    )
    count_blocks = block_lists.shape[0]
    query_blocks = query.reshape(count_blocks, BLK, heads_here, HD)
    block_ids = section_id * blocks_here + jnp.arange(count_blocks, dtype=jnp.int32)

    def one_block(carry, item):
        query_block, block_row, block_id = item
        live_slots = jnp.sum((block_row >= 0).astype(jnp.int32))
        query_positions = block_id * BLK + jnp.arange(BLK, dtype=jnp.int32)

        def one_slot(slot, state):
            highest, total, weighted = state
            source = block_row[slot]
            key_block = lax.dynamic_slice_in_dim(keys_all, source * BLK, BLK, 0).reshape(
                BLK, heads_here, HD
            )
            value_block = lax.dynamic_slice_in_dim(values_all, source * BLK, BLK, 0).reshape(
                BLK, heads_here, HD
            )
            scores = (
                jnp.einsum(
                    "qhd,khd->hqk", query_block, key_block, preferred_element_type=jnp.float32
                )
                * scale
            )
            key_positions = source * BLK + jnp.arange(BLK, dtype=jnp.int32)
            scores = jnp.where(
                key_positions[None, None, :] <= query_positions[None, :, None], scores, -jnp.inf
            )
            new_highest = jnp.maximum(highest, jnp.max(scores, axis=-1))
            factor = jnp.exp(highest - new_highest)
            weights = jnp.exp(scores - new_highest[..., None])
            total = total * factor + jnp.sum(weights, axis=-1)
            update = jnp.einsum(
                "hqk,khd->hqd",
                weights.astype(jnp.bfloat16),
                value_block,
                preferred_element_type=jnp.float32,
            )
            weighted = weighted * factor[..., None] + update
            return (new_highest, total, weighted)

        start_state = (
            jnp.full((heads_here, BLK), -jnp.inf, jnp.float32),
            jnp.zeros((heads_here, BLK), jnp.float32),
            jnp.zeros((heads_here, BLK, HD), jnp.float32),
        )
        highest, total, weighted = lax.fori_loop(0, live_slots, one_slot, start_state)
        result = (
            (weighted / total[..., None])
            .transpose(1, 0, 2)
            .reshape(BLK, width)
            .astype(jnp.bfloat16)
        )
        return (carry, result)

    _, results = lax.scan(
        one_block, jnp.zeros((), jnp.int32), (query_blocks, block_lists, block_ids)
    )
    attended = results.reshape(count_blocks * BLK, width)
    regrouped = lax.all_to_all(attended, "head", split_axis=0, concat_axis=1, tiled=True)
    summed = jnp.dot(
        regrouped,
        lax.all_gather(w_out, "head", axis=0, tiled=True),
        preferred_element_type=jnp.float32,
    )
    return (resid + summed).astype(jnp.bfloat16)


def solution(mesh):
    placed = (
        P(("section", "head"), None),
        P(),
        P(None, None, "head"),
        P("head", None),
        P("section", None),
    )
    return jax.shard_map(
        local, mesh=mesh, in_specs=placed, out_specs=P(("section", "head"), None), check_vma=False
    )
```

profile of v0, /device:TPU:24, one launch (start us, length us, event | category | flops | bytes accessed | tf_op | source)
XLA Modules:
  0.0 707.0 jit_solution(16907976378496304270)
XLA Ops:
  6.5 1.9 fusion.11
  8.5 2.3 fusion.13
  10.8 3.2 copy.22
  14.1 3.8 multiply_cosine_fusion
  17.9 66.1 %all-gather.5.cloned.1.call-done = bf16[3072,2048]{1,0:T(8,128)(2,1)} async-done(((bf16[384,2048]{1,0:T(8,128)(2,1)}), bf16[3072,2048]{1,0:T(8,128)(2,1)}) %all-gather.5.cloned.1.call-update) | async-done | bytes 12582928 | tf_op jit(solution)/shard_map/all_gather | solution.py:39
  84.0 12.6 %fusion.9 = f32[3072,3,2,128]{0,3,2,1:T(8,128)S(1)} fusion(bf16[3,2,128,2048]{3,2,1,0:T(8,128)(2,1)S(1)} %bitcast.65, bf16[3072,2048]{1,0:T(8,128)(2,1)} %all-gather.5.cloned.1.call-done), kind=kOutput, calls=%fused_computation.22 | convolution fusion | flops 9663676416 | bytes 25165824 | tf_op jit(solution)/shard_map/dot_general | solution.py:41
  97.3 2.9 copy-done
  100.3 1.1 subtract_convert_fusion
  101.4 1.3 pad_maximum_fusion.1
  102.7 3.3 slice.47
  107.6 2.0 concatenate.14
  109.6 1.7 pad_maximum_fusion
  111.3 2.6 copy.23
  113.9 101.2 %all-gather.7.cloned.1.call-done = bf16[12288,256]{0,1:T(8,128)(2,1)} async-done(((bf16[3072,256]{0,1:T(8,128)(2,1)}), bf16[12288,256]{0,1:T(8,128)(2,1)}) %all-gather.7.cloned.1.call-update) | async-done | bytes 6291472 | tf_op jit(solution)/shard_map/all_gather | solution.py:56
  215.1 115.2 %all-gather.9.cloned.1.call-done = bf16[12288,256]{0,1:T(8,128)(2,1)} async-done(((bf16[3072,256]{0,1:T(8,128)(2,1)}), bf16[12288,256]{0,1:T(8,128)(2,1)}) %all-gather.9.cloned.1.call-update) | async-done | bytes 6291472 | tf_op jit(solution)/shard_map/all_gather | solution.py:57
  330.3 335.1 %while.26 = (s32[]{:T(128)}, bf16[6,512,256]{2,1,0:T(8,128)(2,1)}, s32[6,12]{1,0:T(8,128)}, bf16[6,512,2,128]{3,1,2,0:T(8,128)(2,1)}, s32[6]{0:T(128)S(1)}, /*in...) while((s32[]{:T(128)}, bf16[6,512,256]{2,1,0:T(8,128)(2,1)}, ...), condition=%wide.region_7.8_spmd, body=%wide.region_1.7_spmd.sunk | while | flops 272895008 | bytes 13194402 | solution.py:114
  330.3 1.3 fusion.31
  333.8 43.8 %while.27 = (s32[]{:T(128)}, f32[2,512]{1,0:T(2,128)S(1)}, f32[2,512]{1,0:T(2,128)S(1)}, f32[2,512,128]{2,1,0:T(8,128)S(1)}, s32[]{:T(128)}, /*index=5*/s32[12]{...) while((s32[]{:T(128)}, f32[2,512]{1,0:T(2,128)S(1)}, ...), condition=%wide.region_6.6_spmd.clone, body=%wide.region_3.5_spmd.clone.sunk | while | flops 272632832 | bytes 9773301 | solution.py:105
  335.6 1.1 constant_dynamic-slice_fusion.4
  340.4 1.1 constant_dynamic-slice_fusion.4
  345.2 1.1 constant_dynamic-slice_fusion.4
  350.0 1.1 constant_dynamic-slice_fusion.4
  354.8 1.1 constant_dynamic-slice_fusion.4
  359.6 1.1 constant_dynamic-slice_fusion.4
  364.4 1.1 constant_dynamic-slice_fusion.4
  369.2 1.1 constant_dynamic-slice_fusion.4
  374.0 1.1 constant_dynamic-slice_fusion.4
  379.0 1.3 fusion.31
  382.5 48.5 %while.27 = (s32[]{:T(128)}, f32[2,512]{1,0:T(2,128)S(1)}, f32[2,512]{1,0:T(2,128)S(1)}, f32[2,512,128]{2,1,0:T(8,128)S(1)}, s32[]{:T(128)}, /*index=5*/s32[12]{...) while((s32[]{:T(128)}, f32[2,512]{1,0:T(2,128)S(1)}, ...), condition=%wide.region_6.6_spmd.clone, body=%wide.region_3.5_spmd.clone.sunk | while | flops 272632832 | bytes 9773301 | solution.py:105
  384.3 1.1 constant_dynamic-slice_fusion.4
  389.1 1.1 constant_dynamic-slice_fusion.4
  393.9 1.1 constant_dynamic-slice_fusion.4
  398.7 1.1 constant_dynamic-slice_fusion.4
  403.5 1.1 constant_dynamic-slice_fusion.4
  408.3 1.1 constant_dynamic-slice_fusion.4
  413.1 1.1 constant_dynamic-slice_fusion.4
  417.9 1.1 constant_dynamic-slice_fusion.4
  432.5 1.3 fusion.31
  436.0 48.5 %while.27 = (s32[]{:T(128)}, f32[2,512]{1,0:T(2,128)S(1)}, f32[2,512]{1,0:T(2,128)S(1)}, f32[2,512,128]{2,1,0:T(8,128)S(1)}, s32[]{:T(128)}, /*index=5*/s32[12]{...) while((s32[]{:T(128)}, f32[2,512]{1,0:T(2,128)S(1)}, ...), condition=%wide.region_6.6_spmd.clone, body=%wide.region_3.5_spmd.clone.sunk | while | flops 272632832 | bytes 9773301 | solution.py:105
  485.9 1.3 fusion.31
  489.4 53.3 %while.27 = (s32[]{:T(128)}, f32[2,512]{1,0:T(2,128)S(1)}, f32[2,512]{1,0:T(2,128)S(1)}, f32[2,512,128]{2,1,0:T(8,128)S(1)}, s32[]{:T(128)}, /*index=5*/s32[12]{...) while((s32[]{:T(128)}, f32[2,512]{1,0:T(2,128)S(1)}, ...), condition=%wide.region_6.6_spmd.clone, body=%wide.region_3.5_spmd.clone.sunk | while | flops 272632832 | bytes 9773301 | solution.py:105
  544.1 1.3 fusion.31
  547.6 53.3 %while.27 = (s32[]{:T(128)}, f32[2,512]{1,0:T(2,128)S(1)}, f32[2,512]{1,0:T(2,128)S(1)}, f32[2,512,128]{2,1,0:T(8,128)S(1)}, s32[]{:T(128)}, /*index=5*/s32[12]{...) while((s32[]{:T(128)}, f32[2,512]{1,0:T(2,128)S(1)}, ...), condition=%wide.region_6.6_spmd.clone, body=%wide.region_3.5_spmd.clone.sunk | while | flops 272632832 | bytes 9773301 | solution.py:105
  602.4 1.3 fusion.31
  605.9 58.1 %while.27 = (s32[]{:T(128)}, f32[2,512]{1,0:T(2,128)S(1)}, f32[2,512]{1,0:T(2,128)S(1)}, f32[2,512,128]{2,1,0:T(8,128)S(1)}, s32[]{:T(128)}, /*index=5*/s32[12]{...) while((s32[]{:T(128)}, f32[2,512]{1,0:T(2,128)S(1)}, ...), condition=%wide.region_6.6_spmd.clone, body=%wide.region_3.5_spmd.clone.sunk | while | flops 272632832 | bytes 9773301 | solution.py:105
  665.4 25.0 %all_to_all.19 = bf16[8,384,256]{2,1,0:T(8,128)(2,1)S(1)} all-to-all(bf16[8,384,256]{2,1,0:T(8,128)(2,1)} %bitcast.66), channel_id=1, replica_groups=mesh['section'=4,'head'=8] {'head'}, dimensions={0} | all-to-all | bytes 3145728 | tf_op jit(solution)/shard_map/all_to_all | solution.py:118
  690.3 1.6 copy.24
  692.0 8.5 %fusion.14 = bf16[384,2048]{1,0:T(8,128)(2,1)} fusion(bf16[384,2048]{1,0:T(8,128)(2,1)S(1)} %copy-done.2, bf16[384,2048]{0,1:T(8,128)(2,1)} %bitcast.67, bf16[2048,2048]{1,0:T(8,128)(2,1)} %all-gather.11.cloned.1.call-done), kind=kOutput, calls=%fused_computation.30 | convolution fusion | flops 3223584768 | bytes 13107200 | tf_op jit(solution)/shard_map/dot_general | solution.py:119
  (692 shorter events, 224.2 us)
Async XLA Ops:
  6.5 1.9 copy-start.1
  6.5 77.5 %all-gather.5.cloned.1.call-start = ((), (), s32[]{:S(2)}) async-start(), calls=%async_computation.1 | async-start | bytes 14155776 | tf_op jit(solution)/shard_map/all_gather | solution.py:39
  10.8 204.4 %all-gather.7.cloned.1.call-start = ((), (), s32[]{:S(2)}) async-start(), calls=%async_computation.2 | async-start | bytes 7864320 | tf_op jit(solution)/shard_map/all_gather | solution.py:56
  96.6 3.7 copy-start
  96.6 3.7 copy-start.3
  96.6 3.7 copy-start.4
  102.7 227.6 %all-gather.9.cloned.1.call-start = ((), (), s32[]{:S(2)}) async-start(), calls=%async_computation.3 | async-start | bytes 7864320 | tf_op jit(solution)/shard_map/all_gather | solution.py:57
  106.1 585.9 %all-gather.11.cloned.1.call-start = ((), (), s32[]{:S(2)}) async-start(), calls=%async_computation.4 | async-start | bytes 9437184 | tf_op jit(solution)/shard_map/all_gather | solution.py:121
  690.3 1.6 copy-start.2
Sparse Core Ops, SparseCore 0:
  10.9 73.0 all-gather.4
  102.8 112.3 all-gather.6
  216.7 113.5 all-gather.8
  332.0 55.5 all-gather.10
where the time goes:
time: 710 us; the launch traced here: 707 us
  waiting for transfers between devices  283 us (40%)
  local copies, waits for them, and re-layouts  138 us (19%)
  matrix products  105 us (15%)
  loops' own time  87 us (12%)
  other arithmetic  55.9 us (8%)
  blocking collectives  25 us (4%)
  between operations  13.2 us (2%)
    all_gather x1, waiting for transfers between devices, local(): lax.all_gather(values, 'section', axis=0, tiled=True)  115 us
    all_gather x1, waiting for transfers between devices, local(): lax.all_gather(keys, 'section', axis=0, tiled=True)  101 us
    another operation x6, loops' own time, one_block(): lax.fori_loop(0, live_slots, one_slot, start_state)  83.3 us
    dynamic_slice x63, local copies, waits for them, and re-layouts, one_slot(): lax.dynamic_slice_in_dim(values_all, source * BLK, BLK, 0)  67.6 us
    all_gather x1, waiting for transfers between devices, local(): piece = lax.all_gather(normed, 'head', axis=0, tiled=True)  66.1 us
    dot_general x63, matrix products, one_slot(): jnp.einsum('hqk,khd->hqd', weights.astype(jnp.bfloat16), value_block, pre...  44.4 us
    dot_general x63, matrix products, one_slot(): jnp.einsum('qhd,khd->hqk', query_block, key_block, preferred_element_type...  39.5 us
    dynamic_slice x63, local copies, waits for them, and re-layouts, one_slot(): source = block_row[slot]  36.3 us
  transfers between devices with their start and end apart: 4, of which 3 were waited for; matrix products, arithmetic and copies ran while one was open for 38% of the time, Pallas kernels for 0%

commit v1 on v0

--- a/solution.py
+++ b/solution.py
@@ -1,17 +1,22 @@
+import functools
 import math
 
 import jax
 import jax.numpy as jnp
 from jax import lax
+from jax.experimental import pallas as pl
+from jax.experimental.pallas import tpu as pltpu
 from jax.sharding import PartitionSpec as P
 
 D = 2048
 HD = 128
 BLK = 512
+TILE = 128
 
 
 EPS = 1e-05
 THETA = 10000.0
+VMEM_LIMIT = 56 * 1024 * 1024
 
 
 def rotate(vectors, cosine, sine):
@@ -23,7 +28,7 @@
     )
 
 
-def local(hidden_in, norm_gain, w_qkv, w_out, block_lists):
+def general(hidden_in, norm_gain, w_qkv, w_out, block_lists):
     section_id = lax.axis_index("section")
     width = w_qkv.shape[2]
     heads_here = width // HD
@@ -45,13 +50,9 @@
     angle = positions[:, None] * frequency[None, :]
     cosine = jnp.cos(angle)[:, None, :]
     sine = jnp.sin(angle)[:, None, :]
-    query_part = rotate(mixed_rows[:, 0], cosine, sine).astype(jnp.bfloat16).reshape(count, width)
-    key_part = rotate(mixed_rows[:, 1], cosine, sine).astype(jnp.bfloat16).reshape(count, width)
-    value_part = mixed_rows[:, 2].astype(jnp.bfloat16).reshape(count, width)
-    section_rows = jnp.concatenate([query_part, key_part, value_part], axis=1)
-    query = section_rows[:, :width]
-    keys = section_rows[:, width : 2 * width]
-    values = section_rows[:, 2 * width :]
+    query = rotate(mixed_rows[:, 0], cosine, sine).astype(jnp.bfloat16).reshape(count, width)
+    keys = rotate(mixed_rows[:, 1], cosine, sine).astype(jnp.bfloat16).reshape(count, width)
+    values = mixed_rows[:, 2].astype(jnp.bfloat16).reshape(count, width)
     keys_all, values_all = (
         lax.all_gather(keys, "section", axis=0, tiled=True),
         lax.all_gather(values, "section", axis=0, tiled=True),
@@ -124,6 +125,372 @@
     return (resid + summed).astype(jnp.bfloat16)
 
 
+def project_kernel(place, first, second, own, other, cosine, sine, *rest):
+    outs, (rows, weights, results, row_sems, weight_sems, out_sems) = rest[:4], rest[4:]
+    half = first.shape[0]
+    width = own.shape[1] // 3
+    row_copies = [
+        pltpu.make_async_copy(ref, rows.at[pl.ds(i * half, half)], row_sems.at[i])
+        for i, ref in enumerate((first, second))
+    ]
+    weight_copies = [
+        pltpu.make_async_copy(
+            ref.at[:, pl.ds(part * width, width)],
+            weights.at[w * 3 + part],
+            weight_sems.at[w * 3 + part],
+        )
+        for w, ref in enumerate((own, other))
+        for part in range(3)
+    ]
+    for copy in row_copies + weight_copies:
+        copy.start()
+    for copy in row_copies:
+        copy.wait()
+    query_scale = math.log2(math.e) / math.sqrt(HD)
+    for w in range(2):
+        for part in range(3):
+            weight_copies[w * 3 + part].wait()
+            product = jnp.dot(
+                rows[...], weights[w * 3 + part], preferred_element_type=jnp.float32
+            )
+            for h in range(2):
+                vector = product[:, h * HD : (h + 1) * HD]
+                if part < 2:
+                    vector = vector * cosine[...] + pltpu.roll(vector, HD // 2, 1) * sine[...]
+                if part == 0:
+                    vector = vector * query_scale
+                results[w * 2 + h, :, part * HD : (part + 1) * HD] = vector.astype(jnp.bfloat16)
+    copies = [
+        pltpu.make_async_copy(results.at[place[shift]], outs[shift], out_sems.at[shift])
+        for shift in range(4)
+    ]
+    for copy in copies:
+        copy.start()
+    for copy in copies:
+        copy.wait()
+
+
+def project(place, first, second, own, other, cosine, sine):
+    half = first.shape[0]
+    count = 2 * half
+    width = own.shape[1] // 3
+    any_space = pl.BlockSpec(memory_space=pl.ANY)
+    vmem = pl.BlockSpec(memory_space=pltpu.VMEM)
+    return pl.pallas_call(
+        project_kernel,
+        out_shape=[jax.ShapeDtypeStruct((count, 3 * HD), jnp.bfloat16)] * 4,
+        in_specs=[pl.BlockSpec(memory_space=pltpu.SMEM)] + [any_space] * 4 + [vmem] * 2,
+        out_specs=[any_space] * 4,
+        scratch_shapes=[
+            pltpu.VMEM((count, D), jnp.bfloat16),
+            pltpu.VMEM((6, D, width), jnp.bfloat16),
+            pltpu.VMEM((4, count, 3 * HD), jnp.bfloat16),
+            pltpu.SemaphoreType.DMA((2,)),
+            pltpu.SemaphoreType.DMA((6,)),
+            pltpu.SemaphoreType.DMA((4,)),
+        ],
+        compiler_params=pltpu.CompilerParams(vmem_limit_bytes=VMEM_LIMIT),
+        cost_estimate=pl.CostEstimate(
+            flops=2 * count * D * 6 * width, bytes_accessed=2 * 6 * D * width, transcendentals=0
+        ),
+        name="project_and_rotate",
+    )(place, first, second, own, other, cosine, sine)
+
+
+def attend_kernel(blocks_here, place, *rest):
+    lists, pieces, out = rest[:4], rest[4:36], rest[36]
+    rows, values_t, sems = rest[37:]
+    section, chip, core = place[0], place[1], place[2]
+    half = pieces[0].shape[0] // 2
+    tok = blocks_here * BLK
+    total_blocks = 4 * blocks_here
+    copies = []
+    for chunk in range(4):
+        for shift in range(4):
+            for far in range(2):
+                number = (chunk * 4 + shift) * 2 + far
+                source = lax.rem(section - shift + 4, 4)
+                side = core if far == 0 else 1 - core
+                for part in range(2):
+                    if chunk == 0:
+                        relative, which = 0, part
+                    elif chunk == 3:
+                        relative, which = 3, part
+                    else:
+                        relative, which = 1 + part, chunk - 1
+                    owner = chip ^ relative
+                    start = source * tok + owner * (4 * half) + side * (2 * half) + which * half
+                    copies.append(
+                        pltpu.make_async_copy(
+                            pieces[number].at[pl.ds(part * half, half)],
+                            rows.at[pl.ds(pl.multiple_of(start, half), half)],
+                            sems.at[number * 2 + part],
+                        )
+                    )
+    for copy in copies:
+        copy.start()
+    for copy in copies:
+        copy.wait()
+
+    def turn(i, carry):
+        at = pl.multiple_of(i * BLK, BLK)
+        values_t[:, pl.ds(at, BLK)] = rows[pl.ds(at, BLK), 2 * HD : 3 * HD].T
+        return carry
+
+    lax.fori_loop(0, total_blocks, turn, 0)
+
+    lane = lax.broadcasted_iota(jnp.int32, (BLK, 2 * TILE), 1)
+    key_at = lax.broadcasted_iota(jnp.int32, (BLK, 2 * TILE), 0)
+
+    for shift in range(4):
+        target = lax.rem(section + shift, 4)
+        block_list = lists[(4 - shift) % 4]
+
+        def one_block(local, carry, shift=shift, target=target, block_list=block_list):
+            block = target * blocks_here + local
+            middle = lax.rem(local, 3) == 1
+            offset = jnp.where(middle, core * TILE, core * 2 * TILE)
+            gap = jnp.where(middle, TILE, 0)
+            start = pl.multiple_of(block * BLK + offset, TILE)
+            later = pl.multiple_of(start + TILE + gap, TILE)
+            query = jnp.concatenate(
+                [rows[pl.ds(start, TILE), 0:HD], rows[pl.ds(later, TILE), 0:HD]], axis=0
+            )
+            live = jnp.int32(0)
+            for slot in range(block_list.shape[1]):
+                live = live + (block_list[local, slot] >= 0).astype(jnp.int32)
+
+            def scores_of(source):
+                at = pl.multiple_of(source * BLK, BLK)
+                return lax.dot_general(
+                    rows[pl.ds(at, BLK), HD : 2 * HD],
+                    query,
+                    (((1,), (1,)), ((), ())),
+                    preferred_element_type=jnp.float32,
+                )
+
+            def weigh(source, weights):
+                at = pl.multiple_of(source * BLK, BLK)
+                return jnp.dot(
+                    values_t[:, pl.ds(at, BLK)],
+                    weights.astype(jnp.bfloat16),
+                    preferred_element_type=jnp.float32,
+                )
+
+            query_at = offset + lane + jnp.where(lane >= TILE, gap, 0)
+            scores = jnp.where(key_at <= query_at, scores_of(block), -jnp.inf)
+            highest = jnp.max(scores, axis=0, keepdims=True)
+            weights = jnp.exp2(scores - highest)
+            total = jnp.sum(weights, axis=0, keepdims=True)
+            weighted = weigh(block, weights)
+
+            def one_slot(slot, state):
+                highest, total, weighted = state
+                source = block_list[local, slot]
+                scores = scores_of(source)
+                new_highest = jnp.maximum(highest, jnp.max(scores, axis=0, keepdims=True))
+                factor = jnp.exp2(highest - new_highest)
+                weights = jnp.exp2(scores - new_highest)
+                total = total * factor + jnp.sum(weights, axis=0, keepdims=True)
+                weighted = weighted * factor + weigh(source, weights)
+                return (new_highest, total, weighted)
+
+            _, total, weighted = lax.fori_loop(1, live, one_slot, (highest, total, weighted))
+            result = (weighted / total).T.astype(jnp.bfloat16)
+            for part in range(2):
+                tile = 2 * local + part
+                owner = tile // 3
+                where = (owner ^ chip) * 3 + lax.rem(tile, 3)
+                out[shift, where] = result[part * TILE : (part + 1) * TILE]
+            return carry
+
+        lax.fori_loop(0, blocks_here, one_block, 0)
+
+
+def attend(place, lists, pieces):
+    blocks_here = lists[0].shape[0]
+    tokens = 4 * blocks_here * BLK
+    tiles = blocks_here * 2
+    smem = pl.BlockSpec(memory_space=pltpu.SMEM)
+    pairs = tokens // BLK * lists[0].shape[1] // 2
+    return pl.pallas_call(
+        functools.partial(attend_kernel, blocks_here),
+        out_shape=jax.ShapeDtypeStruct((4, tiles, TILE, HD), jnp.bfloat16),
+        in_specs=[smem] * 5 + [pl.BlockSpec(memory_space=pl.ANY)] * 32,
+        out_specs=pl.BlockSpec(memory_space=pltpu.VMEM),
+        scratch_shapes=[
+            pltpu.VMEM((tokens, 3 * HD), jnp.bfloat16),
+            pltpu.VMEM((HD, tokens), jnp.bfloat16),
+            pltpu.SemaphoreType.DMA((64,)),
+        ],
+        compiler_params=pltpu.CompilerParams(vmem_limit_bytes=VMEM_LIMIT),
+        cost_estimate=pl.CostEstimate(
+            flops=pairs * 4 * BLK * 2 * TILE * HD,
+            bytes_accessed=tokens * 10 * HD,
+            transcendentals=pairs * BLK * 2 * TILE,
+        ),
+        name="attend_one_head",
+    )(place, *lists, *pieces)
+
+
+def finish_kernel(place, *rest):
+    parts, swapped, w_out, hidden, out = rest[:4], rest[4], rest[5], rest[6], rest[7]
+    attended, sems, swap_sems = rest[8:]
+    section, chip, core = place[0], place[1], place[2]
+    odd = lax.rem(chip, 2)
+
+    @pl.when(pl.program_id(0) == 0)
+    def _():
+        copies = []
+        for relative in range(4):
+            for shift in range(4):
+                head = (chip ^ relative) * 4 + lax.rem(section - shift + 4, 4)
+                column = pl.ds(pl.multiple_of(head * HD, HD), HD)
+                number = relative * 4 + shift
+                for kept in range(2):
+                    tile = kept + core
+                    to = jnp.where(
+                        core == 0, kept * (1 + odd), jnp.where(kept == 0, odd, 2)
+                    )
+                    copies.append(
+                        pltpu.make_async_copy(
+                            parts[relative].at[shift, tile],
+                            attended.at[pl.ds(pl.multiple_of(to * TILE, TILE), TILE), column],
+                            sems.at[number * 2 + kept],
+                        )
+                    )
+                to = jnp.where(core == 0, 2 - odd, 1 - odd)
+                copies.append(
+                    pltpu.make_async_copy(
+                        swapped.at[relative, shift],
+                        attended.at[pl.ds(pl.multiple_of(to * TILE, TILE), TILE), column],
+                        swap_sems.at[number],
+                    )
+                )
+        for copy in copies:
+            copy.start()
+        for copy in copies:
+            copy.wait()
+
+    summed = jnp.dot(attended[...], w_out[...], preferred_element_type=jnp.float32)
+    out[...] = (hidden[...].astype(jnp.float32) + summed).astype(jnp.bfloat16)
+
+
+def finish(place, parts, swapped, w_out, hidden):
+    count = hidden.shape[0]
+    step = 256
+    any_space = pl.BlockSpec(memory_space=pl.ANY)
+    return pl.pallas_call(
+        finish_kernel,
+        out_shape=jax.ShapeDtypeStruct((count, D), jnp.bfloat16),
+        grid=(D // step,),
+        in_specs=[pl.BlockSpec(memory_space=pltpu.SMEM)]
+        + [any_space] * 5
+        + [
+            pl.BlockSpec((D, step), lambda i: (0, i)),
+            pl.BlockSpec((count, step), lambda i: (0, i)),
+        ],
+        out_specs=pl.BlockSpec((count, step), lambda i: (0, i)),
+        scratch_shapes=[
+            pltpu.VMEM((count, D), jnp.bfloat16),
+            pltpu.SemaphoreType.DMA((32,)),
+            pltpu.SemaphoreType.DMA((16,)),
+        ],
+        compiler_params=pltpu.CompilerParams(
+            vmem_limit_bytes=VMEM_LIMIT, dimension_semantics=("arbitrary",)
+        ),
+        cost_estimate=pl.CostEstimate(
+            flops=2 * count * D * D, bytes_accessed=2 * D * D, transcendentals=0
+        ),
+        name="project_out",
+    )(place, *parts, swapped, w_out, hidden)
+
+
+def by_head(hidden_in, norm_gain, w_qkv, w_out, block_lists):
+    section = lax.axis_index("section")
+    device = lax.axis_index("head")
+    chip, core = device // 2, device % 2
+    width = w_qkv.shape[2]
+    blocks_here = block_lists.shape[0]
+    tok = blocks_here * BLK
+    rows = hidden_in.shape[0]
+    half = rows // 2
+
+    other_core = [(i, i ^ 1) for i in range(8)]
+    along_x = [(i, i ^ 2) for i in range(8)]
+    along_y = [(i, i ^ 4) for i in range(8)]
+    diagonal = [(i, i ^ 6) for i in range(8)]
+
+    def to_section(array, shift):
+        return lax.ppermute(array, "section", [(i, (i + shift) % 4) for i in range(4)])
+
+    place = jnp.stack([section, chip, core]).astype(jnp.int32)
+    shifts = jnp.arange(4, dtype=jnp.int32)
+    chosen = (section + shifts - 2 * core + 4) % 4
+
+    own = w_qkv.reshape(D, 3 * width)
+    other = lax.ppermute(own, "head", other_core)
+    lists = [block_lists] + [to_section(block_lists, shift) for shift in range(1, 4)]
+
+    resid = hidden_in.astype(jnp.float32)
+    normed = (
+        resid * lax.rsqrt(jnp.mean(resid * resid, axis=-1, keepdims=True) + EPS) * norm_gain
+    ).astype(jnp.bfloat16)
+    low, high = normed[:half], normed[half:]
+    x_low = lax.ppermute(low, "head", along_x)
+    y_low = lax.ppermute(low, "head", along_y)
+    x_high = lax.ppermute(high, "head", along_x)
+    y_high = lax.ppermute(high, "head", along_y)
+    d_low = lax.ppermute(y_low, "head", along_x)
+    d_high = lax.ppermute(x_high, "head", along_y)
+    chunks = [(low, high), (x_low, y_low), (x_high, y_high), (d_low, d_high)]
+    origins = [
+        ((0, 0), (0, 1)),
+        ((1, 0), (2, 0)),
+        ((1, 1), (2, 1)),
+        ((3, 0), (3, 1)),
+    ]
+
+    frequency = THETA ** (-(2.0 * jnp.arange(HD // 2, dtype=jnp.float32)) / HD)
+    starts = jnp.stack(
+        [
+            section * tok + (chip ^ relative) * (2 * rows) + core * rows + which * half
+            for chunk in origins
+            for relative, which in chunk
+        ]
+    )
+    positions = (starts[:, None] + jnp.arange(half, dtype=jnp.int32)[None, :]).reshape(4, rows)
+    angle = positions.astype(jnp.float32)[:, :, None] * frequency
+    cosine, sine = jnp.cos(angle), jnp.sin(angle)
+    cosine = jnp.concatenate([cosine, cosine], axis=-1)
+    sine = jnp.concatenate([-sine, sine], axis=-1)
+
+    pieces = []
+    for number, (first, second) in enumerate(chunks):
+        outs = project(chosen, first, second, own, other, cosine[number], sine[number])
+        for shift in range(4):
+            arrived = outs[shift] if shift == 0 else to_section(outs[shift], shift)
+            pieces += [arrived, lax.ppermute(arrived, "head", other_core)]
+
+    late_w_out, _, _ = lax.optimization_barrier((w_out, d_low, d_high))
+    w_out_all = lax.all_gather(late_w_out, "head", axis=0, tiled=True)
+
+    attended = attend(place, lists, pieces)
+    back = [attended[0]] + [to_section(attended[shift], shift) for shift in range(1, 4)]
+    back = jnp.stack(back).reshape(4, 4, 3, TILE, HD)
+    parts = [back[:, 0]] + [
+        lax.ppermute(back[:, relative], "head", perm)
+        for relative, perm in ((1, along_x), (2, along_y), (3, diagonal))
+    ]
+    given = jnp.where(core == 0, 2, 0)
+    swapped = lax.ppermute(
+        jnp.stack([lax.dynamic_index_in_dim(part, given, 1, keepdims=False) for part in parts]),
+        "head",
+        other_core,
+    )
+    return finish(place, parts, swapped, w_out_all, hidden_in)
+
+
 def solution(mesh):
     placed = (
         P(("section", "head"), None),
@@ -132,6 +499,17 @@
         P("head", None),
         P("section", None),
     )
+
+    def local(hidden_in, norm_gain, w_qkv, w_out, block_lists):
+        fits = (
+            mesh.shape["section"] == 4
+            and mesh.shape["head"] == 8
+            and w_qkv.shape[2] == 2 * HD
+            and block_lists.shape[0] % 6 == 0
+        )
+        form = by_head if fits else general
+        return form(hidden_in, norm_gain, w_qkv, w_out, block_lists)
+
     return jax.shard_map(
         local, mesh=mesh, in_specs=placed, out_specs=P(("section", "head"), None), check_vma=False
     )

time: 710 us -> 363 us (0.51)
  the two profiles are of different devices: /device:TPU:24 before, /device:TPU:0 now
where the time goes in v1:
time: 363 us
  Pallas kernels  145 us (40%)
  waiting for transfers between devices  113 us (31%)
  starting transfers between devices  70.4 us (19%)
  between operations  14.1 us (4%)
  local copies, waits for them, and re-layouts  12 us (3%)
  other arithmetic  8.3 us (2%)
    pallas_call x1, Pallas kernels, attend(): pl.pallas_call(functools.partial(attend_kernel, blocks_here), out_shape=j...  89.3 us
    ppermute x18, starting transfers between devices, to_section(): lax.ppermute(array, 'section', [(i, (i + shift) % 4) for i in range(4)])  54.1 us
    ppermute x18, waiting for transfers between devices, to_section(): lax.ppermute(array, 'section', [(i, (i + shift) % 4) for i in range(4)])  52.3 us
    pallas_call x4, Pallas kernels, project(): pl.pallas_call(project_kernel, out_shape=[jax.ShapeDtypeStruct((count, 3...  45.2 us
    ppermute x3, waiting for transfers between devices, by_head(): lax.ppermute(back[:, relative], 'head', perm)  16.2 us
    ppermute x1, waiting for transfers between devices, by_head(): y_low = lax.ppermute(low, 'head', along_y)  16 us
    ppermute x1, waiting for transfers between devices, by_head(): d_low = lax.ppermute(y_low, 'head', along_x)  15.4 us
    pallas_call x1, Pallas kernels, finish(): pl.pallas_call(finish_kernel, out_shape=jax.ShapeDtypeStruct((count, D),...  11 us
  transfers between devices with their start and end apart: 46, of which 19 were waited for; matrix products, arithmetic and copies ran while one was open for 4% of the time, Pallas kernels for 37%

profile of v1, /device:TPU:0, one launch (start us, length us, event | category | flops | bytes accessed | tf_op | source)
XLA Modules:
  0.0 362.8 jit_solution(13141980832801217765)
XLA Ops:
  6.5 1.9 fusion
  9.1 3.0 collective-permute-start.12
  12.1 1.5 collective-permute-start.20
  13.6 16.0 %collective-permute-done.12.second = bf16[192,2048]{1,0:T(8,128)(2,1)S(1)} collective-permute-done((bf16[192,2048]{1,0:T(8,128)(2,1)S(1)}, bf16[192,2048]{1,0:T(8,128)(2,1)S(1)}, u32[]{:S(2)}, u32[]{:S(2)}) %collective-permute-start.12) | collective-permute-done | bytes 786464 | tf_op jit(solution)/shard_map/ppermute | solution.py:441
  29.7 1.7 collective-permute-start.29
  31.4 1.6 collective-permute-start.30
  33.0 15.4 %collective-permute-done.29.first = bf16[192,2048]{1,0:T(8,128)(2,1)S(1)} collective-permute-done((bf16[192,2048]{1,0:T(8,128)(2,1)S(1)}, bf16[192,2048]{1,0:T(8,128)(2,1)S(1)}, u32[]{:S(2)}, u32[]{:S(2)}) %collective-permute-start.29) | collective-permute-done | bytes 786464 | tf_op jit(solution)/shard_map/ppermute | solution.py:444
  48.4 0.9 copy-done.9
  49.7 3.2 copy.7
  53.0 2.9 copy.9.own
  55.8 1.6 collective-permute-start
  57.4 2.6 collective-permute-start.1
  60.0 1.1 collective-permute-start.11
  61.1 1.4 collective-permute-start.21
  63.0 2.8 multiply_sine_fusion
  66.4 1.6 fusion.16
  68.0 11.3 %project_and_rotate.4 = (bf16[384,384]{1,0:T(8,128)(2,1)}, bf16[384,384]{1,0:T(8,128)(2,1)}, bf16[384,384]{1,0:T(8,128)(2,1)}, bf16[384,384]{1,0:T(8,128)(2,1)}) custom-call(s32[4]{0:T(128)} %and_select_fusion.place, bf16[192,2048]{1,0:T(8,128)(2,1)} %copy-done.2, bf16[192,2048]{1,0:T(8,128)(2,1)} %copy-done.1, bf16[2048,768]{1,0:T(8,128)(2,1)} %copy.9.own, ...), custom_call_target="tpu_custom_call" | custom-call | flops 2415919104 | bytes 6291456 | tf_op jit(solution)/shard_map/project_and_rotate/pallas_call | solution.py:179
  79.6 1.7 collective-permute-start.7
  81.3 8.0 %collective-permute-done.11.first = bf16[192,2048]{1,0:T(8,128)(2,1)} collective-permute-done((bf16[192,2048]{1,0:T(8,128)(2,1)}, bf16[192,2048]{1,0:T(8,128)(2,1)}, u32[]{:S(2)}, u32[]{:S(2)}) %collective-permute-start.11) | collective-permute-done | bytes 786464 | tf_op jit(solution)/shard_map/ppermute | solution.py:440
  89.3 3.0 collective-permute-start.2
  92.3 11.4 %project_and_rotate.5 = (bf16[384,384]{1,0:T(8,128)(2,1)}, bf16[384,384]{1,0:T(8,128)(2,1)}, bf16[384,384]{1,0:T(8,128)(2,1)}, bf16[384,384]{1,0:T(8,128)(2,1)}) custom-call(s32[4]{0:T(128)} %and_select_fusion.place, bf16[192,2048]{1,0:T(8,128)(2,1)} %collective-permute-done.11.first, bf16[192,2048]{1,0:T(8,128)(2,1)} %copy-done.11, ...), custom_call_target="tpu_custom_call" | custom-call | flops 2415919104 | bytes 6291456 | tf_op jit(solution)/shard_map/project_and_rotate/pallas_call | solution.py:179
  103.7 0.9 collective-permute-start.9
  104.7 1.2 collective-permute-start.14
  106.0 2.6 collective-permute-start.18
  108.6 11.2 %project_and_rotate.7 = (bf16[384,384]{1,0:T(8,128)(2,1)}, bf16[384,384]{1,0:T(8,128)(2,1)}, bf16[384,384]{1,0:T(8,128)(2,1)}, bf16[384,384]{1,0:T(8,128)(2,1)}) custom-call(s32[4]{0:T(128)} %and_select_fusion.place, bf16[192,2048]{1,0:T(8,128)(2,1)} %copy-done.9, bf16[192,2048]{1,0:T(8,128)(2,1)} %collective-permute-done.30.second, ...), custom_call_target="tpu_custom_call" | custom-call | flops 2415919104 | bytes 6291456 | tf_op jit(solution)/shard_map/project_and_rotate/pallas_call | solution.py:179
  119.9 11.3 %project_and_rotate.6 = (bf16[384,384]{1,0:T(8,128)(2,1)}, bf16[384,384]{1,0:T(8,128)(2,1)}, bf16[384,384]{1,0:T(8,128)(2,1)}, bf16[384,384]{1,0:T(8,128)(2,1)}) custom-call(s32[4]{0:T(128)} %and_select_fusion.place, bf16[192,2048]{1,0:T(8,128)(2,1)} %copy-done.8, bf16[192,2048]{1,0:T(8,128)(2,1)} %copy-done.10, bf16[2048,768]{1,0:T(8,128)(2,1)} %copy.9.own, ...), custom_call_target="tpu_custom_call" | custom-call | flops 2415919104 | bytes 6291456 | tf_op jit(solution)/shard_map/project_and_rotate/pallas_call | solution.py:179
  131.4 0.8 collective-permute-start.23
  132.2 1.6 collective-permute-start.25
  133.8 6.9 %collective-permute-start.27 = (bf16[384,384]{1,0:T(8,128)(2,1)}, bf16[384,384]{1,0:T(8,128)(2,1)S(1)}, u32[]{:S(2)}, u32[]{:S(2)}) collective-permute-start(bf16[384,384]{1,0:T(8,128)(2,1)} %get-tuple-element.33), channel_id=1, source_target_pairs={{0,24},{8,0},{16,8},{24,16},{1,25},{9,1},{17,9},{25,17},{2,26},{10... | collective-permute-start | bytes 884744 | tf_op jit(solution)/shard_map/ppermute | solution.py:425
  140.8 9.4 %collective-permute-start.32 = (bf16[384,384]{1,0:T(8,128)(2,1)S(1)}, bf16[384,384]{1,0:T(8,128)(2,1)S(1)}, u32[]{:S(2)}, u32[]{:S(2)}) collective-permute-start(bf16[384,384]{1,0:T(8,128)(2,1)S(1)} %copy-done.36), channel_id=1, source_target_pairs={{0,8},{8,16},{16,24},{24,0},{1,9},{9,17},{17,25},{25,1},{2,10},{10... | collective-permute-start | bytes 884744 | tf_op jit(solution)/shard_map/ppermute | solution.py:425
  150.1 8.6 %collective-permute-start.34 = (bf16[384,384]{1,0:T(8,128)(2,1)S(1)}, bf16[384,384]{1,0:T(8,128)(2,1)S(1)}, u32[]{:S(2)}, u32[]{:S(2)}) collective-permute-start(bf16[384,384]{1,0:T(8,128)(2,1)S(1)} %copy-done.33), channel_id=1, source_target_pairs={{0,16},{8,24},{16,0},{24,8},{1,17},{9,25},{17,1},{25,9},{2,18},{10... | collective-permute-start | bytes 884744 | tf_op jit(solution)/shard_map/ppermute | solution.py:425
  158.7 9.8 %collective-permute-done.25.rest_24_ = bf16[384,384]{1,0:T(8,128)(2,1)S(1)} collective-permute-done((bf16[384,384]{1,0:T(8,128)(2,1)}, bf16[384,384]{1,0:T(8,128)(2,1)S(1)}, u32[]{:S(2)}, u32[]{:S(2)}) %collective-permute-start.25) | collective-permute-done | bytes 294944 | tf_op jit(solution)/shard_map/ppermute | solution.py:425
  168.6 3.7 %collective-permute-start.36 = (bf16[384,384]{1,0:T(8,128)(2,1)S(1)}, bf16[384,384]{1,0:T(8,128)(2,1)S(1)}, u32[]{:S(2)}, u32[]{:S(2)}) collective-permute-start(bf16[384,384]{1,0:T(8,128)(2,1)S(1)} %copy-done.31), channel_id=1, source_target_pairs={{0,24},{8,0},{16,8},{24,16},{1,25},{9,1},{17,9},{25,17},{2,26},{10... | collective-permute-start | bytes 884744 | tf_op jit(solution)/shard_map/ppermute | solution.py:425
  173.0 8.2 %collective-permute-done.34.rest_32_ = bf16[384,384]{1,0:T(8,128)(2,1)S(1)} collective-permute-done((bf16[384,384]{1,0:T(8,128)(2,1)S(1)}, bf16[384,384]{1,0:T(8,128)(2,1)S(1)}, u32[]{:S(2)}, u32[]{:S(2)}) %collective-permute-start.34) | collective-permute-done | bytes 294944 | tf_op jit(solution)/shard_map/ppermute | solution.py:425
  181.2 1.8 collective-permute-done.36.rest_34_
  187.9 0.7 copy-done.44
  188.6 89.3 %attend_one_head.1 = bf16[4,12,128,128]{3,2,1,0:T(8,128)(2,1)} custom-call(s32[3]{0:T(128)} %pad_add_fusion.place, s32[6,12]{1,0:T(8,128)} %rest_0_.1, s32[6,12]{1,0:T(8,128)} %copy-done.46, s32[6,12]{1,0:T(8,128)} %copy-done.47, s32[6,12]{1,0:T(8,128)} %copy-done.48, bf16[384,384]{1,0:T(8,128)(2,1)} %get-tuple-element.22.rest_4_, ...), custom_call_target="tpu_custom_call" | custom-call | flops 9663676416 | bytes 15728640 | tf_op jit(solution)/shard_map/attend_one_head/pallas_call | solution.py:316
  277.9 1.5 fusion.20
  279.4 8.6 %collective-permute-start.40 = (bf16[12,128,128]{2,1,0:T(8,128)(2,1)S(1)}, bf16[12,128,128]{2,1,0:T(8,128)(2,1)S(1)}, u32[]{:S(2)}, u32[]{:S(2)}) collective-permute-start(bf16[12,128,128]{2,1,0:T(8,128)(2,1)S(1)} %get-tuple-element.45), channel_id=1, source_target_pairs={{0,24},{8,0},{16,8},{24,16},{1,25},{9,1},{17,9},{25,17},{2,26},{10... | collective-permute-start | bytes 1179656 | tf_op jit(solution)/shard_map/ppermute | solution.py:425
  288.6 8.9 %collective-permute-done.40 = bf16[12,128,128]{2,1,0:T(8,128)(2,1)S(1)} collective-permute-done((bf16[12,128,128]{2,1,0:T(8,128)(2,1)S(1)}, bf16[12,128,128]{2,1,0:T(8,128)(2,1)S(1)}, u32[]{:S(2)}, u32[]{:S(2)}) %collective-permute-start.40) | collective-permute-done | bytes 393248 | tf_op jit(solution)/shard_map/ppermute | solution.py:425
  297.5 23.4 %collective-permute-done.39 = bf16[12,128,128]{2,1,0:T(8,128)(2,1)S(1)} collective-permute-done((bf16[12,128,128]{2,1,0:T(8,128)(2,1)S(1)}, bf16[12,128,128]{2,1,0:T(8,128)(2,1)S(1)}, u32[]{:S(2)}, u32[]{:S(2)}) %collective-permute-start.39) | collective-permute-done | bytes 393248 | tf_op jit(solution)/shard_map/ppermute | solution.py:425
  321.2 1.2 fusion.19
  322.3 2.4 collective-permute-start.43
  325.8 9.5 %collective-permute-done.43.rest_3_ = bf16[4,3,128,128]{3,2,1,0:T(8,128)(2,1)S(1)} collective-permute-done((bf16[4,3,128,128]{3,2,1,0:T(8,128)(2,1)S(1)}, bf16[4,3,128,128]{3,2,1,0:T(8,128)(2,1)S(1)}, u32[]{:S(2)}, u32[]{:S(2)}) %collective-permute-start.43) | collective-permute-done | bytes 393248 | tf_op jit(solution)/shard_map/ppermute | solution.py:482
  335.3 6.6 %collective-permute-done.42.rest_2_ = bf16[4,3,128,128]{3,2,1,0:T(8,128)(2,1)S(1)} collective-permute-done((bf16[4,3,128,128]{3,2,1,0:T(8,128)(2,1)S(1)}, bf16[4,3,128,128]{3,2,1,0:T(8,128)(2,1)S(1)}, u32[]{:S(2)}, u32[]{:S(2)}) %collective-permute-start.42) | collective-permute-done | bytes 393248 | tf_op jit(solution)/shard_map/ppermute | solution.py:482
  342.2 1.9 collective-permute-done.44.rest_4_
  344.1 0.8 copy-done.6
  344.9 11.0 %project_out.1 = bf16[384,2048]{1,0:T(8,128)(2,1)} custom-call(s32[3]{0:T(128)} %pad_add_fusion.place, bf16[4,3,128,128]{3,2,1,0:T(8,128)(2,1)} %get-tuple-element.40.rest_0_, bf16[4,3,128,128]{3,2,1,0:T(8,128)(2,1)} %copy-done.5, bf16[4,3,128,128]{3,2,1,0:T(8,128)(2,1)} %copy-done.4, bf16[4,3,128,128]{3,2,1,0:T(8,128)(2,1)} %copy-done.3, ...), custom_call_target="tpu_custom_call" | custom-call | flops 3221225472 | bytes 8388608 | tf_op jit(solution)/shard_map/project_out/pallas_call | solution.py:383
  (175 shorter events, 10.3 us)
Async XLA Ops:
  6.5 337.6 %all-gather.2.cloned.1.call-start = ((), (), s32[]{:S(2)}) async-start(), calls=%async_computation | async-start | bytes 9437184 | tf_op jit(solution)/shard_map/all_gather | solution.py:476
  9.1 20.6 %collective-permute-start.12 = (bf16[192,2048]{1,0:T(8,128)(2,1)S(1)}, bf16[192,2048]{1,0:T(8,128)(2,1)S(1)}, u32[]{:S(2)}, u32[]{:S(2)}) collective-permute-start(bf16[192,2048]{1,0:T(8,128)(2,1)S(1)} %get-tuple-element.53.first), channel_id=1, source_target_pairs={{0,4},{1,5},{2,6},{3,7},{4,0},{5,1},{6,2},{7,3},{8,12},{9,13},{10,... | collective-permute-start | bytes 2359304 | tf_op jit(solution)/shard_map/ppermute | solution.py:441
  12.1 19.3 %collective-permute-start.20 = (bf16[192,2048]{1,0:T(8,128)(2,1)S(1)}, bf16[192,2048]{1,0:T(8,128)(2,1)S(1)}, u32[]{:S(2)}, u32[]{:S(2)}) collective-permute-start(bf16[192,2048]{1,0:T(8,128)(2,1)S(1)} %get-tuple-element.52.second), channel_id=1, source_target_pairs={{0,2},{1,3},{2,0},{3,1},{4,6},{5,7},{6,4},{7,5},{8,10},{9,11},{10,... | collective-permute-start | bytes 2359304 | tf_op jit(solution)/shard_map/ppermute | solution.py:442
  29.7 18.7 %collective-permute-start.29 = (bf16[192,2048]{1,0:T(8,128)(2,1)S(1)}, bf16[192,2048]{1,0:T(8,128)(2,1)S(1)}, u32[]{:S(2)}, u32[]{:S(2)}) collective-permute-start(bf16[192,2048]{1,0:T(8,128)(2,1)S(1)} %collective-permute-done.12.second), channel_id=1, source_target_pairs={{0,2},{1,3},{2,0},{3,1},{4,6},{5,7},{6,4},{7,5},{8,10},{9,11},{10,... | collective-permute-start | bytes 2359304 | tf_op jit(solution)/shard_map/ppermute | solution.py:444
  31.4 18.3 %collective-permute-start.30 = (bf16[192,2048]{1,0:T(8,128)(2,1)S(1)}, bf16[192,2048]{1,0:T(8,128)(2,1)}, u32[]{:S(2)}, u32[]{:S(2)}) collective-permute-start(bf16[192,2048]{1,0:T(8,128)(2,1)S(1)} %collective-permute-done.20.first), channel_id=1, source_target_pairs={{0,4},{1,5},{2,6},{3,7},{4,0},{5,1},{6,2},{7,3},{8,12},{9,13},{10,... | collective-permute-start | bytes 2359304 | tf_op jit(solution)/shard_map/ppermute | solution.py:445
  55.8 12.2 %collective-permute-start.3 = (bf16[2048,768]{1,0:T(8,128)(2,1)}, bf16[2048,768]{1,0:T(8,128)(2,1)}, u32[]{:S(2)}, u32[]{:S(2)}) collective-permute-start(bf16[2048,768]{1,0:T(8,128)(2,1)} %copy.9.own), channel_id=1, source_target_pairs={{0,1},{1,0},{2,3},{3,2},{4,5},{5,4},{6,7},{7,6},{8,9},{9,8},{10,11... | collective-permute-start | bytes 9437192 | tf_op jit(solution)/shard_map/ppermute | solution.py:432
  55.8 23.5 %collective-permute-start = (s32[6,12]{1,0:T(8,128)S(1)}, s32[6,12]{1,0:T(8,128)S(1)}, u32[]{:S(2)}, u32[]{:S(2)}) collective-permute-start(s32[6,12]{1,0:T(8,128)S(1)} %copy-done.45), channel_id=1, source_target_pairs={{0,8},{8,16},{16,24},{24,0},{1,9},{9,17},{17,25},{25,1},{2,10},{10... | collective-permute-start | bytes 872 | tf_op jit(solution)/shard_map/ppermute | solution.py:425
  57.4 22.2 %collective-permute-start.1 = (s32[6,12]{1,0:T(8,128)S(1)}, s32[6,12]{1,0:T(8,128)S(1)}, u32[]{:S(2)}, u32[]{:S(2)}) collective-permute-start(s32[6,12]{1,0:T(8,128)S(1)} %copy-done.45), channel_id=1, source_target_pairs={{0,16},{8,24},{16,0},{24,8},{1,17},{9,25},{17,1},{25,9},{2,18},{10... | collective-permute-start | bytes 872 | tf_op jit(solution)/shard_map/ppermute | solution.py:425
  60.0 29.3 %collective-permute-start.11 = (bf16[192,2048]{1,0:T(8,128)(2,1)}, bf16[192,2048]{1,0:T(8,128)(2,1)}, u32[]{:S(2)}, u32[]{:S(2)}) collective-permute-start(bf16[192,2048]{1,0:T(8,128)(2,1)} %copy-done.2), channel_id=1, source_target_pairs={{0,2},{1,3},{2,0},{3,1},{4,6},{5,7},{6,4},{7,5},{8,10},{9,11},{10,... | collective-permute-start | bytes 2359304 | tf_op jit(solution)/shard_map/ppermute | solution.py:440
  61.1 43.5 %collective-permute-start.21 = (bf16[192,2048]{1,0:T(8,128)(2,1)}, bf16[192,2048]{1,0:T(8,128)(2,1)S(1)}, u32[]{:S(2)}, u32[]{:S(2)}) collective-permute-start(bf16[192,2048]{1,0:T(8,128)(2,1)} %copy-done.1), channel_id=1, source_target_pairs={{0,4},{1,5},{2,6},{3,7},{4,0},{5,1},{6,2},{7,3},{8,12},{9,13},{10,... | collective-permute-start | bytes 2359304 | tf_op jit(solution)/shard_map/ppermute | solution.py:443
  79.3 25.4 %collective-permute-start.4 = (bf16[384,384]{1,0:T(8,128)(2,1)}, bf16[384,384]{1,0:T(8,128)(2,1)S(1)}, u32[]{:S(2)}, u32[]{:S(2)}) collective-permute-start(bf16[384,384]{1,0:T(8,128)(2,1)} %get-tuple-element.22.rest_4_), channel_id=1, source_target_pairs={{0,1},{1,0},{2,3},{3,2},{4,5},{5,4},{6,7},{7,6},{8,9},{9,8},{10,11... | collective-permute-start | bytes 884744 | tf_op jit(solution)/shard_map/ppermute | solution.py:473
  79.4 26.5 %collective-permute-start.5 = (bf16[384,384]{1,0:T(8,128)(2,1)}, bf16[384,384]{1,0:T(8,128)(2,1)S(1)}, u32[]{:S(2)}, u32[]{:S(2)}) collective-permute-start(bf16[384,384]{1,0:T(8,128)(2,1)} %get-tuple-element.23), channel_id=1, source_target_pairs={{0,8},{8,16},{16,24},{24,0},{1,9},{9,17},{17,25},{25,1},{2,10},{10... | collective-permute-start | bytes 884744 | tf_op jit(solution)/shard_map/ppermute | solution.py:425
  79.6 26.4 %collective-permute-start.7 = (bf16[384,384]{1,0:T(8,128)(2,1)}, bf16[384,384]{1,0:T(8,128)(2,1)S(1)}, u32[]{:S(2)}, u32[]{:S(2)}) collective-permute-start(bf16[384,384]{1,0:T(8,128)(2,1)} %get-tuple-element.24), channel_id=1, source_target_pairs={{0,16},{8,24},{16,0},{24,8},{1,17},{9,25},{17,1},{25,9},{2,18},{10... | collective-permute-start | bytes 884744 | tf_op jit(solution)/shard_map/ppermute | solution.py:425
  89.3 14.4 %collective-permute-start.2 = (s32[6,12]{1,0:T(8,128)S(1)}, s32[6,12]{1,0:T(8,128)S(1)}, u32[]{:S(2)}, u32[]{:S(2)}) collective-permute-start(s32[6,12]{1,0:T(8,128)S(1)} %copy-done.45), channel_id=1, source_target_pairs={{0,24},{8,0},{16,8},{24,16},{1,25},{9,1},{17,9},{25,17},{2,26},{10... | collective-permute-start | bytes 872 | tf_op jit(solution)/shard_map/ppermute | solution.py:425
  103.7 27.6 %collective-permute-start.9 = (bf16[384,384]{1,0:T(8,128)(2,1)S(1)}, bf16[384,384]{1,0:T(8,128)(2,1)S(1)}, u32[]{:S(2)}, u32[]{:S(2)}) collective-permute-start(bf16[384,384]{1,0:T(8,128)(2,1)S(1)} %copy-done.35), channel_id=1, source_target_pairs={{0,24},{8,0},{16,8},{24,16},{1,25},{9,1},{17,9},{25,17},{2,26},{10... | collective-permute-start | bytes 884744 | tf_op jit(solution)/shard_map/ppermute | solution.py:425
  104.6 26.7 %collective-permute-start.13 = (bf16[384,384]{1,0:T(8,128)(2,1)}, bf16[384,384]{1,0:T(8,128)(2,1)S(1)}, u32[]{:S(2)}, u32[]{:S(2)}) collective-permute-start(bf16[384,384]{1,0:T(8,128)(2,1)} %get-tuple-element.26.rest_12_), channel_id=1, source_target_pairs={{0,1},{1,0},{2,3},{3,2},{4,5},{5,4},{6,7},{7,6},{8,9},{9,8},{10,11... | collective-permute-start | bytes 884744 | tf_op jit(solution)/shard_map/ppermute | solution.py:473
  104.7 27.5 %collective-permute-start.14 = (bf16[384,384]{1,0:T(8,128)(2,1)}, bf16[384,384]{1,0:T(8,128)(2,1)S(1)}, u32[]{:S(2)}, u32[]{:S(2)}) collective-permute-start(bf16[384,384]{1,0:T(8,128)(2,1)} %get-tuple-element.27), channel_id=1, source_target_pairs={{0,8},{8,16},{16,24},{24,0},{1,9},{9,17},{17,25},{25,1},{2,10},{10... | collective-permute-start | bytes 884744 | tf_op jit(solution)/shard_map/ppermute | solution.py:425
  105.9 66.4 %copy-start.13 = (bf16[384,384]{1,0:T(8,128)(2,1)}, bf16[384,384]{1,0:T(8,128)(2,1)S(1)}, u32[]{:S(2)}) copy-start(bf16[384,384]{1,0:T(8,128)(2,1)S(1)} %collective-permute-done.5.rest_6_) | copy-start | bytes 884740
  105.9 27.9 %collective-permute-start.16 = (bf16[384,384]{1,0:T(8,128)(2,1)}, bf16[384,384]{1,0:T(8,128)(2,1)S(1)}, u32[]{:S(2)}, u32[]{:S(2)}) collective-permute-start(bf16[384,384]{1,0:T(8,128)(2,1)} %get-tuple-element.28), channel_id=1, source_target_pairs={{0,16},{8,24},{16,0},{24,8},{1,17},{9,25},{17,1},{25,9},{2,18},{10... | collective-permute-start | bytes 884744 | tf_op jit(solution)/shard_map/ppermute | solution.py:425
  106.0 66.3 %copy-start.14 = (bf16[384,384]{1,0:T(8,128)(2,1)}, bf16[384,384]{1,0:T(8,128)(2,1)S(1)}, u32[]{:S(2)}) copy-start(bf16[384,384]{1,0:T(8,128)(2,1)S(1)} %collective-permute-done.7.rest_8_) | copy-start | bytes 884740
  106.0 34.6 %collective-permute-start.18 = (bf16[384,384]{1,0:T(8,128)(2,1)}, bf16[384,384]{1,0:T(8,128)(2,1)S(1)}, u32[]{:S(2)}, u32[]{:S(2)}) collective-permute-start(bf16[384,384]{1,0:T(8,128)(2,1)} %get-tuple-element.29), channel_id=1, source_target_pairs={{0,24},{8,0},{16,8},{24,16},{1,25},{9,1},{17,9},{25,17},{2,26},{10... | collective-permute-start | bytes 884744 | tf_op jit(solution)/shard_map/ppermute | solution.py:425
  131.3 9.4 %collective-permute-start.22 = (bf16[384,384]{1,0:T(8,128)(2,1)}, bf16[384,384]{1,0:T(8,128)(2,1)S(1)}, u32[]{:S(2)}, u32[]{:S(2)}) collective-permute-start(bf16[384,384]{1,0:T(8,128)(2,1)} %get-tuple-element.30.rest_20_), channel_id=1, source_target_pairs={{0,1},{1,0},{2,3},{3,2},{4,5},{5,4},{6,7},{7,6},{8,9},{9,8},{10,11... | collective-permute-start | bytes 884744 | tf_op jit(solution)/shard_map/ppermute | solution.py:473
  131.4 18.7 %collective-permute-start.23 = (bf16[384,384]{1,0:T(8,128)(2,1)}, bf16[384,384]{1,0:T(8,128)(2,1)S(1)}, u32[]{:S(2)}, u32[]{:S(2)}) collective-permute-start(bf16[384,384]{1,0:T(8,128)(2,1)} %get-tuple-element.31), channel_id=1, source_target_pairs={{0,8},{8,16},{16,24},{24,0},{1,9},{9,17},{17,25},{25,1},{2,10},{10... | collective-permute-start | bytes 884744 | tf_op jit(solution)/shard_map/ppermute | solution.py:425
  132.2 36.3 %collective-permute-start.25 = (bf16[384,384]{1,0:T(8,128)(2,1)}, bf16[384,384]{1,0:T(8,128)(2,1)S(1)}, u32[]{:S(2)}, u32[]{:S(2)}) collective-permute-start(bf16[384,384]{1,0:T(8,128)(2,1)} %get-tuple-element.32), channel_id=1, source_target_pairs={{0,16},{8,24},{16,0},{24,8},{1,17},{9,25},{17,1},{25,9},{2,18},{10... | collective-permute-start | bytes 884744 | tf_op jit(solution)/shard_map/ppermute | solution.py:425
  133.8 38.4 %collective-permute-start.27 = (bf16[384,384]{1,0:T(8,128)(2,1)}, bf16[384,384]{1,0:T(8,128)(2,1)S(1)}, u32[]{:S(2)}, u32[]{:S(2)}) collective-permute-start(bf16[384,384]{1,0:T(8,128)(2,1)} %get-tuple-element.33), channel_id=1, source_target_pairs={{0,24},{8,0},{16,8},{24,16},{1,25},{9,1},{17,9},{25,17},{2,26},{10... | collective-permute-start | bytes 884744 | tf_op jit(solution)/shard_map/ppermute | solution.py:425
  140.7 31.7 %collective-permute-start.31 = (bf16[384,384]{1,0:T(8,128)(2,1)S(1)}, bf16[384,384]{1,0:T(8,128)(2,1)S(1)}, u32[]{:S(2)}, u32[]{:S(2)}) collective-permute-start(bf16[384,384]{1,0:T(8,128)(2,1)S(1)} %copy-done.20), channel_id=1, source_target_pairs={{0,1},{1,0},{2,3},{3,2},{4,5},{5,4},{6,7},{7,6},{8,9},{9,8},{10,11... | collective-permute-start | bytes 884744 | tf_op jit(solution)/shard_map/ppermute | solution.py:473
  140.8 32.1 %collective-permute-start.32 = (bf16[384,384]{1,0:T(8,128)(2,1)S(1)}, bf16[384,384]{1,0:T(8,128)(2,1)S(1)}, u32[]{:S(2)}, u32[]{:S(2)}) collective-permute-start(bf16[384,384]{1,0:T(8,128)(2,1)S(1)} %copy-done.36), channel_id=1, source_target_pairs={{0,8},{8,16},{16,24},{24,0},{1,9},{9,17},{17,25},{25,1},{2,10},{10... | collective-permute-start | bytes 884744 | tf_op jit(solution)/shard_map/ppermute | solution.py:425
  150.1 31.1 %collective-permute-start.34 = (bf16[384,384]{1,0:T(8,128)(2,1)S(1)}, bf16[384,384]{1,0:T(8,128)(2,1)S(1)}, u32[]{:S(2)}, u32[]{:S(2)}) collective-permute-start(bf16[384,384]{1,0:T(8,128)(2,1)S(1)} %copy-done.33), channel_id=1, source_target_pairs={{0,16},{8,24},{16,0},{24,8},{1,17},{9,25},{17,1},{25,9},{2,18},{10... | collective-permute-start | bytes 884744 | tf_op jit(solution)/shard_map/ppermute | solution.py:425
  168.6 14.5 %collective-permute-start.36 = (bf16[384,384]{1,0:T(8,128)(2,1)S(1)}, bf16[384,384]{1,0:T(8,128)(2,1)S(1)}, u32[]{:S(2)}, u32[]{:S(2)}) collective-permute-start(bf16[384,384]{1,0:T(8,128)(2,1)S(1)} %copy-done.31), channel_id=1, source_target_pairs={{0,24},{8,0},{16,8},{24,16},{1,25},{9,1},{17,9},{25,17},{2,26},{10... | collective-permute-start | bytes 884744 | tf_op jit(solution)/shard_map/ppermute | solution.py:425
  172.2 10.8 %collective-permute-start.6 = (bf16[384,384]{1,0:T(8,128)(2,1)S(1)}, bf16[384,384]{1,0:T(8,128)(2,1)S(1)}, u32[]{:S(2)}, u32[]{:S(2)}) collective-permute-start(bf16[384,384]{1,0:T(8,128)(2,1)S(1)} %collective-permute-done.5.rest_6_), channel_id=1, source_target_pairs={{0,1},{1,0},{2,3},{3,2},{4,5},{5,4},{6,7},{7,6},{8,9},{9,8},{10,11... | collective-permute-start | bytes 884744 | tf_op jit(solution)/shard_map/ppermute | solution.py:473
  172.4 11.2 %collective-permute-start.8 = (bf16[384,384]{1,0:T(8,128)(2,1)S(1)}, bf16[384,384]{1,0:T(8,128)(2,1)S(1)}, u32[]{:S(2)}, u32[]{:S(2)}) collective-permute-start(bf16[384,384]{1,0:T(8,128)(2,1)S(1)} %collective-permute-done.7.rest_8_), channel_id=1, source_target_pairs={{0,1},{1,0},{2,3},{3,2},{4,5},{5,4},{6,7},{7,6},{8,9},{9,8},{10,11... | collective-permute-start | bytes 884744 | tf_op jit(solution)/shard_map/ppermute | solution.py:473
  172.9 10.8 %collective-permute-start.10 = (bf16[384,384]{1,0:T(8,128)(2,1)S(1)}, bf16[384,384]{1,0:T(8,128)(2,1)S(1)}, u32[]{:S(2)}, u32[]{:S(2)}) collective-permute-start(bf16[384,384]{1,0:T(8,128)(2,1)S(1)} %collective-permute-done.9.rest_10_), channel_id=1, source_target_pairs={{0,1},{1,0},{2,3},{3,2},{4,5},{5,4},{6,7},{7,6},{8,9},{9,8},{10,11... | collective-permute-start | bytes 884744 | tf_op jit(solution)/shard_map/ppermute | solution.py:473
  181.2 2.9 collective-permute-start.15
  183.0 1.6 collective-permute-start.17
  183.1 2.0 collective-permute-start.19
  183.6 1.9 collective-permute-start.24
  183.7 2.6 collective-permute-start.26
  184.1 2.2 collective-permute-start.28
  184.6 2.1 collective-permute-start.33
  185.1 2.1 collective-permute-start.35
  185.5 2.1 collective-permute-start.37
  279.4 18.2 %collective-permute-start.40 = (bf16[12,128,128]{2,1,0:T(8,128)(2,1)S(1)}, bf16[12,128,128]{2,1,0:T(8,128)(2,1)S(1)}, u32[]{:S(2)}, u32[]{:S(2)}) collective-permute-start(bf16[12,128,128]{2,1,0:T(8,128)(2,1)S(1)} %get-tuple-element.45), channel_id=1, source_target_pairs={{0,24},{8,0},{16,8},{24,16},{1,25},{9,1},{17,9},{25,17},{2,26},{10... | collective-permute-start | bytes 1179656 | tf_op jit(solution)/shard_map/ppermute | solution.py:425
  288.0 33.0 %collective-permute-start.39 = (bf16[12,128,128]{2,1,0:T(8,128)(2,1)S(1)}, bf16[12,128,128]{2,1,0:T(8,128)(2,1)S(1)}, u32[]{:S(2)}, u32[]{:S(2)}) collective-permute-start(bf16[12,128,128]{2,1,0:T(8,128)(2,1)S(1)} %get-tuple-element.46), channel_id=1, source_target_pairs={{0,16},{8,24},{16,0},{24,8},{1,17},{9,25},{17,1},{25,9},{2,18},{10... | collective-permute-start | bytes 1179656 | tf_op jit(solution)/shard_map/ppermute | solution.py:425
  288.0 33.0 %collective-permute-start.38 = (bf16[12,128,128]{2,1,0:T(8,128)(2,1)S(1)}, bf16[12,128,128]{2,1,0:T(8,128)(2,1)S(1)}, u32[]{:S(2)}, u32[]{:S(2)}) collective-permute-start(bf16[12,128,128]{2,1,0:T(8,128)(2,1)S(1)} %get-tuple-element.47), channel_id=1, source_target_pairs={{0,8},{8,16},{16,24},{24,0},{1,9},{9,17},{17,25},{25,1},{2,10},{10... | collective-permute-start | bytes 1179656 | tf_op jit(solution)/shard_map/ppermute | solution.py:425
  322.3 13.0 %collective-permute-start.43 = (bf16[4,3,128,128]{3,2,1,0:T(8,128)(2,1)S(1)}, bf16[4,3,128,128]{3,2,1,0:T(8,128)(2,1)S(1)}, u32[]{:S(2)}, u32[]{:S(2)}) collective-permute-start(bf16[4,3,128,128]{3,2,1,0:T(8,128)(2,1)S(1)} %get-tuple-element.41), channel_id=1, source_target_pairs={{0,6},{1,7},{2,4},{3,5},{4,2},{5,3},{6,0},{7,1},{8,14},{9,15},{10,... | collective-permute-start | bytes 1179656 | tf_op jit(solution)/shard_map/ppermute | solution.py:482
  324.8 17.2 %collective-permute-start.42 = (bf16[4,3,128,128]{3,2,1,0:T(8,128)(2,1)S(1)}, bf16[4,3,128,128]{3,2,1,0:T(8,128)(2,1)S(1)}, u32[]{:S(2)}, u32[]{:S(2)}) collective-permute-start(bf16[4,3,128,128]{3,2,1,0:T(8,128)(2,1)S(1)} %get-tuple-element.42), channel_id=1, source_target_pairs={{0,4},{1,5},{2,6},{3,7},{4,0},{5,1},{6,2},{7,3},{8,12},{9,13},{10,... | collective-permute-start | bytes 1179656 | tf_op jit(solution)/shard_map/ppermute | solution.py:482
  325.3 16.8 %collective-permute-start.41 = (bf16[4,3,128,128]{3,2,1,0:T(8,128)(2,1)S(1)}, bf16[4,3,128,128]{3,2,1,0:T(8,128)(2,1)S(1)}, u32[]{:S(2)}, u32[]{:S(2)}) collective-permute-start(bf16[4,3,128,128]{3,2,1,0:T(8,128)(2,1)S(1)} %get-tuple-element.43), channel_id=1, source_target_pairs={{0,2},{1,3},{2,0},{3,1},{4,6},{5,7},{6,4},{7,5},{8,10},{9,11},{10,... | collective-permute-start | bytes 1179656 | tf_op jit(solution)/shard_map/ppermute | solution.py:482
  342.1 2.0 collective-permute-start.44
  (47 other events, 752.5 us)
Sparse Core Ops, SparseCore 0:
  49.8 66.3 all-gather.1

commit v2 on v1

--- a/solution.py
+++ b/solution.py
@@ -12,6 +12,7 @@
 HD = 128
 BLK = 512
 TILE = 128
+STEP = 12
 
 
 EPS = 1e-05
@@ -128,14 +129,14 @@
 def project_kernel(place, first, second, own, other, cosine, sine, *rest):
     outs, (rows, weights, results, row_sems, weight_sems, out_sems) = rest[:4], rest[4:]
     half = first.shape[0]
-    width = own.shape[1] // 3
+    count = rows.shape[0]
     row_copies = [
         pltpu.make_async_copy(ref, rows.at[pl.ds(i * half, half)], row_sems.at[i])
         for i, ref in enumerate((first, second))
     ]
     weight_copies = [
         pltpu.make_async_copy(
-            ref.at[:, pl.ds(part * width, width)],
+            ref.at[part],
             weights.at[w * 3 + part],
             weight_sems.at[w * 3 + part],
         )
@@ -150,16 +151,20 @@
     for w in range(2):
         for part in range(3):
             weight_copies[w * 3 + part].wait()
-            product = jnp.dot(
-                rows[...], weights[w * 3 + part], preferred_element_type=jnp.float32
-            )
-            for h in range(2):
-                vector = product[:, h * HD : (h + 1) * HD]
-                if part < 2:
-                    vector = vector * cosine[...] + pltpu.roll(vector, HD // 2, 1) * sine[...]
-                if part == 0:
-                    vector = vector * query_scale
-                results[w * 2 + h, :, part * HD : (part + 1) * HD] = vector.astype(jnp.bfloat16)
+            for at in range(0, count, half):
+                piece = slice(at, at + half)
+                product = jnp.dot(
+                    rows[piece], weights[w * 3 + part], preferred_element_type=jnp.float32
+                )
+                for h in range(2):
+                    vector = product[:, h * HD : (h + 1) * HD]
+                    if part < 2:
+                        turned = pltpu.roll(vector, HD // 2, 1)
+                        vector = vector * cosine[piece] + turned * sine[piece]
+                    if part == 0:
+                        vector = vector * query_scale
+                    column = slice(part * HD, (part + 1) * HD)
+                    results[w * 2 + h, piece, column] = vector.astype(jnp.bfloat16)
     copies = [
         pltpu.make_async_copy(results.at[place[shift]], outs[shift], out_sems.at[shift])
         for shift in range(4)
@@ -173,7 +178,7 @@
 def project(place, first, second, own, other, cosine, sine):
     half = first.shape[0]
     count = 2 * half
-    width = own.shape[1] // 3
+    width = own.shape[2]
     any_space = pl.BlockSpec(memory_space=pl.ANY)
     vmem = pl.BlockSpec(memory_space=pltpu.VMEM)
     return pl.pallas_call(
@@ -199,11 +204,13 @@
 
 def attend_kernel(blocks_here, place, *rest):
     lists, pieces, out = rest[:4], rest[4:36], rest[36]
-    rows, values_t, sems = rest[37:]
+    rows, values_t, queries, tops, sums, item_q, item_k, sems = rest[37:]
     section, chip, core = place[0], place[1], place[2]
     half = pieces[0].shape[0] // 2
     tok = blocks_here * BLK
     total_blocks = 4 * blocks_here
+    slots = lists[0].shape[1]
+    wide = 2 * TILE
     copies = []
     for chunk in range(4):
         for shift in range(4):
@@ -229,98 +236,174 @@
                     )
     for copy in copies:
         copy.start()
+
+    count = jnp.int32(0)
+    for shift in range(4):
+        block_list = lists[(4 - shift) % 4]
+        first_block = lax.rem(section + shift, 4) * blocks_here
+
+        def note(local, count, block_list=block_list, first_block=first_block):
+            for slot in range(1, slots):
+                source = block_list[local, slot]
+                item_q[count] = first_block + local
+                item_k[count] = source
+                count = count + (source >= 0).astype(jnp.int32)
+            return count
+
+        count = lax.fori_loop(0, blocks_here, note, count)
+    for extra in range(STEP):
+        item_q[count + extra] = total_blocks
+        item_k[count + extra] = 0
+
+    values_t[HD:, :] = jnp.ones((values_t.shape[0] - HD, values_t.shape[1]), jnp.bfloat16)
+    queries[total_blocks] = jnp.zeros((wide, HD), jnp.bfloat16)
+    tops[total_blocks] = jnp.zeros((8, wide), jnp.float32)
+    sums[total_blocks] = jnp.zeros(sums.shape[1:], jnp.float32)
     for copy in copies:
         copy.wait()
 
-    def turn(i, carry):
-        at = pl.multiple_of(i * BLK, BLK)
-        values_t[:, pl.ds(at, BLK)] = rows[pl.ds(at, BLK), 2 * HD : 3 * HD].T
-        return carry
-
-    lax.fori_loop(0, total_blocks, turn, 0)
-
-    lane = lax.broadcasted_iota(jnp.int32, (BLK, 2 * TILE), 1)
-    key_at = lax.broadcasted_iota(jnp.int32, (BLK, 2 * TILE), 0)
-
-    for shift in range(4):
-        target = lax.rem(section + shift, 4)
-        block_list = lists[(4 - shift) % 4]
-
-        def one_block(local, carry, shift=shift, target=target, block_list=block_list):
-            block = target * blocks_here + local
-            middle = lax.rem(local, 3) == 1
-            offset = jnp.where(middle, core * TILE, core * 2 * TILE)
-            gap = jnp.where(middle, TILE, 0)
+    lane = lax.broadcasted_iota(jnp.int32, (BLK, wide), 1)
+    key_at = lax.broadcasted_iota(jnp.int32, (BLK, wide), 0)
+
+    def query_place(local):
+        middle = lax.rem(local, 3) == 1
+        offset = jnp.where(middle, core * TILE, core * wide)
+        return offset, jnp.where(middle, TILE, 0)
+
+    def scores_of(source, query):
+        at = pl.multiple_of(source * BLK, BLK)
+        return lax.dot_general(
+            rows[pl.ds(at, BLK), HD : 2 * HD],
+            query,
+            (((1,), (1,)), ((), ())),
+            preferred_element_type=jnp.float32,
+        )
+
+    def weigh(source, weights):
+        at = pl.multiple_of(source * BLK, BLK)
+        return jnp.dot(
+            values_t[:, pl.ds(at, BLK)],
+            weights.astype(jnp.bfloat16),
+            preferred_element_type=jnp.float32,
+        )
+
+    def masked(local, scores):
+        offset, gap = query_place(local)
+        query_at = offset + lane + jnp.where(lane >= TILE, gap, 0)
+        return jnp.where(key_at <= query_at, scores, -jnp.inf)
+
+    def diagonal(step, carry):
+        blocks = [step * 4 + i for i in range(4)]
+        scores = []
+        for block in blocks:
+            local = lax.rem(block, blocks_here)
+            at = pl.multiple_of(block * BLK, BLK)
+            values_t[:HD, pl.ds(at, BLK)] = rows[pl.ds(at, BLK), 2 * HD : 3 * HD].T
+            offset, gap = query_place(local)
             start = pl.multiple_of(block * BLK + offset, TILE)
             later = pl.multiple_of(start + TILE + gap, TILE)
             query = jnp.concatenate(
                 [rows[pl.ds(start, TILE), 0:HD], rows[pl.ds(later, TILE), 0:HD]], axis=0
             )
-            live = jnp.int32(0)
-            for slot in range(block_list.shape[1]):
-                live = live + (block_list[local, slot] >= 0).astype(jnp.int32)
-
-            def scores_of(source):
-                at = pl.multiple_of(source * BLK, BLK)
-                return lax.dot_general(
-                    rows[pl.ds(at, BLK), HD : 2 * HD],
-                    query,
-                    (((1,), (1,)), ((), ())),
-                    preferred_element_type=jnp.float32,
-                )
-
-            def weigh(source, weights):
-                at = pl.multiple_of(source * BLK, BLK)
-                return jnp.dot(
-                    values_t[:, pl.ds(at, BLK)],
-                    weights.astype(jnp.bfloat16),
-                    preferred_element_type=jnp.float32,
-                )
-
-            query_at = offset + lane + jnp.where(lane >= TILE, gap, 0)
-            scores = jnp.where(key_at <= query_at, scores_of(block), -jnp.inf)
-            highest = jnp.max(scores, axis=0, keepdims=True)
-            weights = jnp.exp2(scores - highest)
-            total = jnp.sum(weights, axis=0, keepdims=True)
-            weighted = weigh(block, weights)
-
-            def one_slot(slot, state):
-                highest, total, weighted = state
-                source = block_list[local, slot]
-                scores = scores_of(source)
-                new_highest = jnp.maximum(highest, jnp.max(scores, axis=0, keepdims=True))
-                factor = jnp.exp2(highest - new_highest)
-                weights = jnp.exp2(scores - new_highest)
-                total = total * factor + jnp.sum(weights, axis=0, keepdims=True)
-                weighted = weighted * factor + weigh(source, weights)
-                return (new_highest, total, weighted)
-
-            _, total, weighted = lax.fori_loop(1, live, one_slot, (highest, total, weighted))
-            result = (weighted / total).T.astype(jnp.bfloat16)
-            for part in range(2):
-                tile = 2 * local + part
-                owner = tile // 3
-                where = (owner ^ chip) * 3 + lax.rem(tile, 3)
-                out[shift, where] = result[part * TILE : (part + 1) * TILE]
-            return carry
-
-        lax.fori_loop(0, blocks_here, one_block, 0)
+            queries[block] = query
+            scores.append(scores_of(block, query))
+        for block, score in zip(blocks, scores):
+            score = masked(lax.rem(block, blocks_here), score)
+            top = jnp.max(score, axis=0, keepdims=True)
+            tops[block] = jnp.broadcast_to(top, (8, wide))
+            sums[block] = weigh(block, jnp.exp2(score - top))
+        return carry
+
+    lax.fori_loop(0, total_blocks // 4, diagonal, 0)
+
+    def below(step, carry):
+        items = [step * STEP + i for i in range(STEP)]
+        scores = scores_of(item_k[items[0]], queries[item_q[items[0]]])
+        held = None
+        for i, item in enumerate(items):
+            if i + 1 < STEP:
+                ahead = scores_of(item_k[items[i + 1]], queries[item_q[items[i + 1]]])
+            weights = jnp.exp2(scores - tops[item_q[item], 0:1]).astype(jnp.bfloat16)
+            if held is not None:
+                sums[item_q[items[i - 1]]] += weigh(item_k[items[i - 1]], held)
+            held, scores = weights, ahead
+        sums[item_q[items[-1]]] += weigh(item_k[items[-1]], held)
+        return carry
+
+    lax.fori_loop(0, (count + STEP - 1) // STEP, below, 0)
+
+    def store(block, result):
+        local = lax.rem(block, blocks_here)
+        shift = lax.rem(block // blocks_here - section + 4, 4)
+        for part in range(2):
+            tile = 2 * local + part
+            where = ((tile // 3) ^ chip) * 3 + lax.rem(tile, 3)
+            out[shift, where] = result[part * TILE : (part + 1) * TILE]
+
+    def leave(step, over):
+        for i in range(4):
+            block = step * 4 + i
+            total = sums[block, HD : HD + 1]
+            over = jnp.maximum(over, jnp.where(total < 2.0**100, 0.0, 1.0))
+            store(block, (sums[block, 0:HD] / total).T.astype(jnp.bfloat16))
+        return over
+
+    over = lax.fori_loop(0, total_blocks // 4, leave, jnp.zeros((1, wide), jnp.float32))
+
+    @pl.when(jnp.max(over) > 0)
+    def _():
+        for shift in range(4):
+            block_list = lists[(4 - shift) % 4]
+            first_block = lax.rem(section + shift, 4) * blocks_here
+
+            def one_block(local, carry, block_list=block_list, first_block=first_block):
+                block = first_block + local
+                query = queries[block]
+                live = jnp.int32(0)
+                for slot in range(slots):
+                    live = live + (block_list[local, slot] >= 0).astype(jnp.int32)
+                scores = masked(local, scores_of(block, query))
+                highest = jnp.max(scores, axis=0, keepdims=True)
+                weighted = weigh(block, jnp.exp2(scores - highest))
+
+                def one_slot(slot, state):
+                    highest, weighted = state
+                    source = block_list[local, slot]
+                    scores = scores_of(source, query)
+                    new_highest = jnp.maximum(highest, jnp.max(scores, axis=0, keepdims=True))
+                    weights = jnp.exp2(scores - new_highest)
+                    weighted = weighted * jnp.exp2(highest - new_highest) + weigh(source, weights)
+                    return (new_highest, weighted)
+
+                _, weighted = lax.fori_loop(1, live, one_slot, (highest, weighted))
+                result = weighted[0:HD] / weighted[HD : HD + 1]
+                store(block, result.T.astype(jnp.bfloat16))
+                return carry
+
+            lax.fori_loop(0, blocks_here, one_block, 0)
 
 
 def attend(place, lists, pieces):
-    blocks_here = lists[0].shape[0]
-    tokens = 4 * blocks_here * BLK
+    blocks_here, slots = lists[0].shape
+    total_blocks = 4 * blocks_here
+    tokens = total_blocks * BLK
     tiles = blocks_here * 2
-    smem = pl.BlockSpec(memory_space=pltpu.SMEM)
-    pairs = tokens // BLK * lists[0].shape[1] // 2
+    room = total_blocks * slots + STEP
+    pairs = total_blocks * slots // 2
     return pl.pallas_call(
         functools.partial(attend_kernel, blocks_here),
         out_shape=jax.ShapeDtypeStruct((4, tiles, TILE, HD), jnp.bfloat16),
-        in_specs=[smem] * 5 + [pl.BlockSpec(memory_space=pl.ANY)] * 32,
+        in_specs=[pl.BlockSpec(memory_space=pltpu.SMEM)] * 5
+        + [pl.BlockSpec(memory_space=pl.ANY)] * 32,
         out_specs=pl.BlockSpec(memory_space=pltpu.VMEM),
         scratch_shapes=[
             pltpu.VMEM((tokens, 3 * HD), jnp.bfloat16),
-            pltpu.VMEM((HD, tokens), jnp.bfloat16),
+            pltpu.VMEM((HD + 16, tokens), jnp.bfloat16),
+            pltpu.VMEM((total_blocks + 1, 2 * TILE, HD), jnp.bfloat16),
+            pltpu.VMEM((total_blocks + 1, 8, 2 * TILE), jnp.float32),
+            pltpu.VMEM((total_blocks + 1, HD + 16, 2 * TILE), jnp.float32),
+            pltpu.SMEM((room,), jnp.int32),
+            pltpu.SMEM((room,), jnp.int32),
             pltpu.SemaphoreType.DMA((64,)),
         ],
         compiler_params=pltpu.CompilerParams(vmem_limit_bytes=VMEM_LIMIT),
@@ -410,7 +493,6 @@
     section = lax.axis_index("section")
     device = lax.axis_index("head")
     chip, core = device // 2, device % 2
-    width = w_qkv.shape[2]
     blocks_here = block_lists.shape[0]
     tok = blocks_here * BLK
     rows = hidden_in.shape[0]
@@ -428,8 +510,9 @@
     shifts = jnp.arange(4, dtype=jnp.int32)
     chosen = (section + shifts - 2 * core + 4) % 4
 
-    own = w_qkv.reshape(D, 3 * width)
+    own = jnp.transpose(w_qkv, (1, 0, 2))
     other = lax.ppermute(own, "head", other_core)
+    hidden_in, own = lax.optimization_barrier((hidden_in, own))
     lists = [block_lists] + [to_section(block_lists, shift) for shift in range(1, 4)]
 
     resid = hidden_in.astype(jnp.float32)
@@ -441,9 +524,6 @@
     y_low = lax.ppermute(low, "head", along_y)
     x_high = lax.ppermute(high, "head", along_x)
     y_high = lax.ppermute(high, "head", along_y)
-    d_low = lax.ppermute(y_low, "head", along_x)
-    d_high = lax.ppermute(x_high, "head", along_y)
-    chunks = [(low, high), (x_low, y_low), (x_high, y_high), (d_low, d_high)]
     origins = [
         ((0, 0), (0, 1)),
         ((1, 0), (2, 0)),
@@ -466,11 +546,23 @@
     sine = jnp.concatenate([-sine, sine], axis=-1)
 
     pieces = []
-    for number, (first, second) in enumerate(chunks):
+
+    def send(number, first, second):
         outs = project(chosen, first, second, own, other, cosine[number], sine[number])
         for shift in range(4):
             arrived = outs[shift] if shift == 0 else to_section(outs[shift], shift)
-            pieces += [arrived, lax.ppermute(arrived, "head", other_core)]
+            pieces.extend([arrived, lax.ppermute(arrived, "head", other_core)])
+        return outs[0]
+
+    mark = send(0, low, high)
+    x_high, y_high, x_low, y_low, mark = lax.optimization_barrier(
+        (x_high, y_high, x_low, y_low, mark)
+    )
+    d_low = lax.ppermute(y_low, "head", along_x)
+    d_high = lax.ppermute(x_high, "head", along_y)
+    send(1, x_low, y_low)
+    send(2, x_high, y_high)
+    send(3, d_low, d_high)
 
     late_w_out, _, _ = lax.optimization_barrier((w_out, d_low, d_high))
     w_out_all = lax.all_gather(late_w_out, "head", axis=0, tiled=True)

time: 363 us -> 316 us (0.87)
  Pallas kernels: 145 us -> 79.3 us
  waiting for transfers between devices: 113 us -> 147 us
  starting transfers between devices: 70.4 us -> 62 us
  local copies, waits for them, and re-layouts: 12 us -> 5.03 us
    pallas_call x1, Pallas kernels: 89.3 us -> 31.6 us  [attend(): pl.pallas_call(functools.partial(attend_kernel, blocks_here), out_shape=j...]
    ppermute x18, waiting for transfers between devices: 52.3 us -> 90.6 us  [to_section(): lax.ppermute(array, 'section', [(i, (i + shift) % 4) for i in range(4)])]
    ppermute x1, waiting for transfers between devices: 16 us -> 1.46 us  [by_head(): y_low = lax.ppermute(low, 'head', along_y)]
    pallas_call x4, Pallas kernels: 45.2 us -> 36.6 us  [project(): pl.pallas_call(project_kernel, out_shape=[jax.ShapeDtypeStruct((count, 3...]
    ppermute x1, waiting for transfers between devices: 7.99 us -> 14.6 us  [by_head(): x_low = lax.ppermute(low, 'head', along_x)]
    ppermute x18, starting transfers between devices: 54.1 us -> 48 us  [to_section(): lax.ppermute(array, 'section', [(i, (i + shift) % 4) for i in range(4)])]
    unnamed x99 -> x90, local copies, waits for them, and re-layouts: 5.82 us -> 1.81 us
  transfers between devices with their start and end apart: 46 -> 46, of which waited for: 19 -> 20; matrix products, arithmetic and copies ran while one was open for 4% -> 4% of each run, Pallas kernels for 37% -> 22%
where the time goes in v2:
time: 316 us; the launch traced here: 315 us
  waiting for transfers between devices  147 us (47%)
  Pallas kernels  79.3 us (25%)
  starting transfers between devices  62 us (20%)
  between operations  14.1 us (4%)
  other arithmetic  8.13 us (3%)
  local copies, waits for them, and re-layouts  5.03 us (2%)
    ppermute x18, waiting for transfers between devices, to_section(): lax.ppermute(array, 'section', [(i, (i + shift) % 4) for i in range(4)])  90.6 us
    ppermute x18, starting transfers between devices, to_section(): lax.ppermute(array, 'section', [(i, (i + shift) % 4) for i in range(4)])  48 us
    pallas_call x4, Pallas kernels, project(): pl.pallas_call(project_kernel, out_shape=[jax.ShapeDtypeStruct((count, 3...  36.6 us
    pallas_call x1, Pallas kernels, attend(): pl.pallas_call(functools.partial(attend_kernel, blocks_here), out_shape=j...  31.6 us
    ppermute x1, waiting for transfers between devices, by_head(): d_low = lax.ppermute(y_low, 'head', along_x)  16.8 us
    ppermute x3, waiting for transfers between devices, by_head(): lax.ppermute(back[:, relative], 'head', perm)  16.6 us
    ppermute x1, waiting for transfers between devices, by_head(): x_low = lax.ppermute(low, 'head', along_x)  14.6 us
    pallas_call x1, Pallas kernels, finish(): pl.pallas_call(finish_kernel, out_shape=jax.ShapeDtypeStruct((count, D),...  11 us
  transfers between devices with their start and end apart: 46, of which 20 were waited for; matrix products, arithmetic and copies ran while one was open for 4% of the time, Pallas kernels for 22%

profile of v2, /device:TPU:0, one launch (start us, length us, event | category | flops | bytes accessed | tf_op | source)
XLA Modules:
  0.0 315.3 jit_solution(10667031686182628644)
XLA Ops:
  7.0 1.8 fusion
  9.4 2.7 collective-permute-start.11
  12.1 1.5 collective-permute-start.12
  15.2 2.8 multiply_sine_fusion
  18.0 1.6 fusion.16
  19.6 9.1 %project_and_rotate.4 = (bf16[384,384]{1,0:T(8,128)(2,1)}, bf16[384,384]{1,0:T(8,128)(2,1)}, bf16[384,384]{1,0:T(8,128)(2,1)}, bf16[384,384]{1,0:T(8,128)(2,1)}) custom-call(s32[4]{0:T(128)} %and_select_fusion.place, bf16[192,2048]{1,0:T(8,128)(2,1)} %copy-done.1, bf16[192,2048]{1,0:T(8,128)(2,1)} %copy-done.2, bf16[3,2048,256]{2,1,0:T(8,128)(2,1)} %bitcast.59, ...), custom_call_target="tpu_custom_call" | custom-call | flops 2415919104 | bytes 6291456 | tf_op jit(solution)/shard_map/project_and_rotate/pallas_call | solution.py:184
  28.8 1.7 collective-permute-done.11.first
  30.4 2.0 collective-permute-done.12.second
  32.5 14.6 %collective-permute-done.13.first = bf16[192,2048]{1,0:T(8,128)(2,1)} collective-permute-done((bf16[192,2048]{1,0:T(8,128)(2,1)S(1)}, bf16[192,2048]{1,0:T(8,128)(2,1)}, u32[]{:S(2)}, u32[]{:S(2)}) %collective-permute-start.13) | collective-permute-done | bytes 786464 | tf_op jit(solution)/shard_map/ppermute | solution.py:523
  47.1 1.5 collective-permute-done.14.second
  48.9 1.7 collective-permute-start.30
  50.6 16.8 %collective-permute-done.29.first = bf16[192,2048]{1,0:T(8,128)(2,1)S(1)} collective-permute-done((bf16[192,2048]{1,0:T(8,128)(2,1)}, bf16[192,2048]{1,0:T(8,128)(2,1)S(1)}, u32[]{:S(2)}, u32[]{:S(2)}) %collective-permute-start.29) | collective-permute-done | bytes 786464 | tf_op jit(solution)/shard_map/ppermute | solution.py:561
  67.8 1.6 collective-permute-start.5
  69.3 2.6 collective-permute-start.7
  72.2 1.6 collective-permute-start.1
  73.8 11.9 %collective-permute-done.rest_1_ = s32[6,12]{1,0:T(8,128)S(1)} collective-permute-done((s32[6,12]{1,0:T(8,128)S(1)}, s32[6,12]{1,0:T(8,128)S(1)}, u32[]{:S(2)}, u32[]{:S(2)}) %collective-permute-start) | collective-permute-done | bytes 320 | tf_op jit(solution)/shard_map/ppermute | solution.py:507
  85.7 9.2 %project_and_rotate.5 = (bf16[384,384]{1,0:T(8,128)(2,1)}, bf16[384,384]{1,0:T(8,128)(2,1)}, bf16[384,384]{1,0:T(8,128)(2,1)}, bf16[384,384]{1,0:T(8,128)(2,1)}) custom-call(s32[4]{0:T(128)} %and_select_fusion.place, bf16[192,2048]{1,0:T(8,128)(2,1)} %collective-permute-done.13.first, bf16[192,2048]{1,0:T(8,128)(2,1)} %collective-permute-done.14.second, ...), custom_call_target="tpu_custom_call" | custom-call | flops 2415919104 | bytes 6291456 | tf_op jit(solution)/shard_map/project_and_rotate/pallas_call | solution.py:184
  95.0 8.6 %collective-permute-start.9 = (bf16[384,384]{1,0:T(8,128)(2,1)S(1)}, bf16[384,384]{1,0:T(8,128)(2,1)S(1)}, u32[]{:S(2)}, u32[]{:S(2)}) collective-permute-start(bf16[384,384]{1,0:T(8,128)(2,1)S(1)} %copy-done.30), channel_id=1, source_target_pairs={{0,24},{8,0},{16,8},{24,16},{1,25},{9,1},{17,9},{25,17},{2,26},{10... | collective-permute-start | bytes 884744 | tf_op jit(solution)/shard_map/ppermute | solution.py:507
  103.7 0.6 collective-permute-start.18
  104.4 3.4 %collective-permute-start.20 = (bf16[384,384]{1,0:T(8,128)(2,1)}, bf16[384,384]{1,0:T(8,128)(2,1)S(1)}, u32[]{:S(2)}, u32[]{:S(2)}) collective-permute-start(bf16[384,384]{1,0:T(8,128)(2,1)} %get-tuple-element.39), channel_id=1, source_target_pairs={{0,24},{8,0},{16,8},{24,16},{1,25},{9,1},{17,9},{25,17},{2,26},{10... | collective-permute-start | bytes 884744 | tf_op jit(solution)/shard_map/ppermute | solution.py:507
  107.8 9.2 %project_and_rotate.6 = (bf16[384,384]{1,0:T(8,128)(2,1)}, bf16[384,384]{1,0:T(8,128)(2,1)}, bf16[384,384]{1,0:T(8,128)(2,1)}, bf16[384,384]{1,0:T(8,128)(2,1)}) custom-call(s32[4]{0:T(128)} %and_select_fusion.place, bf16[192,2048]{1,0:T(8,128)(2,1)} %copy-done.8, bf16[192,2048]{1,0:T(8,128)(2,1)} %copy-done.9, bf16[3,2048,256]{2,1,0:T(8,128)(2,1)} %bitcast.61, ...), custom_call_target="tpu_custom_call" | custom-call | flops 2415919104 | bytes 6291456 | tf_op jit(solution)/shard_map/project_and_rotate/pallas_call | solution.py:184
  117.9 1.7 collective-permute-start.25
  119.7 10.3 %collective-permute-done.18.rest_16_ = bf16[384,384]{1,0:T(8,128)(2,1)S(1)} collective-permute-done((bf16[384,384]{1,0:T(8,128)(2,1)}, bf16[384,384]{1,0:T(8,128)(2,1)S(1)}, u32[]{:S(2)}, u32[]{:S(2)}) %collective-permute-start.18) | collective-permute-done | bytes 294944 | tf_op jit(solution)/shard_map/ppermute | solution.py:507
  130.0 9.5 %collective-permute-start.27 = (bf16[384,384]{1,0:T(8,128)(2,1)}, bf16[384,384]{1,0:T(8,128)(2,1)S(1)}, u32[]{:S(2)}, u32[]{:S(2)}) collective-permute-start(bf16[384,384]{1,0:T(8,128)(2,1)} %get-tuple-element.45), channel_id=1, source_target_pairs={{0,24},{8,0},{16,8},{24,16},{1,25},{9,1},{17,9},{25,17},{2,26},{10... | collective-permute-start | bytes 884744 | tf_op jit(solution)/shard_map/ppermute | solution.py:507
  139.6 0.5 collective-permute-start.8
  140.3 14.0 %collective-permute-done.25.rest_24_ = bf16[384,384]{1,0:T(8,128)(2,1)S(1)} collective-permute-done((bf16[384,384]{1,0:T(8,128)(2,1)}, bf16[384,384]{1,0:T(8,128)(2,1)S(1)}, u32[]{:S(2)}, u32[]{:S(2)}) %collective-permute-start.25) | collective-permute-done | bytes 294944 | tf_op jit(solution)/shard_map/ppermute | solution.py:507
  154.8 9.1 %project_and_rotate.7 = (bf16[384,384]{1,0:T(8,128)(2,1)}, bf16[384,384]{1,0:T(8,128)(2,1)}, bf16[384,384]{1,0:T(8,128)(2,1)}, bf16[384,384]{1,0:T(8,128)(2,1)}) custom-call(s32[4]{0:T(128)} %and_select_fusion.place, bf16[192,2048]{1,0:T(8,128)(2,1)} %copy-done.10, bf16[192,2048]{1,0:T(8,128)(2,1)} %copy-done.11, bf16[3,2048,256]{2,1,0:T(8,128)(2,1)} %bitcast.62, ...), custom_call_target="tpu_custom_call" | custom-call | flops 2415919104 | bytes 6291456 | tf_op jit(solution)/shard_map/project_and_rotate/pallas_call | solution.py:184
  164.7 6.5 %collective-permute-start.32 = (bf16[384,384]{1,0:T(8,128)(2,1)}, bf16[384,384]{1,0:T(8,128)(2,1)S(1)}, u32[]{:S(2)}, u32[]{:S(2)}) collective-permute-start(bf16[384,384]{1,0:T(8,128)(2,1)} %get-tuple-element.47), channel_id=1, source_target_pairs={{0,8},{8,16},{16,24},{24,0},{1,9},{9,17},{17,25},{25,1},{2,10},{10... | collective-permute-start | bytes 884744 | tf_op jit(solution)/shard_map/ppermute | solution.py:507
  171.2 3.3 %collective-permute-start.34 = (bf16[384,384]{1,0:T(8,128)(2,1)}, bf16[384,384]{1,0:T(8,128)(2,1)S(1)}, u32[]{:S(2)}, u32[]{:S(2)}) collective-permute-start(bf16[384,384]{1,0:T(8,128)(2,1)} %get-tuple-element.48), channel_id=1, source_target_pairs={{0,16},{8,24},{16,0},{24,8},{1,17},{9,25},{17,1},{25,9},{2,18},{10... | collective-permute-start | bytes 884744 | tf_op jit(solution)/shard_map/ppermute | solution.py:507
  175.1 7.0 %collective-permute-done.32.rest_30_ = bf16[384,384]{1,0:T(8,128)(2,1)S(1)} collective-permute-done((bf16[384,384]{1,0:T(8,128)(2,1)}, bf16[384,384]{1,0:T(8,128)(2,1)S(1)}, u32[]{:S(2)}, u32[]{:S(2)}) %collective-permute-start.32) | collective-permute-done | bytes 294944 | tf_op jit(solution)/shard_map/ppermute | solution.py:507
  182.1 12.3 %collective-permute-done.34.rest_32_ = bf16[384,384]{1,0:T(8,128)(2,1)S(1)} collective-permute-done((bf16[384,384]{1,0:T(8,128)(2,1)}, bf16[384,384]{1,0:T(8,128)(2,1)S(1)}, u32[]{:S(2)}, u32[]{:S(2)}) %collective-permute-start.34) | collective-permute-done | bytes 294944 | tf_op jit(solution)/shard_map/ppermute | solution.py:507
  194.9 0.6 pad_add_fusion.place
  196.7 0.7 copy-done.40
  197.4 31.6 %attend_one_head.1 = bf16[4,12,128,128]{3,2,1,0:T(8,128)(2,1)} custom-call(s32[3]{0:T(128)} %pad_add_fusion.place, s32[6,12]{1,0:T(8,128)} %rest_0_.1, s32[6,12]{1,0:T(8,128)} %copy-done.42, s32[6,12]{1,0:T(8,128)} %copy-done.43, s32[6,12]{1,0:T(8,128)} %copy-done.44, bf16[384,384]{1,0:T(8,128)(2,1)} %get-tuple-element.30.rest_4_, ...), custom_call_target="tpu_custom_call" | custom-call | flops 9663676416 | bytes 15728640 | tf_op jit(solution)/shard_map/attend_one_head/pallas_call | solution.py:393
  229.1 1.5 fusion.20
  230.6 5.9 %collective-permute-start.40 = (bf16[12,128,128]{2,1,0:T(8,128)(2,1)S(1)}, bf16[12,128,128]{2,1,0:T(8,128)(2,1)S(1)}, u32[]{:S(2)}, u32[]{:S(2)}) collective-permute-start(bf16[12,128,128]{2,1,0:T(8,128)(2,1)S(1)} %get-tuple-element.57), channel_id=1, source_target_pairs={{0,24},{8,0},{16,8},{24,16},{1,25},{9,1},{17,9},{25,17},{2,26},{10... | collective-permute-start | bytes 1179656 | tf_op jit(solution)/shard_map/ppermute | solution.py:507
  236.5 1.9 collective-permute-start.39
  238.4 8.3 %collective-permute-done.40 = bf16[12,128,128]{2,1,0:T(8,128)(2,1)S(1)} collective-permute-done((bf16[12,128,128]{2,1,0:T(8,128)(2,1)S(1)}, bf16[12,128,128]{2,1,0:T(8,128)(2,1)S(1)}, u32[]{:S(2)}, u32[]{:S(2)}) %collective-permute-start.40) | collective-permute-done | bytes 393248 | tf_op jit(solution)/shard_map/ppermute | solution.py:507
  246.6 26.5 %collective-permute-done.39 = bf16[12,128,128]{2,1,0:T(8,128)(2,1)S(1)} collective-permute-done((bf16[12,128,128]{2,1,0:T(8,128)(2,1)S(1)}, bf16[12,128,128]{2,1,0:T(8,128)(2,1)S(1)}, u32[]{:S(2)}, u32[]{:S(2)}) %collective-permute-start.39) | collective-permute-done | bytes 393248 | tf_op jit(solution)/shard_map/ppermute | solution.py:507
  273.3 1.1 fusion.19
  274.4 2.3 collective-permute-start.43
  276.8 0.5 collective-permute-start.42
  277.3 0.6 collective-permute-start.41
  277.9 9.5 %collective-permute-done.43.rest_3_ = bf16[4,3,128,128]{3,2,1,0:T(8,128)(2,1)S(1)} collective-permute-done((bf16[4,3,128,128]{3,2,1,0:T(8,128)(2,1)S(1)}, bf16[4,3,128,128]{3,2,1,0:T(8,128)(2,1)S(1)}, u32[]{:S(2)}, u32[]{:S(2)}) %collective-permute-start.43) | collective-permute-done | bytes 393248 | tf_op jit(solution)/shard_map/ppermute | solution.py:574
  287.4 7.0 %collective-permute-done.42.rest_2_ = bf16[4,3,128,128]{3,2,1,0:T(8,128)(2,1)S(1)} collective-permute-done((bf16[4,3,128,128]{3,2,1,0:T(8,128)(2,1)S(1)}, bf16[4,3,128,128]{3,2,1,0:T(8,128)(2,1)S(1)}, u32[]{:S(2)}, u32[]{:S(2)}) %collective-permute-start.42) | collective-permute-done | bytes 393248 | tf_op jit(solution)/shard_map/ppermute | solution.py:574
  294.7 1.9 collective-permute-done.44.rest_4_
  296.6 0.8 copy-done.6
  297.4 11.0 %project_out.1 = bf16[384,2048]{1,0:T(8,128)(2,1)} custom-call(s32[3]{0:T(128)} %pad_add_fusion.place, bf16[4,3,128,128]{3,2,1,0:T(8,128)(2,1)} %get-tuple-element.52.rest_0_, bf16[4,3,128,128]{3,2,1,0:T(8,128)(2,1)} %copy-done.5, bf16[4,3,128,128]{3,2,1,0:T(8,128)(2,1)} %copy-done.4, bf16[4,3,128,128]{3,2,1,0:T(8,128)(2,1)} %copy-done.3, ...), custom_call_target="tpu_custom_call" | custom-call | flops 3221225472 | bytes 8388608 | tf_op jit(solution)/shard_map/project_out/pallas_call | solution.py:466
  (165 shorter events, 8.5 us)
Async XLA Ops:
  6.5 290.1 %all-gather.2.cloned.1.call-start = ((), (), s32[]{:S(2)}) async-start(), calls=%async_computation | async-start | bytes 9437184 | tf_op jit(solution)/shard_map/all_gather | solution.py:568
  6.5 13.1 %collective-permute-start.3 = (bf16[3,2048,256]{2,1,0:T(8,128)(2,1)}, bf16[3,2048,256]{2,1,0:T(8,128)(2,1)}, u32[]{:S(2)}, u32[]{:S(2)}) collective-permute-start(bf16[3,2048,256]{2,1,0:T(8,128)(2,1)} %bitcast.58), channel_id=1, source_target_pairs={{0,1},{1,0},{2,3},{3,2},{4,5},{5,4},{6,7},{7,6},{8,9},{9,8},{10,11... | collective-permute-start | bytes 9437192 | tf_op jit(solution)/shard_map/ppermute | solution.py:514
  9.4 21.0 %collective-permute-start.11 = (bf16[192,2048]{1,0:T(8,128)(2,1)S(1)}, bf16[192,2048]{1,0:T(8,128)(2,1)S(1)}, u32[]{:S(2)}, u32[]{:S(2)}) collective-permute-start(bf16[192,2048]{1,0:T(8,128)(2,1)S(1)} %get-tuple-element.64.second), channel_id=1, source_target_pairs={{0,2},{1,3},{2,0},{3,1},{4,6},{5,7},{6,4},{7,5},{8,10},{9,11},{10,... | collective-permute-start | bytes 2359304 | tf_op jit(solution)/shard_map/ppermute | solution.py:525
  12.1 20.4 %collective-permute-start.12 = (bf16[192,2048]{1,0:T(8,128)(2,1)S(1)}, bf16[192,2048]{1,0:T(8,128)(2,1)S(1)}, u32[]{:S(2)}, u32[]{:S(2)}) collective-permute-start(bf16[192,2048]{1,0:T(8,128)(2,1)S(1)} %get-tuple-element.64.second), channel_id=1, source_target_pairs={{0,4},{1,5},{2,6},{3,7},{4,0},{5,1},{6,2},{7,3},{8,12},{9,13},{10,... | collective-permute-start | bytes 2359304 | tf_op jit(solution)/shard_map/ppermute | solution.py:526
  13.6 33.5 %collective-permute-start.13 = (bf16[192,2048]{1,0:T(8,128)(2,1)S(1)}, bf16[192,2048]{1,0:T(8,128)(2,1)}, u32[]{:S(2)}, u32[]{:S(2)}) collective-permute-start(bf16[192,2048]{1,0:T(8,128)(2,1)S(1)} %get-tuple-element.65.first), channel_id=1, source_target_pairs={{0,2},{1,3},{2,0},{3,1},{4,6},{5,7},{6,4},{7,5},{8,10},{9,11},{10,... | collective-permute-start | bytes 2359304 | tf_op jit(solution)/shard_map/ppermute | solution.py:523
  14.1 34.4 %collective-permute-start.14 = (bf16[192,2048]{1,0:T(8,128)(2,1)S(1)}, bf16[192,2048]{1,0:T(8,128)(2,1)}, u32[]{:S(2)}, u32[]{:S(2)}) collective-permute-start(bf16[192,2048]{1,0:T(8,128)(2,1)S(1)} %get-tuple-element.65.first), channel_id=1, source_target_pairs={{0,4},{1,5},{2,6},{3,7},{4,0},{5,1},{6,2},{7,3},{8,12},{9,13},{10,... | collective-permute-start | bytes 2359304 | tf_op jit(solution)/shard_map/ppermute | solution.py:524
  30.4 64.5 %copy-start.8 = (bf16[192,2048]{1,0:T(8,128)(2,1)}, bf16[192,2048]{1,0:T(8,128)(2,1)S(1)}, u32[]{:S(2)}) copy-start(bf16[192,2048]{1,0:T(8,128)(2,1)S(1)} %collective-permute-done.11.first) | copy-start | bytes 2359300
  32.5 62.4 %copy-start.9 = (bf16[192,2048]{1,0:T(8,128)(2,1)}, bf16[192,2048]{1,0:T(8,128)(2,1)S(1)}, u32[]{:S(2)}) copy-start(bf16[192,2048]{1,0:T(8,128)(2,1)S(1)} %collective-permute-done.12.second) | copy-start | bytes 2359300
  48.6 18.9 %collective-permute-start.29 = (bf16[192,2048]{1,0:T(8,128)(2,1)}, bf16[192,2048]{1,0:T(8,128)(2,1)S(1)}, u32[]{:S(2)}, u32[]{:S(2)}) collective-permute-start(bf16[192,2048]{1,0:T(8,128)(2,1)} %collective-permute-done.14.second), channel_id=1, source_target_pairs={{0,2},{1,3},{2,0},{3,1},{4,6},{5,7},{6,4},{7,5},{8,10},{9,11},{10,... | collective-permute-start | bytes 2359304 | tf_op jit(solution)/shard_map/ppermute | solution.py:561
  48.9 18.7 %collective-permute-start.30 = (bf16[192,2048]{1,0:T(8,128)(2,1)S(1)}, bf16[192,2048]{1,0:T(8,128)(2,1)S(1)}, u32[]{:S(2)}, u32[]{:S(2)}) collective-permute-start(bf16[192,2048]{1,0:T(8,128)(2,1)S(1)} %collective-permute-done.11.first), channel_id=1, source_target_pairs={{0,4},{1,5},{2,6},{3,7},{4,0},{5,1},{6,2},{7,3},{8,12},{9,13},{10,... | collective-permute-start | bytes 2359304 | tf_op jit(solution)/shard_map/ppermute | solution.py:562
  67.7 35.9 %collective-permute-start.4 = (bf16[384,384]{1,0:T(8,128)(2,1)}, bf16[384,384]{1,0:T(8,128)(2,1)S(1)}, u32[]{:S(2)}, u32[]{:S(2)}) collective-permute-start(bf16[384,384]{1,0:T(8,128)(2,1)} %get-tuple-element.30.rest_4_), channel_id=1, source_target_pairs={{0,1},{1,0},{2,3},{3,2},{4,5},{5,4},{6,7},{7,6},{8,9},{9,8},{10,11... | collective-permute-start | bytes 884744 | tf_op jit(solution)/shard_map/ppermute | solution.py:554
  67.8 35.9 %collective-permute-start.5 = (bf16[384,384]{1,0:T(8,128)(2,1)}, bf16[384,384]{1,0:T(8,128)(2,1)S(1)}, u32[]{:S(2)}, u32[]{:S(2)}) collective-permute-start(bf16[384,384]{1,0:T(8,128)(2,1)} %get-tuple-element.31), channel_id=1, source_target_pairs={{0,8},{8,16},{16,24},{24,0},{1,9},{9,17},{17,25},{25,1},{2,10},{10... | collective-permute-start | bytes 884744 | tf_op jit(solution)/shard_map/ppermute | solution.py:507
  69.3 35.0 %collective-permute-start.7 = (bf16[384,384]{1,0:T(8,128)(2,1)}, bf16[384,384]{1,0:T(8,128)(2,1)S(1)}, u32[]{:S(2)}, u32[]{:S(2)}) collective-permute-start(bf16[384,384]{1,0:T(8,128)(2,1)} %get-tuple-element.32), channel_id=1, source_target_pairs={{0,16},{8,24},{16,0},{24,8},{1,17},{9,25},{17,1},{25,9},{2,18},{10... | collective-permute-start | bytes 884744 | tf_op jit(solution)/shard_map/ppermute | solution.py:507
  71.9 13.8 %collective-permute-start = (s32[6,12]{1,0:T(8,128)S(1)}, s32[6,12]{1,0:T(8,128)S(1)}, u32[]{:S(2)}, u32[]{:S(2)}) collective-permute-start(s32[6,12]{1,0:T(8,128)S(1)} %copy-done.41), channel_id=1, source_target_pairs={{0,8},{8,16},{16,24},{24,0},{1,9},{9,17},{17,25},{25,1},{2,10},{10... | collective-permute-start | bytes 872 | tf_op jit(solution)/shard_map/ppermute | solution.py:507
  72.2 22.7 %collective-permute-start.1 = (s32[6,12]{1,0:T(8,128)S(1)}, s32[6,12]{1,0:T(8,128)S(1)}, u32[]{:S(2)}, u32[]{:S(2)}) collective-permute-start(s32[6,12]{1,0:T(8,128)S(1)} %copy-done.41), channel_id=1, source_target_pairs={{0,16},{8,24},{16,0},{24,8},{1,17},{9,25},{17,1},{25,9},{2,18},{10... | collective-permute-start | bytes 872 | tf_op jit(solution)/shard_map/ppermute | solution.py:507
  85.7 17.9 %collective-permute-start.2 = (s32[6,12]{1,0:T(8,128)S(1)}, s32[6,12]{1,0:T(8,128)S(1)}, u32[]{:S(2)}, u32[]{:S(2)}) collective-permute-start(s32[6,12]{1,0:T(8,128)S(1)} %copy-done.41), channel_id=1, source_target_pairs={{0,24},{8,0},{16,8},{24,16},{1,25},{9,1},{17,9},{25,17},{2,26},{10... | collective-permute-start | bytes 872 | tf_op jit(solution)/shard_map/ppermute | solution.py:507
  95.0 22.0 %collective-permute-start.9 = (bf16[384,384]{1,0:T(8,128)(2,1)S(1)}, bf16[384,384]{1,0:T(8,128)(2,1)S(1)}, u32[]{:S(2)}, u32[]{:S(2)}) collective-permute-start(bf16[384,384]{1,0:T(8,128)(2,1)S(1)} %copy-done.30), channel_id=1, source_target_pairs={{0,24},{8,0},{16,8},{24,16},{1,25},{9,1},{17,9},{25,17},{2,26},{10... | collective-permute-start | bytes 884744 | tf_op jit(solution)/shard_map/ppermute | solution.py:507
  103.6 13.5 %collective-permute-start.15 = (bf16[384,384]{1,0:T(8,128)(2,1)}, bf16[384,384]{1,0:T(8,128)(2,1)S(1)}, u32[]{:S(2)}, u32[]{:S(2)}) collective-permute-start(bf16[384,384]{1,0:T(8,128)(2,1)} %get-tuple-element.36.rest_12_), channel_id=1, source_target_pairs={{0,1},{1,0},{2,3},{3,2},{4,5},{5,4},{6,7},{7,6},{8,9},{9,8},{10,11... | collective-permute-start | bytes 884744 | tf_op jit(solution)/shard_map/ppermute | solution.py:554
  103.6 14.3 %collective-permute-start.16 = (bf16[384,384]{1,0:T(8,128)(2,1)}, bf16[384,384]{1,0:T(8,128)(2,1)S(1)}, u32[]{:S(2)}, u32[]{:S(2)}) collective-permute-start(bf16[384,384]{1,0:T(8,128)(2,1)} %get-tuple-element.37), channel_id=1, source_target_pairs={{0,8},{8,16},{16,24},{24,0},{1,9},{9,17},{17,25},{25,1},{2,10},{10... | collective-permute-start | bytes 884744 | tf_op jit(solution)/shard_map/ppermute | solution.py:507
  103.7 26.3 %collective-permute-start.18 = (bf16[384,384]{1,0:T(8,128)(2,1)}, bf16[384,384]{1,0:T(8,128)(2,1)S(1)}, u32[]{:S(2)}, u32[]{:S(2)}) collective-permute-start(bf16[384,384]{1,0:T(8,128)(2,1)} %get-tuple-element.38), channel_id=1, source_target_pairs={{0,16},{8,24},{16,0},{24,8},{1,17},{9,25},{17,1},{25,9},{2,18},{10... | collective-permute-start | bytes 884744 | tf_op jit(solution)/shard_map/ppermute | solution.py:507
  104.4 35.2 %collective-permute-start.20 = (bf16[384,384]{1,0:T(8,128)(2,1)}, bf16[384,384]{1,0:T(8,128)(2,1)S(1)}, u32[]{:S(2)}, u32[]{:S(2)}) collective-permute-start(bf16[384,384]{1,0:T(8,128)(2,1)} %get-tuple-element.39), channel_id=1, source_target_pairs={{0,24},{8,0},{16,8},{24,16},{1,25},{9,1},{17,9},{25,17},{2,26},{10... | collective-permute-start | bytes 884744 | tf_op jit(solution)/shard_map/ppermute | solution.py:507
  117.0 22.6 %collective-permute-start.22 = (bf16[384,384]{1,0:T(8,128)(2,1)}, bf16[384,384]{1,0:T(8,128)(2,1)S(1)}, u32[]{:S(2)}, u32[]{:S(2)}) collective-permute-start(bf16[384,384]{1,0:T(8,128)(2,1)} %get-tuple-element.42.rest_20_), channel_id=1, source_target_pairs={{0,1},{1,0},{2,3},{3,2},{4,5},{5,4},{6,7},{7,6},{8,9},{9,8},{10,11... | collective-permute-start | bytes 884744 | tf_op jit(solution)/shard_map/ppermute | solution.py:554
  117.1 23.1 %collective-permute-start.23 = (bf16[384,384]{1,0:T(8,128)(2,1)}, bf16[384,384]{1,0:T(8,128)(2,1)S(1)}, u32[]{:S(2)}, u32[]{:S(2)}) collective-permute-start(bf16[384,384]{1,0:T(8,128)(2,1)} %get-tuple-element.43), channel_id=1, source_target_pairs={{0,8},{8,16},{16,24},{24,0},{1,9},{9,17},{17,25},{25,1},{2,10},{10... | collective-permute-start | bytes 884744 | tf_op jit(solution)/shard_map/ppermute | solution.py:507
  117.9 36.3 %collective-permute-start.25 = (bf16[384,384]{1,0:T(8,128)(2,1)}, bf16[384,384]{1,0:T(8,128)(2,1)S(1)}, u32[]{:S(2)}, u32[]{:S(2)}) collective-permute-start(bf16[384,384]{1,0:T(8,128)(2,1)} %get-tuple-element.44), channel_id=1, source_target_pairs={{0,16},{8,24},{16,0},{24,8},{1,17},{9,25},{17,1},{25,9},{2,18},{10... | collective-permute-start | bytes 884744 | tf_op jit(solution)/shard_map/ppermute | solution.py:507
  130.0 24.3 %collective-permute-start.27 = (bf16[384,384]{1,0:T(8,128)(2,1)}, bf16[384,384]{1,0:T(8,128)(2,1)S(1)}, u32[]{:S(2)}, u32[]{:S(2)}) collective-permute-start(bf16[384,384]{1,0:T(8,128)(2,1)} %get-tuple-element.45), channel_id=1, source_target_pairs={{0,24},{8,0},{16,8},{24,16},{1,25},{9,1},{17,9},{25,17},{2,26},{10... | collective-permute-start | bytes 884744 | tf_op jit(solution)/shard_map/ppermute | solution.py:507
  139.5 15.2 %collective-permute-start.6 = (bf16[384,384]{1,0:T(8,128)(2,1)S(1)}, bf16[384,384]{1,0:T(8,128)(2,1)S(1)}, u32[]{:S(2)}, u32[]{:S(2)}) collective-permute-start(bf16[384,384]{1,0:T(8,128)(2,1)S(1)} %collective-permute-done.5.rest_6_), channel_id=1, source_target_pairs={{0,1},{1,0},{2,3},{3,2},{4,5},{5,4},{6,7},{7,6},{8,9},{9,8},{10,11... | collective-permute-start | bytes 884744 | tf_op jit(solution)/shard_map/ppermute | solution.py:554
  139.6 24.4 %collective-permute-start.8 = (bf16[384,384]{1,0:T(8,128)(2,1)S(1)}, bf16[384,384]{1,0:T(8,128)(2,1)S(1)}, u32[]{:S(2)}, u32[]{:S(2)}) collective-permute-start(bf16[384,384]{1,0:T(8,128)(2,1)S(1)} %collective-permute-done.7.rest_8_), channel_id=1, source_target_pairs={{0,1},{1,0},{2,3},{3,2},{4,5},{5,4},{6,7},{7,6},{8,9},{9,8},{10,11... | collective-permute-start | bytes 884744 | tf_op jit(solution)/shard_map/ppermute | solution.py:554
  140.2 24.4 %collective-permute-start.10 = (bf16[384,384]{1,0:T(8,128)(2,1)S(1)}, bf16[384,384]{1,0:T(8,128)(2,1)S(1)}, u32[]{:S(2)}, u32[]{:S(2)}) collective-permute-start(bf16[384,384]{1,0:T(8,128)(2,1)S(1)} %collective-permute-done.9.rest_10_), channel_id=1, source_target_pairs={{0,1},{1,0},{2,3},{3,2},{4,5},{5,4},{6,7},{7,6},{8,9},{9,8},{10,11... | collective-permute-start | bytes 884744 | tf_op jit(solution)/shard_map/ppermute | solution.py:554
  154.2 10.5 %collective-permute-start.17 = (bf16[384,384]{1,0:T(8,128)(2,1)S(1)}, bf16[384,384]{1,0:T(8,128)(2,1)S(1)}, u32[]{:S(2)}, u32[]{:S(2)}) collective-permute-start(bf16[384,384]{1,0:T(8,128)(2,1)S(1)} %collective-permute-done.16.rest_14_), channel_id=1, source_target_pairs={{0,1},{1,0},{2,3},{3,2},{4,5},{5,4},{6,7},{7,6},{8,9},{9,8},{10,11... | collective-permute-start | bytes 884744 | tf_op jit(solution)/shard_map/ppermute | solution.py:554
  154.3 17.0 %collective-permute-start.19 = (bf16[384,384]{1,0:T(8,128)(2,1)S(1)}, bf16[384,384]{1,0:T(8,128)(2,1)S(1)}, u32[]{:S(2)}, u32[]{:S(2)}) collective-permute-start(bf16[384,384]{1,0:T(8,128)(2,1)S(1)} %collective-permute-done.18.rest_16_), channel_id=1, source_target_pairs={{0,1},{1,0},{2,3},{3,2},{4,5},{5,4},{6,7},{7,6},{8,9},{9,8},{10,11... | collective-permute-start | bytes 884744 | tf_op jit(solution)/shard_map/ppermute | solution.py:554
  154.8 19.7 %collective-permute-start.21 = (bf16[384,384]{1,0:T(8,128)(2,1)S(1)}, bf16[384,384]{1,0:T(8,128)(2,1)S(1)}, u32[]{:S(2)}, u32[]{:S(2)}) collective-permute-start(bf16[384,384]{1,0:T(8,128)(2,1)S(1)} %collective-permute-done.20.rest_18_), channel_id=1, source_target_pairs={{0,1},{1,0},{2,3},{3,2},{4,5},{5,4},{6,7},{7,6},{8,9},{9,8},{10,11... | collective-permute-start | bytes 884744 | tf_op jit(solution)/shard_map/ppermute | solution.py:554
  164.1 10.4 %collective-permute-start.24 = (bf16[384,384]{1,0:T(8,128)(2,1)S(1)}, bf16[384,384]{1,0:T(8,128)(2,1)S(1)}, u32[]{:S(2)}, u32[]{:S(2)}) collective-permute-start(bf16[384,384]{1,0:T(8,128)(2,1)S(1)} %collective-permute-done.23.rest_22_), channel_id=1, source_target_pairs={{0,1},{1,0},{2,3},{3,2},{4,5},{5,4},{6,7},{7,6},{8,9},{9,8},{10,11... | collective-permute-start | bytes 884744 | tf_op jit(solution)/shard_map/ppermute | solution.py:554
  164.6 10.1 %collective-permute-start.26 = (bf16[384,384]{1,0:T(8,128)(2,1)S(1)}, bf16[384,384]{1,0:T(8,128)(2,1)S(1)}, u32[]{:S(2)}, u32[]{:S(2)}) collective-permute-start(bf16[384,384]{1,0:T(8,128)(2,1)S(1)} %collective-permute-done.25.rest_24_), channel_id=1, source_target_pairs={{0,1},{1,0},{2,3},{3,2},{4,5},{5,4},{6,7},{7,6},{8,9},{9,8},{10,11... | collective-permute-start | bytes 884744 | tf_op jit(solution)/shard_map/ppermute | solution.py:554
  164.7 17.4 %collective-permute-start.32 = (bf16[384,384]{1,0:T(8,128)(2,1)}, bf16[384,384]{1,0:T(8,128)(2,1)S(1)}, u32[]{:S(2)}, u32[]{:S(2)}) collective-permute-start(bf16[384,384]{1,0:T(8,128)(2,1)} %get-tuple-element.47), channel_id=1, source_target_pairs={{0,8},{8,16},{16,24},{24,0},{1,9},{9,17},{17,25},{25,1},{2,10},{10... | collective-permute-start | bytes 884744 | tf_op jit(solution)/shard_map/ppermute | solution.py:507
  171.2 23.2 %collective-permute-start.34 = (bf16[384,384]{1,0:T(8,128)(2,1)}, bf16[384,384]{1,0:T(8,128)(2,1)S(1)}, u32[]{:S(2)}, u32[]{:S(2)}) collective-permute-start(bf16[384,384]{1,0:T(8,128)(2,1)} %get-tuple-element.48), channel_id=1, source_target_pairs={{0,16},{8,24},{16,0},{24,8},{1,17},{9,25},{17,1},{25,9},{2,18},{10... | collective-permute-start | bytes 884744 | tf_op jit(solution)/shard_map/ppermute | solution.py:507
  174.5 19.9 %collective-permute-start.36 = (bf16[384,384]{1,0:T(8,128)(2,1)}, bf16[384,384]{1,0:T(8,128)(2,1)S(1)}, u32[]{:S(2)}, u32[]{:S(2)}) collective-permute-start(bf16[384,384]{1,0:T(8,128)(2,1)} %get-tuple-element.49), channel_id=1, source_target_pairs={{0,24},{8,0},{16,8},{24,16},{1,25},{9,1},{17,9},{25,17},{2,26},{10... | collective-permute-start | bytes 884744 | tf_op jit(solution)/shard_map/ppermute | solution.py:507
  174.5 21.0 %collective-permute-start.28 = (bf16[384,384]{1,0:T(8,128)(2,1)S(1)}, bf16[384,384]{1,0:T(8,128)(2,1)S(1)}, u32[]{:S(2)}, u32[]{:S(2)}) collective-permute-start(bf16[384,384]{1,0:T(8,128)(2,1)S(1)} %collective-permute-done.27.rest_26_), channel_id=1, source_target_pairs={{0,1},{1,0},{2,3},{3,2},{4,5},{5,4},{6,7},{7,6},{8,9},{9,8},{10,11... | collective-permute-start | bytes 884744 | tf_op jit(solution)/shard_map/ppermute | solution.py:554
  174.6 20.9 %collective-permute-start.31 = (bf16[384,384]{1,0:T(8,128)(2,1)}, bf16[384,384]{1,0:T(8,128)(2,1)S(1)}, u32[]{:S(2)}, u32[]{:S(2)}) collective-permute-start(bf16[384,384]{1,0:T(8,128)(2,1)} %get-tuple-element.46.rest_28_), channel_id=1, source_target_pairs={{0,1},{1,0},{2,3},{3,2},{4,5},{5,4},{6,7},{7,6},{8,9},{9,8},{10,11... | collective-permute-start | bytes 884744 | tf_op jit(solution)/shard_map/ppermute | solution.py:554
  182.1 13.5 %collective-permute-start.33 = (bf16[384,384]{1,0:T(8,128)(2,1)S(1)}, bf16[384,384]{1,0:T(8,128)(2,1)S(1)}, u32[]{:S(2)}, u32[]{:S(2)}) collective-permute-start(bf16[384,384]{1,0:T(8,128)(2,1)S(1)} %collective-permute-done.32.rest_30_), channel_id=1, source_target_pairs={{0,1},{1,0},{2,3},{3,2},{4,5},{5,4},{6,7},{7,6},{8,9},{9,8},{10,11... | collective-permute-start | bytes 884744 | tf_op jit(solution)/shard_map/ppermute | solution.py:554
  194.4 1.6 collective-permute-start.35
  194.4 2.0 collective-permute-start.37
  230.6 16.1 %collective-permute-start.40 = (bf16[12,128,128]{2,1,0:T(8,128)(2,1)S(1)}, bf16[12,128,128]{2,1,0:T(8,128)(2,1)S(1)}, u32[]{:S(2)}, u32[]{:S(2)}) collective-permute-start(bf16[12,128,128]{2,1,0:T(8,128)(2,1)S(1)} %get-tuple-element.57), channel_id=1, source_target_pairs={{0,24},{8,0},{16,8},{24,16},{1,25},{9,1},{17,9},{25,17},{2,26},{10... | collective-permute-start | bytes 1179656 | tf_op jit(solution)/shard_map/ppermute | solution.py:507
  236.5 36.6 %collective-permute-start.39 = (bf16[12,128,128]{2,1,0:T(8,128)(2,1)S(1)}, bf16[12,128,128]{2,1,0:T(8,128)(2,1)S(1)}, u32[]{:S(2)}, u32[]{:S(2)}) collective-permute-start(bf16[12,128,128]{2,1,0:T(8,128)(2,1)S(1)} %get-tuple-element.58), channel_id=1, source_target_pairs={{0,16},{8,24},{16,0},{24,8},{1,17},{9,25},{17,1},{25,9},{2,18},{10... | collective-permute-start | bytes 1179656 | tf_op jit(solution)/shard_map/ppermute | solution.py:507
  238.4 34.7 %collective-permute-start.38 = (bf16[12,128,128]{2,1,0:T(8,128)(2,1)S(1)}, bf16[12,128,128]{2,1,0:T(8,128)(2,1)S(1)}, u32[]{:S(2)}, u32[]{:S(2)}) collective-permute-start(bf16[12,128,128]{2,1,0:T(8,128)(2,1)S(1)} %get-tuple-element.59), channel_id=1, source_target_pairs={{0,8},{8,16},{16,24},{24,0},{1,9},{9,17},{17,25},{25,1},{2,10},{10... | collective-permute-start | bytes 1179656 | tf_op jit(solution)/shard_map/ppermute | solution.py:507
  274.4 13.0 %collective-permute-start.43 = (bf16[4,3,128,128]{3,2,1,0:T(8,128)(2,1)S(1)}, bf16[4,3,128,128]{3,2,1,0:T(8,128)(2,1)S(1)}, u32[]{:S(2)}, u32[]{:S(2)}) collective-permute-start(bf16[4,3,128,128]{3,2,1,0:T(8,128)(2,1)S(1)} %get-tuple-element.53), channel_id=1, source_target_pairs={{0,6},{1,7},{2,4},{3,5},{4,2},{5,3},{6,0},{7,1},{8,14},{9,15},{10,... | collective-permute-start | bytes 1179656 | tf_op jit(solution)/shard_map/ppermute | solution.py:574
  276.8 17.7 %collective-permute-start.42 = (bf16[4,3,128,128]{3,2,1,0:T(8,128)(2,1)S(1)}, bf16[4,3,128,128]{3,2,1,0:T(8,128)(2,1)S(1)}, u32[]{:S(2)}, u32[]{:S(2)}) collective-permute-start(bf16[4,3,128,128]{3,2,1,0:T(8,128)(2,1)S(1)} %get-tuple-element.54), channel_id=1, source_target_pairs={{0,4},{1,5},{2,6},{3,7},{4,0},{5,1},{6,2},{7,3},{8,12},{9,13},{10,... | collective-permute-start | bytes 1179656 | tf_op jit(solution)/shard_map/ppermute | solution.py:574
  277.3 17.2 %collective-permute-start.41 = (bf16[4,3,128,128]{3,2,1,0:T(8,128)(2,1)S(1)}, bf16[4,3,128,128]{3,2,1,0:T(8,128)(2,1)S(1)}, u32[]{:S(2)}, u32[]{:S(2)}) collective-permute-start(bf16[4,3,128,128]{3,2,1,0:T(8,128)(2,1)S(1)} %get-tuple-element.55), channel_id=1, source_target_pairs={{0,2},{1,3},{2,0},{3,1},{4,6},{5,7},{6,4},{7,5},{8,10},{9,11},{10,... | collective-permute-start | bytes 1179656 | tf_op jit(solution)/shard_map/ppermute | solution.py:574
  294.6 2.0 collective-permute-start.44
  (43 other events, 780.8 us)
Sparse Core Ops, SparseCore 0:
  67.8 55.4 all-gather.1

commit v3 on v2

v3 whole, which is shorter than its diff:
```python
import functools
import math

import jax
import jax.numpy as jnp
from jax import lax
from jax.experimental import pallas as pl
from jax.experimental.pallas import tpu as pltpu
from jax.sharding import PartitionSpec as P

D = 2048
HD = 128
BLK = 512
TILE = 128
STEP = 12


EPS = 1e-05
THETA = 10000.0
VMEM_LIMIT = 56 * 1024 * 1024


def rotate(vectors, cosine, sine):
    half = vectors.shape[-1] // 2
    first = vectors[..., :half]
    second = vectors[..., half:]
    return jnp.concatenate(
        [first * cosine - second * sine, second * cosine + first * sine], axis=-1
    )


def general(hidden_in, norm_gain, w_qkv, w_out, block_lists):
    section_id = lax.axis_index("section")
    width = w_qkv.shape[2]
    heads_here = width // HD
    blocks_here = block_lists.shape[0]
    tok_dev = blocks_here * BLK
    scale = 1.0 / math.sqrt(HD)
    resid = hidden_in.astype(jnp.float32)
    normed = (
        resid * lax.rsqrt(jnp.mean(resid * resid, axis=-1, keepdims=True) + EPS) * norm_gain
    ).astype(jnp.bfloat16)
    flat_weight = w_qkv.reshape(D, 3 * width)
    frequency = THETA ** (-(2.0 * jnp.arange(HD // 2, dtype=jnp.float32)) / HD)
    piece = lax.all_gather(normed, "head", axis=0, tiled=True)
    count = piece.shape[0]
    mixed_rows = jnp.dot(piece, flat_weight, preferred_element_type=jnp.float32).reshape(
        count, 3, heads_here, HD
    )
    positions = (section_id * tok_dev + jnp.arange(count, dtype=jnp.int32)).astype(jnp.float32)
    angle = positions[:, None] * frequency[None, :]
    cosine = jnp.cos(angle)[:, None, :]
    sine = jnp.sin(angle)[:, None, :]
    query = rotate(mixed_rows[:, 0], cosine, sine).astype(jnp.bfloat16).reshape(count, width)
    keys = rotate(mixed_rows[:, 1], cosine, sine).astype(jnp.bfloat16).reshape(count, width)
    values = mixed_rows[:, 2].astype(jnp.bfloat16).reshape(count, width)
    keys_all, values_all = (
        lax.all_gather(keys, "section", axis=0, tiled=True),
        lax.all_gather(values, "section", axis=0, tiled=True),
    )
    count_blocks = block_lists.shape[0]
    query_blocks = query.reshape(count_blocks, BLK, heads_here, HD)
    block_ids = section_id * blocks_here + jnp.arange(count_blocks, dtype=jnp.int32)

    def one_block(carry, item):
        query_block, block_row, block_id = item
        live_slots = jnp.sum((block_row >= 0).astype(jnp.int32))
        query_positions = block_id * BLK + jnp.arange(BLK, dtype=jnp.int32)

        def one_slot(slot, state):
            highest, total, weighted = state
            source = block_row[slot]
            key_block = lax.dynamic_slice_in_dim(keys_all, source * BLK, BLK, 0).reshape(
                BLK, heads_here, HD
            )
            value_block = lax.dynamic_slice_in_dim(values_all, source * BLK, BLK, 0).reshape(
                BLK, heads_here, HD
            )
            scores = (
                jnp.einsum(
                    "qhd,khd->hqk", query_block, key_block, preferred_element_type=jnp.float32
                )
                * scale
            )
            key_positions = source * BLK + jnp.arange(BLK, dtype=jnp.int32)
            scores = jnp.where(
                key_positions[None, None, :] <= query_positions[None, :, None], scores, -jnp.inf
            )
            new_highest = jnp.maximum(highest, jnp.max(scores, axis=-1))
            factor = jnp.exp(highest - new_highest)
            weights = jnp.exp(scores - new_highest[..., None])
            total = total * factor + jnp.sum(weights, axis=-1)
            update = jnp.einsum(
                "hqk,khd->hqd",
                weights.astype(jnp.bfloat16),
                value_block,
                preferred_element_type=jnp.float32,
            )
            weighted = weighted * factor[..., None] + update
            return (new_highest, total, weighted)

        start_state = (
            jnp.full((heads_here, BLK), -jnp.inf, jnp.float32),
            jnp.zeros((heads_here, BLK), jnp.float32),
            jnp.zeros((heads_here, BLK, HD), jnp.float32),
        )
        highest, total, weighted = lax.fori_loop(0, live_slots, one_slot, start_state)
        result = (
            (weighted / total[..., None])
            .transpose(1, 0, 2)
            .reshape(BLK, width)
            .astype(jnp.bfloat16)
        )
        return (carry, result)

    _, results = lax.scan(
        one_block, jnp.zeros((), jnp.int32), (query_blocks, block_lists, block_ids)
    )
    attended = results.reshape(count_blocks * BLK, width)
    regrouped = lax.all_to_all(attended, "head", split_axis=0, concat_axis=1, tiled=True)
    summed = jnp.dot(
        regrouped,
        lax.all_gather(w_out, "head", axis=0, tiled=True),
        preferred_element_type=jnp.float32,
    )
    return (resid + summed).astype(jnp.bfloat16)


def project_kernel(number, groups, place, *rest):
    pieces, rest = rest[:number], rest[number:]
    own, other, cosine, sine = rest[:4]
    outs, rest = rest[4 : 4 + 4 * groups], rest[4 + 4 * groups :]
    rows, weights, results, row_sems, weight_sems, out_sems = rest
    count = rows.shape[0]
    row_copies, start = [], 0
    for i, ref in enumerate(pieces):
        size = ref.shape[0]
        row_copies.append(
            pltpu.make_async_copy(ref, rows.at[pl.ds(start, size)], row_sems.at[i])
        )
        start += size
    weight_copies = [
        pltpu.make_async_copy(
            ref.at[part],
            weights.at[w * 3 + part],
            weight_sems.at[w * 3 + part],
        )
        for w, ref in enumerate((own, other))
        for part in range(3)
    ]
    for copy in row_copies + weight_copies:
        copy.start()
    for copy in row_copies:
        copy.wait()
    query_scale = math.log2(math.e) / math.sqrt(HD)
    step = count // (2 * max(1, count // 384))
    for w in range(2):
        for part in range(3):
            weight_copies[w * 3 + part].wait()

            def tile(at, w=w, part=part):
                piece = pl.ds(at, step)
                product = jnp.dot(
                    rows[piece], weights[w * 3 + part], preferred_element_type=jnp.float32
                )
                for h in range(2):
                    vector = product[:, h * HD : (h + 1) * HD]
                    if part < 2:
                        turned = pltpu.roll(vector, HD // 2, 1)
                        vector = vector * cosine[piece] + turned * sine[piece]
                    if part == 0:
                        vector = vector * query_scale
                    column = slice(part * HD, (part + 1) * HD)
                    results[w * 2 + h, piece, column] = vector.astype(jnp.bfloat16)

            for at in range(0, count, step):
                tile(at)
    copies = [
        pltpu.make_async_copy(
            results.at[place[shift], pl.ds(group * (count // groups), count // groups)],
            outs[group * 4 + shift],
            out_sems.at[group * 4 + shift],
        )
        for group in range(groups)
        for shift in range(4)
    ]
    for copy in copies:
        copy.start()
    for copy in copies:
        copy.wait()


def project(place, pieces, own, other, cosine, sine, groups=1):
    count = sum(piece.shape[0] for piece in pieces)
    number = len(pieces)
    width = own.shape[2]
    any_space = pl.BlockSpec(memory_space=pl.ANY)
    vmem = pl.BlockSpec(memory_space=pltpu.VMEM)
    return pl.pallas_call(
        functools.partial(project_kernel, number, groups),
        out_shape=[jax.ShapeDtypeStruct((count // groups, 3 * HD), jnp.bfloat16)] * (4 * groups),
        in_specs=[pl.BlockSpec(memory_space=pltpu.SMEM)] + [any_space] * (number + 2) + [vmem] * 2,
        out_specs=[any_space] * (4 * groups),
        scratch_shapes=[
            pltpu.VMEM((count, D), jnp.bfloat16),
            pltpu.VMEM((6, D, width), jnp.bfloat16),
            pltpu.VMEM((4, count, 3 * HD), jnp.bfloat16),
            pltpu.SemaphoreType.DMA((number,)),
            pltpu.SemaphoreType.DMA((6,)),
            pltpu.SemaphoreType.DMA((4 * groups,)),
        ],
        compiler_params=pltpu.CompilerParams(vmem_limit_bytes=VMEM_LIMIT),
        cost_estimate=pl.CostEstimate(
            flops=2 * count * D * 6 * width, bytes_accessed=2 * 6 * D * width, transcendentals=0
        ),
        name="project_and_rotate",
    )(place, *pieces, own, other, cosine, sine)


def attend_kernel(blocks_here, near, place, *rest):
    lists, rest = rest[:4], rest[4:]
    near_pieces, far_pieces, rest = rest[:16], rest[16:22], rest[22:]
    out, rows, query_rows, values_t, queries, tops, sums, item_q, item_k, sems = rest
    section, chip, core = place[0], place[1], place[2]
    rows_here = near_pieces[0].shape[0]
    tok = blocks_here * BLK
    slots = lists[0].shape[1]
    wide = 2 * TILE
    pair_blocks = blocks_here // 2
    total_blocks = 4 * pair_blocks
    pair = chip // 2 if near else 1 - chip // 2
    copies = []

    def fetch(ref, relative, source, side):
        owner, size = chip ^ relative, rows_here
        start = source * tok + owner * (2 * rows_here) + side * rows_here
        number = len(copies)
        copies.append(
            pltpu.make_async_copy(
                ref.at[..., pl.ds(HD, 2 * HD)],
                rows.at[pl.ds(pl.multiple_of(start, size), size)],
                sems.at[number],
            )
        )
        if (relative < 2) == near:
            start = source * (tok // 2) + lax.rem(owner, 2) * (2 * rows_here)
            start = start + side * rows_here
            copies.append(
                pltpu.make_async_copy(
                    ref.at[..., pl.ds(0, HD)],
                    query_rows.at[pl.ds(pl.multiple_of(start, size), size)],
                    sems.at[number + 1],
                )
            )

    for far, pieces in enumerate((near_pieces, far_pieces)):
        side = core if far == 0 else 1 - core
        for shift in range(4):
            source = lax.rem(section - shift + 4, 4)
            for relative in range(4):
                if far == 0:
                    ref = pieces[relative * 4 + shift]
                elif relative == 0:
                    ref = pieces[0].at[shift]
                elif relative < 3:
                    ref = pieces[1].at[(relative - 1) * 4 + shift]
                else:
                    ref = pieces[2 + shift]
                fetch(ref, relative, source, side)
    for copy in copies:
        copy.start()

    def key_block(block):
        return block // pair_blocks * blocks_here + pair * pair_blocks + lax.rem(block, pair_blocks)

    count = jnp.int32(0)
    for shift in range(4):
        block_list = lists[shift]
        first_block = lax.rem(section - shift + 4, 4) * pair_blocks

        def note(local, count, block_list=block_list, first_block=first_block):
            for slot in range(1, slots):
                source = block_list[pair * pair_blocks + local, slot]
                item_q[count] = first_block + local
                item_k[count] = source
                count = count + (source >= 0).astype(jnp.int32)
            return count

        count = lax.fori_loop(0, pair_blocks, note, count)
    for extra in range(STEP):
        item_q[count + extra] = total_blocks
        item_k[count + extra] = 0

    values_t[HD:, :] = jnp.ones((values_t.shape[0] - HD, values_t.shape[1]), jnp.bfloat16)
    queries[total_blocks] = jnp.zeros((wide, HD), jnp.bfloat16)
    tops[total_blocks] = jnp.zeros((8, wide), jnp.float32)
    sums[total_blocks] = jnp.zeros(sums.shape[1:], jnp.float32)
    for copy in copies:
        copy.wait()

    lane = lax.broadcasted_iota(jnp.int32, (BLK, wide), 1)
    key_at = lax.broadcasted_iota(jnp.int32, (BLK, wide), 0)

    def query_place(local):
        middle = lax.rem(local, 3) == 1
        offset = jnp.where(middle, core * TILE, core * wide)
        return offset, jnp.where(middle, TILE, 0)

    def scores_of(source, query):
        at = pl.multiple_of(source * BLK, BLK)
        return lax.dot_general(
            rows[pl.ds(at, BLK), 0:HD],
            query,
            (((1,), (1,)), ((), ())),
            preferred_element_type=jnp.float32,
        )

    def weigh(source, weights):
        at = pl.multiple_of(source * BLK, BLK)
        return jnp.dot(
            values_t[:, pl.ds(at, BLK)],
            weights.astype(jnp.bfloat16),
            preferred_element_type=jnp.float32,
        )

    def masked(local, scores):
        offset, gap = query_place(local)
        query_at = offset + lane + jnp.where(lane >= TILE, gap, 0)
        return jnp.where(key_at <= query_at, scores, -jnp.inf)

    def diagonal(step, carry):
        blocks = [step * 4 + i for i in range(4)]
        scores = []
        for block in blocks:
            offset, gap = query_place(lax.rem(block, pair_blocks))
            start = pl.multiple_of(block * BLK + offset, TILE)
            later = pl.multiple_of(start + TILE + gap, TILE)
            query = jnp.concatenate(
                [query_rows[pl.ds(start, TILE)], query_rows[pl.ds(later, TILE)]], axis=0
            )
            queries[block] = query
            scores.append(scores_of(key_block(block), query))
        for block, score in zip(blocks, scores):
            score = masked(lax.rem(block, pair_blocks), score)
            top = jnp.max(score, axis=0, keepdims=True)
            tops[block] = jnp.broadcast_to(top, (8, wide))
            sums[block] = weigh(key_block(block), jnp.exp2(score - top))
        return carry

    def turn(step, carry):
        for i in range(4):
            at = pl.multiple_of((step * 4 + i) * BLK, BLK)
            values_t[:HD, pl.ds(at, BLK)] = rows[pl.ds(at, BLK), HD : 2 * HD].T
        return carry

    lax.fori_loop(0, blocks_here, turn, 0)
    lax.fori_loop(0, total_blocks // 4, diagonal, 0)

    def below(step, carry):
        items = [step * STEP + i for i in range(STEP)]
        scores = scores_of(item_k[items[0]], queries[item_q[items[0]]])
        held = None
        for i, item in enumerate(items):
            if i + 1 < STEP:
                ahead = scores_of(item_k[items[i + 1]], queries[item_q[items[i + 1]]])
            weights = jnp.exp2(scores - tops[item_q[item], 0:1]).astype(jnp.bfloat16)
            if held is not None:
                sums[item_q[items[i - 1]]] += weigh(item_k[items[i - 1]], held)
            held, scores = weights, ahead
        sums[item_q[items[-1]]] += weigh(item_k[items[-1]], held)
        return carry

    lax.fori_loop(0, (count + STEP - 1) // STEP, below, 0)

    def store(block, result):
        local = lax.rem(block, pair_blocks)
        shift = lax.rem(block // pair_blocks - section + 4, 4)
        for part in range(2):
            tile = 2 * local + part
            which = lax.rem(tile // 3, 2) ^ lax.rem(chip, 2)
            i = lax.rem(tile, 3)
            if near:
                where = jnp.where(i == 2 - 2 * core, 4 + which, which * 2 + i - core)
            else:
                where = which * 3 + jnp.where(i == 2 - 2 * core, 2, i - core)
            out[shift, where] = result[part * TILE : (part + 1) * TILE]

    def leave(step, over):
        for i in range(4):
            block = step * 4 + i
            total = sums[block, HD : HD + 1]
            over = jnp.maximum(over, jnp.where(total < 2.0**100, 0.0, 1.0))
            store(block, (sums[block, 0:HD] / total).T.astype(jnp.bfloat16))
        return over

    over = lax.fori_loop(0, total_blocks // 4, leave, jnp.zeros((1, wide), jnp.float32))

    @pl.when(jnp.max(over) > 0)
    def _():
        for shift in range(4):
            block_list = lists[shift]
            first_block = lax.rem(section - shift + 4, 4) * pair_blocks

            def one_block(local, carry, block_list=block_list, first_block=first_block):
                block = first_block + local
                home = key_block(block)
                entry = pair * pair_blocks + local
                query = queries[block]
                live = jnp.int32(0)
                for slot in range(slots):
                    live = live + (block_list[entry, slot] >= 0).astype(jnp.int32)
                scores = masked(local, scores_of(home, query))
                highest = jnp.max(scores, axis=0, keepdims=True)
                weighted = weigh(home, jnp.exp2(scores - highest))

                def one_slot(slot, state):
                    highest, weighted = state
                    source = block_list[entry, slot]
                    scores = scores_of(source, query)
                    new_highest = jnp.maximum(highest, jnp.max(scores, axis=0, keepdims=True))
                    weights = jnp.exp2(scores - new_highest)
                    weighted = weighted * jnp.exp2(highest - new_highest) + weigh(source, weights)
                    return (new_highest, weighted)

                _, weighted = lax.fori_loop(1, live, one_slot, (highest, weighted))
                result = weighted[0:HD] / weighted[HD : HD + 1]
                store(block, result.T.astype(jnp.bfloat16))
                return carry

            lax.fori_loop(0, pair_blocks, one_block, 0)


def attend(near, place, lists, near_pieces, far_pieces):
    blocks_here, slots = lists[0].shape
    total_blocks = 2 * blocks_here
    tokens = 4 * blocks_here * BLK
    room = total_blocks * slots + STEP
    pairs = total_blocks * slots // 2
    return pl.pallas_call(
        functools.partial(attend_kernel, blocks_here, near),
        out_shape=jax.ShapeDtypeStruct((4, blocks_here, TILE, HD), jnp.bfloat16),
        in_specs=[pl.BlockSpec(memory_space=pltpu.SMEM)] * 5
        + [pl.BlockSpec(memory_space=pl.ANY)] * (len(near_pieces) + len(far_pieces)),
        out_specs=pl.BlockSpec(memory_space=pltpu.VMEM),
        scratch_shapes=[
            pltpu.VMEM((tokens, 2 * HD), jnp.bfloat16),
            pltpu.VMEM((tokens // 2, HD), jnp.bfloat16),
            pltpu.VMEM((HD + 16, tokens), jnp.bfloat16),
            pltpu.VMEM((total_blocks + 1, 2 * TILE, HD), jnp.bfloat16),
            pltpu.VMEM((total_blocks + 1, 8, 2 * TILE), jnp.float32),
            pltpu.VMEM((total_blocks + 1, HD + 16, 2 * TILE), jnp.float32),
            pltpu.SMEM((room,), jnp.int32),
            pltpu.SMEM((room,), jnp.int32),
            pltpu.SemaphoreType.DMA((48,)),
        ],
        compiler_params=pltpu.CompilerParams(vmem_limit_bytes=VMEM_LIMIT),
        cost_estimate=pl.CostEstimate(
            flops=pairs * 4 * BLK * 2 * TILE * HD,
            bytes_accessed=tokens * 5 * HD,
            transcendentals=pairs * BLK * 2 * TILE,
        ),
        name="attend_near" if near else "attend_far",
    )(place, *lists, *near_pieces, *far_pieces)


def finish_kernel(relatives, last, place, *rest):
    number = len(relatives)
    kept, given, rest = rest[:number], rest[number : 2 * number], rest[2 * number :]
    w_out, before, out, attended, weights, sems, given_sems, weight_sems = rest
    section, chip, core = place[0], place[1], place[2]
    odd = lax.rem(chip, 2)
    depth = 4 * HD
    copies, weight_copies = [], []
    for r, relative in enumerate(relatives):
        start = pl.multiple_of((chip ^ relative) * depth, depth)
        weight_copies.append(
            pltpu.make_async_copy(
                w_out.at[pl.ds(start, depth)],
                weights.at[pl.ds(r * depth, depth)],
                weight_sems.at[r],
            )
        )
        for shift in range(4):
            head = r * 4 + lax.rem(section - shift + 4, 4)
            column = pl.ds(pl.multiple_of(head * HD, HD), HD)
            for slot in range(2):
                to = jnp.where(core == 0, slot * (1 + odd), odd if slot == 0 else 2)
                copies.append(
                    pltpu.make_async_copy(
                        kept[r].at[shift, slot],
                        attended.at[pl.ds(pl.multiple_of(to * TILE, TILE), TILE), column],
                        sems.at[(r * 4 + shift) * 2 + slot],
                    )
                )
            to = jnp.where(core == 0, 2 - odd, 1 - odd)
            copies.append(
                pltpu.make_async_copy(
                    given[r].at[shift, 0],
                    attended.at[pl.ds(pl.multiple_of(to * TILE, TILE), TILE), column],
                    given_sems.at[r * 4 + shift],
                )
            )
    for copy in weight_copies + copies:
        copy.start()
    for copy in copies + weight_copies:
        copy.wait()
    half = out.shape[0] // 2
    step = 256
    for column in range(0, out.shape[1], step):
        for at in range(0, out.shape[0], half):
            piece = (slice(at, at + half), slice(column, column + step))
            summed = jnp.dot(
                attended[at : at + half],
                weights[:, column : column + step],
                preferred_element_type=jnp.float32,
            )
            out[piece] = (before[piece].astype(jnp.float32) + summed).astype(out.dtype)


def finish(relatives, place, kept, given, w_out, before, last):
    count = before.shape[0]
    number = len(relatives)
    any_space = pl.BlockSpec(memory_space=pl.ANY)
    vmem = pl.BlockSpec(memory_space=pltpu.VMEM)
    depth = number * 4 * HD
    return pl.pallas_call(
        functools.partial(finish_kernel, relatives, last),
        out_shape=jax.ShapeDtypeStruct((count, D), jnp.bfloat16 if last else jnp.float32),
        in_specs=[pl.BlockSpec(memory_space=pltpu.SMEM)] + [any_space] * (2 * number + 1) + [vmem],
        out_specs=vmem,
        scratch_shapes=[
            pltpu.VMEM((count, depth), jnp.bfloat16),
            pltpu.VMEM((depth, D), jnp.bfloat16),
            pltpu.SemaphoreType.DMA((number * 8,)),
            pltpu.SemaphoreType.DMA((number * 4,)),
            pltpu.SemaphoreType.DMA((number,)),
        ],
        compiler_params=pltpu.CompilerParams(vmem_limit_bytes=VMEM_LIMIT),
        cost_estimate=pl.CostEstimate(
            flops=2 * count * D * depth, bytes_accessed=2 * D * depth, transcendentals=0
        ),
        name="project_out_last" if last else "project_out_first",
    )(place, *kept, *given, w_out, before)


def by_head(hidden_in, norm_gain, w_qkv, w_out, block_lists):
    section = lax.axis_index("section")
    device = lax.axis_index("head")
    chip, core = device // 2, device % 2
    blocks_here = block_lists.shape[0]
    tok = blocks_here * BLK
    rows = hidden_in.shape[0]
    half = rows // 2

    other_core = [(i, i ^ 1) for i in range(8)]
    along_x = [(i, i ^ 2) for i in range(8)]
    along_y = [(i, i ^ 4) for i in range(8)]

    def to_section(array, shift):
        return lax.ppermute(array, "section", [(i, (i + shift) % 4) for i in range(4)])

    place = jnp.stack([section, chip, core]).astype(jnp.int32)
    shifts = jnp.arange(4, dtype=jnp.int32)
    chosen = (section + shifts - 2 * core + 4) % 4

    own = jnp.transpose(w_qkv, (1, 0, 2))
    other = lax.ppermute(own, "head", other_core)
    hidden_in, own = lax.optimization_barrier((hidden_in, own))

    resid = hidden_in.astype(jnp.float32)
    normed = (
        resid * lax.rsqrt(jnp.mean(resid * resid, axis=-1, keepdims=True) + EPS) * norm_gain
    ).astype(jnp.bfloat16)
    x_rows = lax.ppermute(normed, "head", along_x)
    y_rows = lax.ppermute(normed, "head", along_y)

    frequency = THETA ** (-(2.0 * jnp.arange(HD // 2, dtype=jnp.float32)) / HD)

    def projected(relatives, pieces, groups=1):
        starts = section * tok + (chip ^ jnp.array(relatives)) * (2 * rows) + core * rows
        positions = (starts[:, None] + jnp.arange(rows, dtype=jnp.int32)[None, :]).reshape(-1)
        angle = positions.astype(jnp.float32)[:, None] * frequency
        cosine, sine = jnp.cos(angle), jnp.sin(angle)
        cosine = jnp.concatenate([cosine, cosine], axis=-1)
        sine = jnp.concatenate([-sine, sine], axis=-1)
        return project(chosen, pieces, own, other, cosine, sine, groups)

    def sent(outs):
        return [outs[0]] + [to_section(outs[shift], shift) for shift in range(1, 4)]

    def to_other(array):
        return lax.ppermute(array, "head", other_core)

    own_parts = sent(projected([0], [normed]))
    axis_outs = projected([1, 2], [x_rows, y_rows], 2)
    x_rows, y_rows, block_lists, *held = lax.optimization_barrier(
        (x_rows, y_rows, block_lists, *own_parts, *axis_outs)
    )
    own_parts, x_outs, y_outs = held[:4], held[4:8], held[8:]
    d_low = lax.ppermute(y_rows[:half], "head", along_x)
    d_high = lax.ppermute(x_rows[half:], "head", along_y)
    x_parts = sent(x_outs)
    lists = [block_lists] + [to_section(block_lists, shift) for shift in range(1, 4)]
    w_out, d_low, d_high, *held = lax.optimization_barrier(
        (w_out, d_low, d_high, *lists, *x_parts, *y_outs)
    )
    lists, x_parts, y_outs = held[:4], held[4:8], held[8:]
    w_out_all = lax.all_gather(w_out, "head", axis=0, tiled=True)
    y_parts = sent(y_outs)
    diagonal_outs = projected([3], [d_low, d_high])
    held = lax.optimization_barrier((*y_parts, *diagonal_outs))
    y_parts, diagonal_outs = list(held[:4]), held[4:]
    diagonal_parts = sent(diagonal_outs)
    near_pieces = own_parts + x_parts + y_parts + diagonal_parts
    far_pieces = [to_other(jnp.stack(own_parts)), to_other(jnp.stack(x_parts + y_parts))]
    far_pieces += [to_other(part) for part in diagonal_parts]

    def back(attended):
        parts = [attended[0]] + [to_section(attended[shift], shift) for shift in range(1, 4)]
        return jnp.stack(parts)

    def to_chip(array, relative, cross):
        flip = 2 * relative + (1 if cross else 0)
        return lax.ppermute(array, "head", [(i, i ^ flip) for i in range(8)])

    far = back(attend(False, place, lists, near_pieces, far_pieces))
    near = back(attend(True, place, lists, near_pieces, far_pieces))
    y_part, d_part = to_chip(far[:, 0:3], 2, False), to_chip(far[:, 3:6], 3, False)
    swapped = to_other(jnp.stack([y_part[:, 2:3], d_part[:, 2:3]]))
    own_given, x_given = to_chip(near[:, 4:5], 0, True), to_chip(near[:, 5:6], 1, True)
    x_kept = to_chip(near[:, 2:4], 1, False)
    kept, given = [y_part, d_part, near[:, 0:2]], [swapped[0], swapped[1], own_given]
    partial = finish((2, 3, 0), place, kept, given, w_out_all, hidden_in, False)
    return finish((1,), place, [x_kept], [x_given], w_out_all, partial, True)


def solution(mesh):
    placed = (
        P(("section", "head"), None),
        P(),
        P(None, None, "head"),
        P("head", None),
        P("section", None),
    )

    def local(hidden_in, norm_gain, w_qkv, w_out, block_lists):
        fits = (
            mesh.shape["section"] == 4
            and mesh.shape["head"] == 8
            and w_qkv.shape[2] == 2 * HD
            and block_lists.shape[0] % 6 == 0
        )
        form = by_head if fits else general
        return form(hidden_in, norm_gain, w_qkv, w_out, block_lists)

    return jax.shard_map(
        local, mesh=mesh, in_specs=placed, out_specs=P(("section", "head"), None), check_vma=False
    )
```

time: 316 us -> 255 us (0.81)
  waiting for transfers between devices: 147 us -> 69.7 us
  local copies, waits for them, and re-layouts: 5.03 us -> 13.4 us
  Pallas kernels: 79.3 us -> 85.7 us
    ppermute x26 -> x16, waiting for transfers between devices: 56.1 us -> 16.6 us  [the longest x1 13.1 us: by_head(): x_rows = lax.ppermute(normed, 'head', along_x)]
    ppermute x18 -> x21, waiting for transfers between devices: 90.6 us -> 53.1 us  [to_section(): lax.ppermute(array, 'section', [(i, (i + shift) % 4) for i in range(4)])]
    pallas_call x6 -> x7, Pallas kernels: 79.3 us -> 85.7 us  [the longest x2 38.7 us: attend(): pl.pallas_call(functools.partial(attend_kernel, blocks_here, near), out_s...]
    unnamed x90, local copies, waits for them, and re-layouts: 1.81 us -> 7.33 us
    ppermute x26 -> x16, starting transfers between devices: 13.5 us -> 12.4 us  [the longest x5 4.86 us: to_chip(): return lax.ppermute(array, 'head', [(i, i ^ flip) for i in range(8)])]
    ppermute x18 -> x21, starting transfers between devices: 48 us -> 48 us  [to_section(): lax.ppermute(array, 'section', [(i, (i + shift) % 4) for i in range(4)])]
  transfers between devices with their start and end apart: 46 -> 39, of which waited for: 20 -> 15; matrix products, arithmetic and copies ran while one was open for 4% -> 7% of each run, Pallas kernels for 22% -> 31%
where the time goes in v3:
time: 255 us; the launch traced here: 254 us
  Pallas kernels  85.7 us (34%)
  waiting for transfers between devices  69.7 us (27%)
  starting transfers between devices  60.9 us (24%)
  between operations  14.1 us (6%)
  local copies, waits for them, and re-layouts  13.4 us (5%)
  other arithmetic  10.6 us (4%)
    ppermute x21, waiting for transfers between devices, to_section(): lax.ppermute(array, 'section', [(i, (i + shift) % 4) for i in range(4)])  53.1 us
    ppermute x21, starting transfers between devices, to_section(): lax.ppermute(array, 'section', [(i, (i + shift) % 4) for i in range(4)])  48 us
    pallas_call x2, Pallas kernels, attend(): pl.pallas_call(functools.partial(attend_kernel, blocks_here, near), out_s...  38.7 us
    pallas_call x3, Pallas kernels, project(): pl.pallas_call(functools.partial(project_kernel, number, groups), out_sha...  31.6 us
    pallas_call x2, Pallas kernels, finish(): pl.pallas_call(functools.partial(finish_kernel, relatives, last), out_sha...  15.4 us
    ppermute x1, waiting for transfers between devices, by_head(): x_rows = lax.ppermute(normed, 'head', along_x)  13.1 us
    unnamed x90, local copies, waits for them, and re-layouts  7.33 us
  transfers between devices with their start and end apart: 39, of which 15 were waited for; matrix products, arithmetic and copies ran while one was open for 7% of the time, Pallas kernels for 31%

profile of v3, /device:TPU:0, one launch (start us, length us, event | category | flops | bytes accessed | tf_op | source)
XLA Modules:
  0.0 254.4 jit_solution(14706548339326100604)
XLA Ops:
  7.0 1.8 fusion
  8.8 1.1 fusion.2.rest_0_
  10.0 2.7 %collective-permute-start = (bf16[384,2048]{1,0:T(8,128)(2,1)S(1)}, bf16[384,2048]{1,0:T(8,128)(2,1)}, u32[]{:S(2)}, u32[]{:S(2)}) collective-permute-start(bf16[384,2048]{1,0:T(8,128)(2,1)S(1)} %fusion.2.rest_0_), channel_id=1, source_target_pairs={{0,2},{1,3},{2,0},{3,1},{4,6},{5,7},{6,4},{7,5},{8,10},{9,11},{10,... | collective-permute-start | bytes 4718600 | tf_op jit(solution)/shard_map/ppermute | solution.py:574
  12.6 1.5 collective-permute-start.1
  14.8 1.4 fusion.5
  17.2 1.4 fusion.3
  18.6 1.2 pad_maximum_fusion.3
  19.8 9.2 %project_and_rotate.3 = (bf16[384,384]{1,0:T(8,128)(2,1)}, bf16[384,384]{1,0:T(8,128)(2,1)}, bf16[384,384]{1,0:T(8,128)(2,1)}, bf16[384,384]{1,0:T(8,128)(2,1)}) custom-call(s32[4]{0:T(128)} %and_select_fusion.place, bf16[384,2048]{1,0:T(8,128)(2,1)} %copy-done.1, bf16[3,2048,256]{2,1,0:T(8,128)(2,1)} %bitcast.72, ...), custom_call_target="tpu_custom_call" | custom-call | flops 2415919104 | bytes 6291456 | tf_op jit(solution)/shard_map/project_and_rotate/pallas_call | solution.py:199
  29.0 1.6 collective-permute-start.3
  30.6 2.6 %collective-permute-start.4 = (bf16[384,384]{1,0:T(8,128)(2,1)}, bf16[384,384]{1,0:T(8,128)(2,1)S(1)}, u32[]{:S(2)}, u32[]{:S(2)}) collective-permute-start(bf16[384,384]{1,0:T(8,128)(2,1)} %get-tuple-element.65), channel_id=1, source_target_pairs={{0,16},{8,24},{16,0},{24,8},{1,17},{9,25},{17,1},{25,9},{2,18},{10... | collective-permute-start | bytes 884744 | tf_op jit(solution)/shard_map/ppermute | solution.py:560
  33.2 1.3 collective-permute-start.5
  34.5 13.1 %collective-permute-done.rest_0_ = bf16[384,2048]{1,0:T(8,128)(2,1)} collective-permute-done((bf16[384,2048]{1,0:T(8,128)(2,1)S(1)}, bf16[384,2048]{1,0:T(8,128)(2,1)}, u32[]{:S(2)}, u32[]{:S(2)}) %collective-permute-start) | collective-permute-done | bytes 1572896 | tf_op jit(solution)/shard_map/ppermute | solution.py:574
  47.7 1.5 collective-permute-done.1.rest_1_
  49.1 12.5 %project_and_rotate.4 = (bf16[384,384]{1,0:T(8,128)(2,1)}, bf16[384,384]{1,0:T(8,128)(2,1)}, bf16[384,384]{1,0:T(8,128)(2,1)}, bf16[384,384]{1,0:T(8,128)(2,1)},...) custom-call(s32[4]{0:T(128)} %and_select_fusion.place, ...), custom_call_target="tpu_custom_call" | custom-call | flops 4831838208 | bytes 6291456 | tf_op jit(solution)/shard_map/project_and_rotate/pallas_call | solution.py:199
  61.8 1.6 slice.60
  63.8 1.2 slice.61
  65.0 1.8 collective-permute-start.7
  66.8 3.6 %collective-permute-start.10 = (s32[6,12]{1,0:T(8,128)S(1)}, s32[6,12]{1,0:T(8,128)S(1)}, u32[]{:S(2)}, u32[]{:S(2)}) collective-permute-start(s32[6,12]{1,0:T(8,128)S(1)} %copy-done.37), channel_id=1, source_target_pairs={{0,24},{8,0},{16,8},{24,16},{1,25},{9,1},{17,9},{25,17},{2,26},{10... | collective-permute-start | bytes 872 | tf_op jit(solution)/shard_map/ppermute | solution.py:560
  70.4 1.0 collective-permute-start.9
  71.7 3.1 %collective-permute-start.11 = (bf16[384,384]{1,0:T(8,128)(2,1)S(1)}, bf16[384,384]{1,0:T(8,128)(2,1)S(1)}, u32[]{:S(2)}, u32[]{:S(2)}) collective-permute-start(bf16[384,384]{1,0:T(8,128)(2,1)S(1)} %copy-done.33), channel_id=1, source_target_pairs={{0,8},{8,16},{16,24},{24,0},{1,9},{9,17},{17,25},{25,1},{2,10},{10... | collective-permute-start | bytes 884744 | tf_op jit(solution)/shard_map/ppermute | solution.py:560
  74.9 1.1 collective-permute-done.8.rest_1_
  76.5 2.4 collective-permute-start.13
  78.9 5.0 %collective-permute-done.11.rest_9_ = bf16[384,384]{1,0:T(8,128)(2,1)S(1)} collective-permute-done((bf16[384,384]{1,0:T(8,128)(2,1)S(1)}, bf16[384,384]{1,0:T(8,128)(2,1)S(1)}, u32[]{:S(2)}, u32[]{:S(2)}) %collective-permute-start.11) | collective-permute-done | bytes 294944 | tf_op jit(solution)/shard_map/ppermute | solution.py:560
  83.8 9.6 %collective-permute-done.12.rest_10_ = bf16[384,384]{1,0:T(8,128)(2,1)S(1)} collective-permute-done((bf16[384,384]{1,0:T(8,128)(2,1)S(1)}, bf16[384,384]{1,0:T(8,128)(2,1)S(1)}, u32[]{:S(2)}, u32[]{:S(2)}) %collective-permute-start.12) | collective-permute-done | bytes 294944 | tf_op jit(solution)/shard_map/ppermute | solution.py:560
  93.4 1.0 copy-done.21
  95.4 6.7 %collective-permute-start.14 = (bf16[384,384]{1,0:T(8,128)(2,1)}, bf16[384,384]{1,0:T(8,128)(2,1)S(1)}, u32[]{:S(2)}, u32[]{:S(2)}) collective-permute-start(bf16[384,384]{1,0:T(8,128)(2,1)} %get-tuple-element.99), channel_id=1, source_target_pairs={{0,8},{8,16},{16,24},{24,0},{1,9},{9,17},{17,25},{25,1},{2,10},{10... | collective-permute-start | bytes 884744 | tf_op jit(solution)/shard_map/ppermute | solution.py:560
  102.2 1.8 collective-permute-start.15
  104.7 9.9 %project_and_rotate.5 = (bf16[384,384]{1,0:T(8,128)(2,1)}, bf16[384,384]{1,0:T(8,128)(2,1)}, bf16[384,384]{1,0:T(8,128)(2,1)}, bf16[384,384]{1,0:T(8,128)(2,1)}) custom-call(s32[4]{0:T(128)} %and_select_fusion.place, bf16[192,2048]{1,0:T(8,128)(2,1)} %copy-done.21, bf16[192,2048]{1,0:T(8,128)(2,1)} %collective-permute-done.7.rest_1_, ...), custom_call_target="tpu_custom_call" | custom-call | flops 2415919104 | bytes 6291456 | tf_op jit(solution)/shard_map/project_and_rotate/pallas_call | solution.py:199
  114.8 6.2 %collective-permute-done.15.rest_14_ = bf16[384,384]{1,0:T(8,128)(2,1)S(1)} collective-permute-done((bf16[384,384]{1,0:T(8,128)(2,1)}, bf16[384,384]{1,0:T(8,128)(2,1)S(1)}, u32[]{:S(2)}, u32[]{:S(2)}) %collective-permute-start.15) | collective-permute-done | bytes 294944 | tf_op jit(solution)/shard_map/ppermute | solution.py:560
  122.7 6.7 %collective-permute-start.17 = (bf16[384,384]{1,0:T(8,128)(2,1)S(1)}, bf16[384,384]{1,0:T(8,128)(2,1)S(1)}, u32[]{:S(2)}, u32[]{:S(2)}) collective-permute-start(bf16[384,384]{1,0:T(8,128)(2,1)S(1)} %copy-done.36), channel_id=1, source_target_pairs={{0,8},{8,16},{16,24},{24,0},{1,9},{9,17},{17,25},{25,1},{2,10},{10... | collective-permute-start | bytes 884744 | tf_op jit(solution)/shard_map/ppermute | solution.py:560
  129.5 3.3 %collective-permute-start.18 = (bf16[384,384]{1,0:T(8,128)(2,1)S(1)}, bf16[384,384]{1,0:T(8,128)(2,1)S(1)}, u32[]{:S(2)}, u32[]{:S(2)}) collective-permute-start(bf16[384,384]{1,0:T(8,128)(2,1)S(1)} %copy-done.34), channel_id=1, source_target_pairs={{0,16},{8,24},{16,0},{24,8},{1,17},{9,25},{17,1},{25,9},{2,18},{10... | collective-permute-start | bytes 884744 | tf_op jit(solution)/shard_map/ppermute | solution.py:560
  132.8 7.3 %collective-permute-done.17.rest_17_ = bf16[384,384]{1,0:T(8,128)(2,1)S(1)} collective-permute-done((bf16[384,384]{1,0:T(8,128)(2,1)S(1)}, bf16[384,384]{1,0:T(8,128)(2,1)S(1)}, u32[]{:S(2)}, u32[]{:S(2)}) %collective-permute-start.17) | collective-permute-done | bytes 294944 | tf_op jit(solution)/shard_map/ppermute | solution.py:560
  140.1 12.1 %collective-permute-done.18.rest_18_ = bf16[384,384]{1,0:T(8,128)(2,1)S(1)} collective-permute-done((bf16[384,384]{1,0:T(8,128)(2,1)S(1)}, bf16[384,384]{1,0:T(8,128)(2,1)S(1)}, u32[]{:S(2)}, u32[]{:S(2)}) %collective-permute-start.18) | collective-permute-done | bytes 294944 | tf_op jit(solution)/shard_map/ppermute | solution.py:560
  155.0 1.4 copy-done.19
  156.4 20.0 %attend_far.1 = bf16[4,6,128,128]{3,2,1,0:T(8,128)(2,1)} custom-call(s32[3]{0:T(128)} %pad_add_fusion.place, s32[6,12]{1,0:T(8,128)} %rest_0_.1, s32[6,12]{1,0:T(8,128)} %copy-done.39, s32[6,12]{1,0:T(8,128)} %copy-done.40, s32[6,12]{1,0:T(8,128)} %copy-done.38, bf16[384,384]{1,0:T(8,128)(2,1)} %get-tuple-element.90.rest_4_, bf16[384,384]{1,0:T(8,128)(2,1)} %copy-done.4, ...), custom_call_target="tpu_custom_call" | custom-call | flops 4831838208 | bytes 7864320 | tf_op jit(solution)/shard_map/attend_far/pallas_call | solution.py:439
  176.5 1.3 slice_bitcast_fusion.3
  177.8 6.4 %collective-permute-start.31 = (bf16[6,128,128]{2,1,0:T(8,128)(2,1)S(1)}, bf16[6,128,128]{2,1,0:T(8,128)(2,1)S(1)}, u32[]{:S(2)}, u32[]{:S(2)}) collective-permute-start(bf16[6,128,128]{2,1,0:T(8,128)(2,1)S(1)} %get-tuple-element.126), channel_id=1, source_target_pairs={{0,8},{8,16},{16,24},{24,0},{1,9},{9,17},{17,25},{25,1},{2,10},{10... | collective-permute-start | bytes 589832 | tf_op jit(solution)/shard_map/ppermute | solution.py:560
  184.2 2.4 collective-permute-start.33
  186.6 18.7 %attend_near.1 = bf16[4,6,128,128]{3,2,1,0:T(8,128)(2,1)} custom-call(s32[3]{0:T(128)} %pad_add_fusion.place, s32[6,12]{1,0:T(8,128)} %rest_0_.1, s32[6,12]{1,0:T(8,128)} %copy-done.39, s32[6,12]{1,0:T(8,128)} %copy-done.40, s32[6,12]{1,0:T(8,128)} %copy-done.38, bf16[384,384]{1,0:T(8,128)(2,1)} %get-tuple-element.90.rest_4_, bf16[384,384]{1,0:T(8,128)(2,1)} %copy-done.4, ...), custom_call_target="tpu_custom_call" | custom-call | flops 4831838208 | bytes 7864320 | tf_op jit(solution)/shard_map/attend_near/pallas_call | solution.py:439
  206.6 2.5 collective-permute-start.27
  209.1 1.3 collective-permute-start.28
  210.4 2.0 collective-permute-start.35
  212.4 3.9 %collective-permute-done.26 = bf16[6,128,128]{2,1,0:T(8,128)(2,1)S(1)} collective-permute-done((bf16[6,128,128]{2,1,0:T(8,128)(2,1)S(1)}, bf16[6,128,128]{2,1,0:T(8,128)(2,1)S(1)}, u32[]{:S(2)}, u32[]{:S(2)}) %collective-permute-start.26) | collective-permute-done | bytes 196640 | tf_op jit(solution)/shard_map/ppermute | solution.py:560
  216.3 7.1 %collective-permute-done.27 = bf16[6,128,128]{2,1,0:T(8,128)(2,1)S(1)} collective-permute-done((bf16[6,128,128]{2,1,0:T(8,128)(2,1)S(1)}, bf16[6,128,128]{2,1,0:T(8,128)(2,1)S(1)}, u32[]{:S(2)}, u32[]{:S(2)}) %collective-permute-start.27) | collective-permute-done | bytes 196640 | tf_op jit(solution)/shard_map/ppermute | solution.py:560
  223.5 1.1 collective-permute-done.34
  225.4 1.1 collective-permute-start.30
  230.8 9.4 %project_out_first.1.rest_3_ = f32[384,2048]{1,0:T(8,128)} custom-call(s32[3]{0:T(128)} %pad_add_fusion.place, bf16[4,3,128,128]{3,2,1,0:T(8,128)(2,1)} %copy.10.rest_0_, bf16[4,3,128,128]{3,2,1,0:T(8,128)(2,1)} %copy.11.rest_1_, bf16[4,2,128,128]{3,2,1,0:T(8,128)(2,1)} %get-tuple-element.119.rest_2_, bf16[4,1,128,128]{3,2,1,0:T(8,128)(2,1)} %get-tuple-element.132.rest_3_, ...), custom_call_target="tpu_custom_call" | custom-call | flops 2415919104 | bytes 6291456 | tf_op jit(solution)/shard_map/project_out_first/pallas_call | solution.py:526
  241.6 6.0 %project_out_last.1 = bf16[384,2048]{1,0:T(8,128)(2,1)} custom-call(s32[3]{0:T(128)} %pad_add_fusion.place, bf16[4,2,128,128]{3,2,1,0:T(8,128)(2,1)} %copy-done.15, bf16[4,1,128,128]{3,2,1,0:T(8,128)(2,1)} %copy-done.16, bf16[2048,2048]{1,0:T(8,128)(2,1)} %all-gather.2.cloned.1.call-done.rest_6_.rest_2_, f32[384,2048]{1,0:T(8,128)} %project_out_first.1.rest_3_), custom_call_target="tpu_custom_call" | custom-call | flops 805306368 | bytes 2097152 | tf_op jit(solution)/shard_map/project_out_last/pallas_call | solution.py:526
  (160 shorter events, 17.3 us)
Async XLA Ops:
  6.5 223.6 %all-gather.2.cloned.1.call-start = ((), (), s32[]{:S(2)}) async-start(), calls=%async_computation | async-start | bytes 9437184 | tf_op jit(solution)/shard_map/all_gather | solution.py:608
  6.5 13.3 %collective-permute-start.2 = (bf16[3,2048,256]{2,1,0:T(8,128)(2,1)}, bf16[3,2048,256]{2,1,0:T(8,128)(2,1)}, u32[]{:S(2)}, u32[]{:S(2)}) collective-permute-start(bf16[3,2048,256]{2,1,0:T(8,128)(2,1)} %bitcast.71), channel_id=1, source_target_pairs={{0,1},{1,0},{2,3},{3,2},{4,5},{5,4},{6,7},{7,6},{8,9},{9,8},{10,11... | collective-permute-start | bytes 9437192 | tf_op jit(solution)/shard_map/ppermute | solution.py:567
  10.0 37.7 %collective-permute-start = (bf16[384,2048]{1,0:T(8,128)(2,1)S(1)}, bf16[384,2048]{1,0:T(8,128)(2,1)}, u32[]{:S(2)}, u32[]{:S(2)}) collective-permute-start(bf16[384,2048]{1,0:T(8,128)(2,1)S(1)} %fusion.2.rest_0_), channel_id=1, source_target_pairs={{0,2},{1,3},{2,0},{3,1},{4,6},{5,7},{6,4},{7,5},{8,10},{9,11},{10,... | collective-permute-start | bytes 4718600 | tf_op jit(solution)/shard_map/ppermute | solution.py:574
  12.6 36.5 %collective-permute-start.1 = (bf16[384,2048]{1,0:T(8,128)(2,1)S(1)}, bf16[384,2048]{1,0:T(8,128)(2,1)}, u32[]{:S(2)}, u32[]{:S(2)}) collective-permute-start(bf16[384,2048]{1,0:T(8,128)(2,1)S(1)} %fusion.2.rest_0_), channel_id=1, source_target_pairs={{0,4},{1,5},{2,6},{3,7},{4,0},{5,1},{6,2},{7,3},{8,12},{9,13},{10,... | collective-permute-start | bytes 4718600 | tf_op jit(solution)/shard_map/ppermute | solution.py:575
  29.0 32.8 %collective-permute-start.3 = (bf16[384,384]{1,0:T(8,128)(2,1)}, bf16[384,384]{1,0:T(8,128)(2,1)S(1)}, u32[]{:S(2)}, u32[]{:S(2)}) collective-permute-start(bf16[384,384]{1,0:T(8,128)(2,1)} %get-tuple-element.64), channel_id=1, source_target_pairs={{0,8},{8,16},{16,24},{24,0},{1,9},{9,17},{17,25},{25,1},{2,10},{10... | collective-permute-start | bytes 884744 | tf_op jit(solution)/shard_map/ppermute | solution.py:560
  30.6 31.2 %collective-permute-start.4 = (bf16[384,384]{1,0:T(8,128)(2,1)}, bf16[384,384]{1,0:T(8,128)(2,1)S(1)}, u32[]{:S(2)}, u32[]{:S(2)}) collective-permute-start(bf16[384,384]{1,0:T(8,128)(2,1)} %get-tuple-element.65), channel_id=1, source_target_pairs={{0,16},{8,24},{16,0},{24,8},{1,17},{9,25},{17,1},{25,9},{2,18},{10... | collective-permute-start | bytes 884744 | tf_op jit(solution)/shard_map/ppermute | solution.py:560
  33.2 28.6 %collective-permute-start.5 = (bf16[384,384]{1,0:T(8,128)(2,1)}, bf16[384,384]{1,0:T(8,128)(2,1)S(1)}, u32[]{:S(2)}, u32[]{:S(2)}) collective-permute-start(bf16[384,384]{1,0:T(8,128)(2,1)} %get-tuple-element.66), channel_id=1, source_target_pairs={{0,24},{8,0},{16,8},{24,16},{1,25},{9,1},{17,9},{25,17},{2,26},{10... | collective-permute-start | bytes 884744 | tf_op jit(solution)/shard_map/ppermute | solution.py:560
  61.7 60.2 %copy-start.4 = (bf16[384,384]{1,0:T(8,128)(2,1)}, bf16[384,384]{1,0:T(8,128)(2,1)S(1)}, u32[]{:S(2)}) copy-start(bf16[384,384]{1,0:T(8,128)(2,1)S(1)} %collective-permute-done.3.rest_5_) | copy-start | bytes 884740
  61.8 60.2 %copy-start.5 = (bf16[384,384]{1,0:T(8,128)(2,1)}, bf16[384,384]{1,0:T(8,128)(2,1)S(1)}, u32[]{:S(2)}) copy-start(bf16[384,384]{1,0:T(8,128)(2,1)S(1)} %collective-permute-done.4.rest_6_) | copy-start | bytes 884740
  61.8 60.2 %copy-start.6 = (bf16[384,384]{1,0:T(8,128)(2,1)}, bf16[384,384]{1,0:T(8,128)(2,1)S(1)}, u32[]{:S(2)}) copy-start(bf16[384,384]{1,0:T(8,128)(2,1)S(1)} %collective-permute-done.5.rest_7_) | copy-start | bytes 884740
  61.8 42.1 %copy-start.23 = (bf16[384,384]{1,0:T(8,128)(2,1)S(1)}, bf16[384,384]{1,0:T(8,128)(2,1)}, u32[]{:S(2)}) copy-start(bf16[384,384]{1,0:T(8,128)(2,1)} %get-tuple-element.101) | copy-start | bytes 884740
  61.8 42.7 %copy-start.7 = (bf16[384,384]{1,0:T(8,128)(2,1)S(1)}, bf16[384,384]{1,0:T(8,128)(2,1)}, u32[]{:S(2)}) copy-start(bf16[384,384]{1,0:T(8,128)(2,1)} %get-tuple-element.94.rest_8_) | copy-start | bytes 884740
  63.4 30.0 %collective-permute-start.6 = (bf16[192,2048]{1,0:T(8,128)(2,1)S(1)}, bf16[192,2048]{1,0:T(8,128)(2,1)S(1)}, u32[]{:S(2)}, u32[]{:S(2)}) collective-permute-start(bf16[192,2048]{1,0:T(8,128)(2,1)S(1)} %slice.60), channel_id=1, source_target_pairs={{0,2},{1,3},{2,0},{3,1},{4,6},{5,7},{6,4},{7,5},{8,10},{9,11},{10,... | collective-permute-start | bytes 2359304 | tf_op jit(solution)/shard_map/ppermute | solution.py:600
  65.0 29.5 %collective-permute-start.7 = (bf16[192,2048]{1,0:T(8,128)(2,1)S(1)}, bf16[192,2048]{1,0:T(8,128)(2,1)}, u32[]{:S(2)}, u32[]{:S(2)}) collective-permute-start(bf16[192,2048]{1,0:T(8,128)(2,1)S(1)} %slice.61), channel_id=1, source_target_pairs={{0,4},{1,5},{2,6},{3,7},{4,0},{5,1},{6,2},{7,3},{8,12},{9,13},{10,... | collective-permute-start | bytes 2359304 | tf_op jit(solution)/shard_map/ppermute | solution.py:601
  66.8 4.9 %collective-permute-start.10 = (s32[6,12]{1,0:T(8,128)S(1)}, s32[6,12]{1,0:T(8,128)S(1)}, u32[]{:S(2)}, u32[]{:S(2)}) collective-permute-start(s32[6,12]{1,0:T(8,128)S(1)} %copy-done.37), channel_id=1, source_target_pairs={{0,24},{8,0},{16,8},{24,16},{1,25},{9,1},{17,9},{25,17},{2,26},{10... | collective-permute-start | bytes 872 | tf_op jit(solution)/shard_map/ppermute | solution.py:560
  70.4 5.6 %collective-permute-start.8 = (s32[6,12]{1,0:T(8,128)S(1)}, s32[6,12]{1,0:T(8,128)S(1)}, u32[]{:S(2)}, u32[]{:S(2)}) collective-permute-start(s32[6,12]{1,0:T(8,128)S(1)} %copy-done.37), channel_id=1, source_target_pairs={{0,8},{8,16},{16,24},{24,0},{1,9},{9,17},{17,25},{25,1},{2,10},{10... | collective-permute-start | bytes 872 | tf_op jit(solution)/shard_map/ppermute | solution.py:560
  70.4 6.0 %collective-permute-start.9 = (s32[6,12]{1,0:T(8,128)S(1)}, s32[6,12]{1,0:T(8,128)S(1)}, u32[]{:S(2)}, u32[]{:S(2)}) collective-permute-start(s32[6,12]{1,0:T(8,128)S(1)} %copy-done.37), channel_id=1, source_target_pairs={{0,16},{8,24},{16,0},{24,8},{1,17},{9,25},{17,1},{25,9},{2,18},{10... | collective-permute-start | bytes 872 | tf_op jit(solution)/shard_map/ppermute | solution.py:560
  71.7 50.0 %copy-start.38 = (s32[6,12]{1,0:T(8,128)}, s32[6,12]{1,0:T(8,128)S(1)}, u32[]{:S(2)}) copy-start(s32[6,12]{1,0:T(8,128)S(1)} %collective-permute-done.10.rest_3_) | copy-start | bytes 868
  71.7 12.1 %collective-permute-start.11 = (bf16[384,384]{1,0:T(8,128)(2,1)S(1)}, bf16[384,384]{1,0:T(8,128)(2,1)S(1)}, u32[]{:S(2)}, u32[]{:S(2)}) collective-permute-start(bf16[384,384]{1,0:T(8,128)(2,1)S(1)} %copy-done.33), channel_id=1, source_target_pairs={{0,8},{8,16},{16,24},{24,0},{1,9},{9,17},{17,25},{25,1},{2,10},{10... | collective-permute-start | bytes 884744 | tf_op jit(solution)/shard_map/ppermute | solution.py:560
  76.0 45.8 %copy-start.39 = (s32[6,12]{1,0:T(8,128)}, s32[6,12]{1,0:T(8,128)S(1)}, u32[]{:S(2)}) copy-start(s32[6,12]{1,0:T(8,128)S(1)} %collective-permute-done.8.rest_1_) | copy-start | bytes 868
  76.0 17.4 %collective-permute-start.12 = (bf16[384,384]{1,0:T(8,128)(2,1)S(1)}, bf16[384,384]{1,0:T(8,128)(2,1)S(1)}, u32[]{:S(2)}, u32[]{:S(2)}) collective-permute-start(bf16[384,384]{1,0:T(8,128)(2,1)S(1)} %copy-done.31), channel_id=1, source_target_pairs={{0,16},{8,24},{16,0},{24,8},{1,17},{9,25},{17,1},{25,9},{2,18},{10... | collective-permute-start | bytes 884744 | tf_op jit(solution)/shard_map/ppermute | solution.py:560
  76.5 45.3 %copy-start.40 = (s32[6,12]{1,0:T(8,128)}, s32[6,12]{1,0:T(8,128)S(1)}, u32[]{:S(2)}) copy-start(s32[6,12]{1,0:T(8,128)S(1)} %collective-permute-done.9.rest_2_) | copy-start | bytes 868
  76.5 17.0 %collective-permute-start.13 = (bf16[384,384]{1,0:T(8,128)(2,1)S(1)}, bf16[384,384]{1,0:T(8,128)(2,1)S(1)}, u32[]{:S(2)}, u32[]{:S(2)}) collective-permute-start(bf16[384,384]{1,0:T(8,128)(2,1)S(1)} %copy-done.30), channel_id=1, source_target_pairs={{0,24},{8,0},{16,8},{24,16},{1,25},{9,1},{17,9},{25,17},{2,26},{10... | collective-permute-start | bytes 884744 | tf_op jit(solution)/shard_map/ppermute | solution.py:560
  83.8 30.8 %copy-start.9 = (bf16[384,384]{1,0:T(8,128)(2,1)}, bf16[384,384]{1,0:T(8,128)(2,1)S(1)}, u32[]{:S(2)}) copy-start(bf16[384,384]{1,0:T(8,128)(2,1)S(1)} %collective-permute-done.11.rest_9_) | copy-start | bytes 884740
  95.4 19.3 %collective-permute-start.14 = (bf16[384,384]{1,0:T(8,128)(2,1)}, bf16[384,384]{1,0:T(8,128)(2,1)S(1)}, u32[]{:S(2)}, u32[]{:S(2)}) collective-permute-start(bf16[384,384]{1,0:T(8,128)(2,1)} %get-tuple-element.99), channel_id=1, source_target_pairs={{0,8},{8,16},{16,24},{24,0},{1,9},{9,17},{17,25},{25,1},{2,10},{10... | collective-permute-start | bytes 884744 | tf_op jit(solution)/shard_map/ppermute | solution.py:560
  102.2 18.8 %collective-permute-start.15 = (bf16[384,384]{1,0:T(8,128)(2,1)}, bf16[384,384]{1,0:T(8,128)(2,1)S(1)}, u32[]{:S(2)}, u32[]{:S(2)}) collective-permute-start(bf16[384,384]{1,0:T(8,128)(2,1)} %get-tuple-element.100), channel_id=1, source_target_pairs={{0,16},{8,24},{16,0},{24,8},{1,17},{9,25},{17,1},{25,9},{2,18},{10... | collective-permute-start | bytes 884744 | tf_op jit(solution)/shard_map/ppermute | solution.py:560
  103.9 17.6 %collective-permute-start.16 = (bf16[384,384]{1,0:T(8,128)(2,1)S(1)}, bf16[384,384]{1,0:T(8,128)(2,1)S(1)}, u32[]{:S(2)}, u32[]{:S(2)}) collective-permute-start(bf16[384,384]{1,0:T(8,128)(2,1)S(1)} %copy-done.23), channel_id=1, source_target_pairs={{0,24},{8,0},{16,8},{24,16},{1,25},{9,1},{17,9},{25,17},{2,26},{10... | collective-permute-start | bytes 884744 | tf_op jit(solution)/shard_map/ppermute | solution.py:560
  121.9 33.1 %collective-permute-start.21 = (bf16[8,384,384]{2,1,0:T(8,128)(2,1)S(1)}, bf16[8,384,384]{2,1,0:T(8,128)(2,1)S(1)}, u32[]{:S(2)}, u32[]{:S(2)}) collective-permute-start(bf16[8,384,384]{2,1,0:T(8,128)(2,1)S(1)} %bitcast_dynamic-update-slice_fusion), channel_id=1, source_target_pairs={{0,1},{1,0},{2,3},{3,2},{4,5},{5,4},{6,7},{7,6},{8,9},{9,8},{10,11... | collective-permute-start | bytes 7077896 | tf_op jit(solution)/shard_map/ppermute | solution.py:592
  122.3 10.5 %collective-permute-start.20 = (bf16[4,384,384]{2,1,0:T(8,128)(2,1)S(1)}, bf16[4,384,384]{2,1,0:T(8,128)(2,1)S(1)}, u32[]{:S(2)}, u32[]{:S(2)}) collective-permute-start(bf16[4,384,384]{2,1,0:T(8,128)(2,1)S(1)} %pad_maximum_fusion), channel_id=1, source_target_pairs={{0,1},{1,0},{2,3},{3,2},{4,5},{5,4},{6,7},{7,6},{8,9},{9,8},{10,11... | collective-permute-start | bytes 3538952 | tf_op jit(solution)/shard_map/ppermute | solution.py:592
  122.7 17.4 %collective-permute-start.17 = (bf16[384,384]{1,0:T(8,128)(2,1)S(1)}, bf16[384,384]{1,0:T(8,128)(2,1)S(1)}, u32[]{:S(2)}, u32[]{:S(2)}) collective-permute-start(bf16[384,384]{1,0:T(8,128)(2,1)S(1)} %copy-done.36), channel_id=1, source_target_pairs={{0,8},{8,16},{16,24},{24,0},{1,9},{9,17},{17,25},{25,1},{2,10},{10... | collective-permute-start | bytes 884744 | tf_op jit(solution)/shard_map/ppermute | solution.py:560
  129.5 22.8 %collective-permute-start.18 = (bf16[384,384]{1,0:T(8,128)(2,1)S(1)}, bf16[384,384]{1,0:T(8,128)(2,1)S(1)}, u32[]{:S(2)}, u32[]{:S(2)}) collective-permute-start(bf16[384,384]{1,0:T(8,128)(2,1)S(1)} %copy-done.34), channel_id=1, source_target_pairs={{0,16},{8,24},{16,0},{24,8},{1,17},{9,25},{17,1},{25,9},{2,18},{10... | collective-permute-start | bytes 884744 | tf_op jit(solution)/shard_map/ppermute | solution.py:560
  132.7 19.5 %collective-permute-start.19 = (bf16[384,384]{1,0:T(8,128)(2,1)S(1)}, bf16[384,384]{1,0:T(8,128)(2,1)S(1)}, u32[]{:S(2)}, u32[]{:S(2)}) collective-permute-start(bf16[384,384]{1,0:T(8,128)(2,1)S(1)} %copy-done.29), channel_id=1, source_target_pairs={{0,24},{8,0},{16,8},{24,16},{1,25},{9,1},{17,9},{25,17},{2,26},{10... | collective-permute-start | bytes 884744 | tf_op jit(solution)/shard_map/ppermute | solution.py:560
  132.8 20.6 %collective-permute-start.22 = (bf16[384,384]{1,0:T(8,128)(2,1)S(1)}, bf16[384,384]{1,0:T(8,128)(2,1)S(1)}, u32[]{:S(2)}, u32[]{:S(2)}) collective-permute-start(bf16[384,384]{1,0:T(8,128)(2,1)S(1)} %copy-done.22), channel_id=1, source_target_pairs={{0,1},{1,0},{2,3},{3,2},{4,5},{5,4},{6,7},{7,6},{8,9},{9,8},{10,11... | collective-permute-start | bytes 884744 | tf_op jit(solution)/shard_map/ppermute | solution.py:592
  140.1 13.3 %collective-permute-start.23 = (bf16[384,384]{1,0:T(8,128)(2,1)S(1)}, bf16[384,384]{1,0:T(8,128)(2,1)S(1)}, u32[]{:S(2)}, u32[]{:S(2)}) collective-permute-start(bf16[384,384]{1,0:T(8,128)(2,1)S(1)} %collective-permute-done.17.rest_17_), channel_id=1, source_target_pairs={{0,1},{1,0},{2,3},{3,2},{4,5},{5,4},{6,7},{7,6},{8,9},{9,8},{10,11... | collective-permute-start | bytes 884744 | tf_op jit(solution)/shard_map/ppermute | solution.py:592
  152.2 1.6 collective-permute-start.24
  152.2 2.0 collective-permute-start.25
  177.8 27.6 %collective-permute-start.31 = (bf16[6,128,128]{2,1,0:T(8,128)(2,1)S(1)}, bf16[6,128,128]{2,1,0:T(8,128)(2,1)S(1)}, u32[]{:S(2)}, u32[]{:S(2)}) collective-permute-start(bf16[6,128,128]{2,1,0:T(8,128)(2,1)S(1)} %get-tuple-element.126), channel_id=1, source_target_pairs={{0,8},{8,16},{16,24},{24,0},{1,9},{9,17},{17,25},{25,1},{2,10},{10... | collective-permute-start | bytes 589832 | tf_op jit(solution)/shard_map/ppermute | solution.py:560
  184.2 21.1 %collective-permute-start.32 = (bf16[6,128,128]{2,1,0:T(8,128)(2,1)S(1)}, bf16[6,128,128]{2,1,0:T(8,128)(2,1)S(1)}, u32[]{:S(2)}, u32[]{:S(2)}) collective-permute-start(bf16[6,128,128]{2,1,0:T(8,128)(2,1)S(1)} %get-tuple-element.125), channel_id=1, source_target_pairs={{0,16},{8,24},{16,0},{24,8},{1,17},{9,25},{17,1},{25,9},{2,18},{10... | collective-permute-start | bytes 589832 | tf_op jit(solution)/shard_map/ppermute | solution.py:560
  184.2 21.1 %collective-permute-start.33 = (bf16[6,128,128]{2,1,0:T(8,128)(2,1)S(1)}, bf16[6,128,128]{2,1,0:T(8,128)(2,1)S(1)}, u32[]{:S(2)}, u32[]{:S(2)}) collective-permute-start(bf16[6,128,128]{2,1,0:T(8,128)(2,1)S(1)} %get-tuple-element.124), channel_id=1, source_target_pairs={{0,24},{8,0},{16,8},{24,16},{1,25},{9,1},{17,9},{25,17},{2,26},{10... | collective-permute-start | bytes 589832 | tf_op jit(solution)/shard_map/ppermute | solution.py:560
  205.5 19.1 %collective-permute-start.34 = (bf16[4,3,128,128]{3,2,0,1:T(8,128)(2,1)S(1)}, bf16[4,3,128,128]{3,2,0,1:T(8,128)(2,1)S(1)}, u32[]{:S(2)}, u32[]{:S(2)}) collective-permute-start(bf16[4,3,128,128]{3,2,0,1:T(8,128)(2,1)S(1)} %get-tuple-element.122), channel_id=1, source_target_pairs={{0,4},{1,5},{2,6},{3,7},{4,0},{5,1},{6,2},{7,3},{8,12},{9,13},{10,... | collective-permute-start | bytes 1179656 | tf_op jit(solution)/shard_map/ppermute | solution.py:624
  206.5 9.8 %collective-permute-start.26 = (bf16[6,128,128]{2,1,0:T(8,128)(2,1)S(1)}, bf16[6,128,128]{2,1,0:T(8,128)(2,1)S(1)}, u32[]{:S(2)}, u32[]{:S(2)}) collective-permute-start(bf16[6,128,128]{2,1,0:T(8,128)(2,1)S(1)} %get-tuple-element.130), channel_id=1, source_target_pairs={{0,8},{8,16},{16,24},{24,0},{1,9},{9,17},{17,25},{25,1},{2,10},{10... | collective-permute-start | bytes 589832 | tf_op jit(solution)/shard_map/ppermute | solution.py:560
  206.6 16.8 %collective-permute-start.27 = (bf16[6,128,128]{2,1,0:T(8,128)(2,1)S(1)}, bf16[6,128,128]{2,1,0:T(8,128)(2,1)S(1)}, u32[]{:S(2)}, u32[]{:S(2)}) collective-permute-start(bf16[6,128,128]{2,1,0:T(8,128)(2,1)S(1)} %get-tuple-element.129), channel_id=1, source_target_pairs={{0,16},{8,24},{16,0},{24,8},{1,17},{9,25},{17,1},{25,9},{2,18},{10... | collective-permute-start | bytes 589832 | tf_op jit(solution)/shard_map/ppermute | solution.py:560
  209.1 14.3 %collective-permute-start.28 = (bf16[6,128,128]{2,1,0:T(8,128)(2,1)S(1)}, bf16[6,128,128]{2,1,0:T(8,128)(2,1)S(1)}, u32[]{:S(2)}, u32[]{:S(2)}) collective-permute-start(bf16[6,128,128]{2,1,0:T(8,128)(2,1)S(1)} %get-tuple-element.128), channel_id=1, source_target_pairs={{0,24},{8,0},{16,8},{24,16},{1,25},{9,1},{17,9},{25,17},{2,26},{10... | collective-permute-start | bytes 589832 | tf_op jit(solution)/shard_map/ppermute | solution.py:560
  210.4 14.2 %collective-permute-start.35 = (bf16[4,3,128,128]{3,2,0,1:T(8,128)(2,1)S(1)}, bf16[4,3,128,128]{3,2,0,1:T(8,128)(2,1)S(1)}, u32[]{:S(2)}, u32[]{:S(2)}) collective-permute-start(bf16[4,3,128,128]{3,2,0,1:T(8,128)(2,1)S(1)} %get-tuple-element.121), channel_id=1, source_target_pairs={{0,6},{1,7},{2,4},{3,5},{4,2},{5,3},{6,0},{7,1},{8,14},{9,15},{10,... | collective-permute-start | bytes 1179656 | tf_op jit(solution)/shard_map/ppermute | solution.py:624
  224.7 4.7 %collective-permute-start.36 = (bf16[2,4,1,128,128]{4,3,1,2,0:T(8,128)(2,1)S(1)}, bf16[2,4,1,128,128]{4,3,1,2,0:T(8,128)(2,1)S(1)}, u32[]{:S(2)}, u32[]{:S(2)}) collective-permute-start(bf16[2,4,1,128,128]{4,3,1,2,0:T(8,128)(2,1)S(1)} %pad_maximum_fusion.5), channel_id=1, source_target_pairs={{0,1},{1,0},{2,3},{3,2},{4,5},{5,4},{6,7},{7,6},{8,9},{9,8},{10,11... | collective-permute-start | bytes 786440 | tf_op jit(solution)/shard_map/ppermute | solution.py:592
  224.8 5.3 %collective-permute-start.37 = (bf16[4,1,128,128]{3,2,1,0:T(8,128)(2,1)S(1)}, bf16[4,1,128,128]{3,2,1,0:T(8,128)(2,1)S(1)}, u32[]{:S(2)}, u32[]{:S(2)}) collective-permute-start(bf16[4,1,128,128]{3,2,1,0:T(8,128)(2,1)S(1)} %get-tuple-element.117), channel_id=1, source_target_pairs={{0,1},{1,0},{2,3},{3,2},{4,5},{5,4},{6,7},{7,6},{8,9},{9,8},{10,11... | collective-permute-start | bytes 393224 | tf_op jit(solution)/shard_map/ppermute | solution.py:624
  225.4 14.8 %collective-permute-start.30 = (bf16[4,1,128,128]{3,2,1,0:T(8,128)(2,1)S(1)}, bf16[4,1,128,128]{3,2,1,0:T(8,128)(2,1)S(1)}, u32[]{:S(2)}, u32[]{:S(2)}) collective-permute-start(bf16[4,1,128,128]{3,2,1,0:T(8,128)(2,1)S(1)} %get-tuple-element.118), channel_id=1, source_target_pairs={{0,3},{1,2},{2,1},{3,0},{4,7},{5,6},{6,5},{7,4},{8,11},{9,10},{10,... | collective-permute-start | bytes 393224 | tf_op jit(solution)/shard_map/ppermute | solution.py:624
  227.2 13.0 %collective-permute-start.29 = (bf16[4,2,128,128]{3,2,1,0:T(8,128)(2,1)S(1)}, bf16[4,2,128,128]{3,2,1,0:T(8,128)(2,1)S(1)}, u32[]{:S(2)}, u32[]{:S(2)}) collective-permute-start(bf16[4,2,128,128]{3,2,1,0:T(8,128)(2,1)S(1)} %get-tuple-element.120), channel_id=1, source_target_pairs={{0,2},{1,3},{2,0},{3,1},{4,6},{5,7},{6,4},{7,5},{8,10},{9,11},{10,... | collective-permute-start | bytes 786440 | tf_op jit(solution)/shard_map/ppermute | solution.py:624
  (32 other events, 224.5 us)
Sparse Core Ops, SparseCore 0:
  94.6 59.3 all-gather.1
